TPU v7x, 32 devices: a whole 2x2x4 slice. The times are simulated.
32 devices in a mesh: lat: 4 (over y, x), lon: 8 (over z, core).
Axes of the slice: x: 2, y: 2, z: 4, core: 2. Of those that a mesh axis runs over, the one named last changes fastest.
Arguments:
- state: bfloat16 [512, 1024, 128], P('lat', 'lon'), may hold values from -6 to 6
- edge_metric: float32 [9, 512, 1024], P(None, 'lat', 'lon'), may hold values from 0.1 to 1
- stencil_coef: float32 [2, 9, 128], replicated, may hold values from -4 to 4
- norm_gain: float32 [2, 128], replicated, may hold values from 0.25 to 1.75
- biases: float32 [2, 4, 128], replicated, may hold values from -3 to 3
- weights: bfloat16 [2, 896, 128], P(None, ('lat', 'lon')), may hold values from -0.5 to 0.5
Outputs:
- refined: bfloat16 [512, 1024, 128], P('lat', 'lon')
All inputs are finite; a program needn't handle non-finite values.
Results may differ from a plain program's by a relative error of at most 0.0069.
Values may be sent and summed in bfloat16 or wider, within the bound.
No kernel may reach another device: no remote copies, remote signals or barrier semaphores. Data moves between devices by JAX's collectives and lax.ppermute only.
A program may use at most 128 MiB of HBM per device.

v0:
```python
import jax
import jax.numpy as jnp
from jax import lax
from jax.sharding import PartitionSpec as P

KMAT = 7
ITERS = 2


EPSILON = 1e-05


def extended(cells, sides, width, closed):
    for axis, dim in sides:
        count = lax.axis_size(axis)
        ends = count if closed else count - 1
        head = lax.slice_in_dim(cells, 0, width, axis=dim)
        tail = lax.slice_in_dim(cells, cells.shape[dim] - width, cells.shape[dim], axis=dim)
        cells = jnp.concatenate(
            [
                lax.ppermute(tail, axis, [(i, (i + 1) % count) for i in range(ends)]),
                cells,
                lax.ppermute(head, axis, [((i + 1) % count, i) for i in range(ends)]),
            ],
            axis=dim,
        )
    return cells


def passed_along(block, axis, distance):
    devices = range(lax.axis_size(axis))
    route = [((i - distance) % len(devices), i) for i in devices]
    return lax.ppermute(block, axis, route)


def grid_update(padded_rows, metric_rows, state_rows, coef, gain, bias, mats):
    row_count = state_rows.shape[0]
    col_count = state_rows.shape[1]
    channels = state_rows.shape[2]
    summed = jnp.zeros(state_rows.shape, jnp.float32)
    for lat_step in range(3):
        for lon_step in range(3):
            direction = 3 * lat_step + lon_step
            view = padded_rows[
                lat_step : lat_step + row_count, lon_step : lon_step + col_count
            ].astype(jnp.float32)
            summed = summed + metric_rows[direction][:, :, None] * coef[direction] * view
    scale = lax.rsqrt(jnp.mean(summed * summed, axis=-1, keepdims=True) + EPSILON)
    normed = (summed * scale * gain).astype(jnp.bfloat16).reshape(-1, channels)
    hidden = state_rows.reshape(-1, channels)
    message = (jnp.dot(normed, mats[0], preferred_element_type=jnp.float32) + bias[0]).astype(
        jnp.bfloat16
    )
    update = jax.nn.sigmoid(
        jnp.dot(message, mats[1], preferred_element_type=jnp.float32)
        + jnp.dot(hidden, mats[4], preferred_element_type=jnp.float32)
        + bias[1]
    )
    reset = jax.nn.sigmoid(
        jnp.dot(message, mats[2], preferred_element_type=jnp.float32)
        + jnp.dot(hidden, mats[5], preferred_element_type=jnp.float32)
        + bias[2]
    )
    candidate = jnp.tanh(
        jnp.dot(message, mats[3], preferred_element_type=jnp.float32)
        + bias[3]
        + reset * jnp.dot(hidden, mats[6], preferred_element_type=jnp.float32)
    )
    result = (1.0 - update) * candidate + update * hidden.astype(jnp.float32)
    return result.astype(jnp.bfloat16).reshape(state_rows.shape)


def place_poles(tall, mirrored, band_index, band_count):
    north = jnp.where(band_index == 0, mirrored[0], tall[0])
    south = jnp.where(band_index == band_count - 1, mirrored[1], tall[-1])
    return jnp.concatenate([north[None], tall[1:-1], south[None]], axis=0)


def pad_tile(current, band_index, band_count, half_cycle):
    widened = extended(current, (("lon", 1),), 1, True)
    tall = extended(widened, (("lat", 0),), 1, False)
    mirrored = passed_along(jnp.stack([widened[0], widened[-1]]), "lon", half_cycle)
    return place_poles(tall, mirrored, band_index, band_count)


def on_device(state, edge_metric, stencil_coef, norm_gain, biases, weights):
    by_tiles = lax.all_gather(weights, "lon", axis=1, tiled=True)
    gathered = lax.all_gather(by_tiles, "lat", axis=1, tiled=True)
    band_index = lax.axis_index("lat")
    band_count = lax.axis_size("lat")
    half_cycle = lax.axis_size("lon") // 2
    channels = state.shape[2]
    current = state
    for iteration in range(ITERS):
        padded = pad_tile(current, band_index, band_count, half_cycle)
        mats = gathered[iteration].reshape(KMAT, channels, channels)
        current = grid_update(
            padded,
            edge_metric,
            current,
            stencil_coef[iteration],
            norm_gain[iteration],
            biases[iteration],
            mats,
        )
    return current


def solution(mesh):
    in_specs = (
        P("lat", "lon", None),
        P(None, "lat", "lon"),
        P(),
        P(),
        P(),
        P(None, ("lat", "lon"), None),
    )
    out_specs = P("lat", "lon", None)
    return jax.shard_map(
        on_device, mesh=mesh, in_specs=in_specs, out_specs=out_specs, check_vma=False
    )
```

profile of v0, /device:TPU:0, one launch (start us, length us, event | category | flops | bytes accessed | tf_op | source)
XLA Modules:
  0.0 187.9 jit_solution(13150619285402979622)
XLA Ops:
  1.6 4.1 %collective-permute-start.1 = (bf16[128,1,128]{2,1,0:T(2,128)(2,1)S(1)}, bf16[128,1,128]{2,1,0:T(2,128)(2,1)S(1)}, u32[]{:S(2)}, u32[]{:S(2)}) collective-permute-start(bf16[128,1,128]{2,1,0:T(2,128)(2,1)S(1)} %get-tuple-element.20), channel_id=1, source_target_pairs={{1,0},{2,1},{3,2},{4,3},{5,4},{6,5},{7,6},{0,7},{9,8},{10,9},{11,1... | collective-permute-start | bytes 98312 | tf_op jit(solution)/shard_map/ppermute | solution.py:23
  6.5 1.5 slice_bitcast_fusion.39
  8.0 1.5 slice_bitcast_fusion.64
  10.6 14.2 %all_gather.6 = bf16[2,224,128]{2,0,1:T(2,128)(2,1)S(1)} all-gather(bf16[2,28,128]{2,0,1:T(2,128)(2,1)} %param.11), channel_id=1, replica_groups=mesh['lat'=4,'lon'=8] {'lon'}, dimensions={1}, use_global_device_ids=true | all-gather | bytes 129024 | tf_op jit(solution)/shard_map/all_gather | solution.py:87
  25.6 3.8 %collective-permute-start.3 = (bf16[1,130,128]{2,1,0:T(8,128)(2,1)S(1)}, bf16[1,130,128]{2,1,0:T(8,128)(2,1)S(1)}, u32[]{:S(2)}, u32[]{:S(2)}) collective-permute-start(bf16[1,130,128]{2,1,0:T(8,128)(2,1)S(1)} %get-tuple-element.15), channel_id=1, source_target_pairs={{0,8},{8,16},{16,24},{1,9},{9,17},{17,25},{2,10},{10,18},{18,26},{... | collective-permute-start | bytes 99848 | tf_op jit(solution)/shard_map/ppermute | solution.py:21
  31.4 12.1 %all_gather.7 = bf16[2,896,128]{2,1,0:T(8,128)(2,1)S(1)} all-gather(bf16[2,224,128]{2,1,0:T(8,128)(2,1)S(1)} %copy.8), channel_id=1, replica_groups=mesh['lat'=4,'lon'=8] {'lat'}, dimensions={1}, use_global_device_ids=true | all-gather | bytes 573440 | tf_op jit(solution)/shard_map/all_gather | solution.py:88
  43.6 9.6 %maximum_maximum_fusion = (bf16[129,130,128]{2,1,0:T(8,128)(2,1)S(1)}, bf16[129,130,128]{2,1,0:T(8,128)(2,1)S(1)}) fusion(bf16[128,1,128]{2,1,0:T(2,128)(2,1)S(1)} %collective-permute-done.1, bf16[128,128,128]{2,1,0:T(8,128)(2,1)} %param.6, bf16[128,1,128]{2,1,0:T(2,128)(2,1)S(1)} %collective-permute-done, bf16[1,130,128]{2,1,0:T(8,128)(2,1)S(1)} %get-tuple-element.32, ...), kind=kLoop, calls=%fused_computation.48 | loop fusion | flops 34344960 | bytes 12912640 | tf_op jit(solution)/shard_map/concatenate | solution.py:76
  53.2 24.2 %multiply_reduce_fusion.1 = (f32[128,128]{1,0:T(8,128)S(1)}, f32[128,128,128]{2,1,0:T(8,128)S(1)}) fusion(bf16[129,130,128]{2,1,0:T(8,128)(2,1)S(1)} %get-tuple-element.14, f32[128]{0:T(128)} %get-tuple-element.41, f32[128,128]{1,0:T(8,128)S(1)} %get-tuple-element.28, f32[128]{0:T(128)} %get-tuple-element.42, f32[128,128]{1,0:T(8,128)S(1)} %get-tuple-element.29, ...), kind=kLoop, calls=%fused_computation.46 | loop fusion | flops 90161152 | bytes 38474240 | tf_op jit(solution)/shard_map/reduce_sum | solution.py:48
  77.5 4.7 %multiply_convert_fusion.1 = bf16[128,128,128]{2,1,0:T(8,128)(2,1)S(1)} fusion(f32[128,128,128]{2,1,0:T(8,128)S(1)} %get-tuple-element.8, f32[128]{0:T(128)S(1)} %get-tuple-element.61, f32[128,128]{1,0:T(8,128)S(1)} %add_rsqrt_fusion.1), kind=kLoop, calls=%fused_computation.45 | loop fusion | flops 6291456 | bytes 12648960 | tf_op jit(solution)/shard_map/convert_element_type | solution.py:49
  85.9 4.5 %convolution_add_fusion.5 = f32[16384,128]{1,0:T(8,128)} fusion(bf16[16384,128]{1,0:T(8,128)(2,1)S(1)} %fusion.26, f32[128]{0:T(128)S(1)} %get-tuple-element.55, bf16[2,896,128]{2,1,0:T(8,128)(2,1)S(1)} %all_gather.7), kind=kOutput, calls=%fused_computation.25 | convolution fusion | flops 538968064 | bytes 12616192 | tf_op jit(solution)/shard_map/dot_general | solution.py:65
  90.4 4.5 %fusion.29 = f32[16384,128]{1,0:T(8,128)} fusion(f32[16384,128]{1,0:T(8,128)S(1)} %fusion.34, bf16[16384,128]{1,0:T(8,128)(2,1)S(1)} %bitcast.139, f32[128]{0:T(128)S(1)} %copy-done.8, bf16[2,896,128]{2,1,0:T(8,128)(2,1)S(1)} %all_gather.7), kind=kOutput, calls=%fused_computation.39 | convolution fusion | flops 547356672 | bytes 21004800 | tf_op jit(solution)/shard_map/dot_general | solution.py:61
  95.0 4.6 %fusion.28 = f32[16384,128]{1,0:T(8,128)} fusion(f32[16384,128]{1,0:T(8,128)S(1)} %fusion.35, bf16[16384,128]{1,0:T(8,128)(2,1)S(1)} %bitcast.140, f32[128]{0:T(128)S(1)} %copy-done.7, bf16[2,896,128]{2,1,0:T(8,128)(2,1)S(1)} %all_gather.7), kind=kOutput, calls=%fused_computation.38 | convolution fusion | flops 547356672 | bytes 21004800 | tf_op jit(solution)/shard_map/dot_general | solution.py:56
  99.6 9.8 %fusion.25 = bf16[16384,128]{1,0:T(8,128)(2,1)S(1)} fusion(f32[16384,128]{1,0:T(8,128)} %convolution_add_fusion.5, f32[16384,128]{1,0:T(8,128)} %fusion.29, bf16[16384,128]{1,0:T(8,128)(2,1)S(1)} %bitcast.141, f32[16384,128]{1,0:T(8,128)} %fusion.28, bf16[2,896,128]{2,1,0:T(8,128)(2,1)S(1)} %all_gather.7), kind=kOutput, calls=%fused_computation.35 | convolution fusion | flops 553648128 | bytes 37781504 | tf_op jit(solution)/shard_map/dot_general | solution.py:67
  109.6 3.6 %collective-permute-start.6 = (bf16[128,1,128]{2,1,0:T(2,128)(2,1)S(1)}, bf16[128,1,128]{2,1,0:T(2,128)(2,1)S(1)}, u32[]{:S(2)}, u32[]{:S(2)}) collective-permute-start(bf16[128,1,128]{2,1,0:T(2,128)(2,1)S(1)} %get-tuple-element.18), channel_id=1, source_target_pairs={{1,0},{2,1},{3,2},{4,3},{5,4},{6,5},{7,6},{0,7},{9,8},{10,9},{11,1... | collective-permute-start | bytes 98312 | tf_op jit(solution)/shard_map/ppermute | solution.py:23
  113.1 2.3 %collective-permute-done.5 = bf16[128,1,128]{2,1,0:T(2,128)(2,1)S(1)} collective-permute-done((bf16[128,1,128]{2,1,0:T(2,128)(2,1)S(1)}, bf16[128,1,128]{2,1,0:T(2,128)(2,1)S(1)}, u32[]{:S(2)}, u32[]{:S(2)}) %collective-permute-start.5) | collective-permute-done | bytes 32800 | tf_op jit(solution)/shard_map/ppermute | solution.py:21
  115.7 2.2 %collective-permute-start.8 = (bf16[1,130,128]{2,1,0:T(8,128)(2,1)S(1)}, bf16[1,130,128]{2,1,0:T(8,128)(2,1)S(1)}, u32[]{:S(2)}, u32[]{:S(2)}) collective-permute-start(bf16[1,130,128]{2,1,0:T(8,128)(2,1)S(1)} %get-tuple-element.11), channel_id=1, source_target_pairs={{0,8},{8,16},{16,24},{1,9},{9,17},{17,25},{2,10},{10,18},{18,26},{... | collective-permute-start | bytes 99848 | tf_op jit(solution)/shard_map/ppermute | solution.py:21
  119.5 4.2 %collective-permute-done.9 = bf16[1,130,128]{2,1,0:T(8,128)(2,1)S(1)} collective-permute-done((bf16[1,130,128]{2,1,0:T(8,128)(2,1)S(1)}, bf16[1,130,128]{2,1,0:T(8,128)(2,1)S(1)}, u32[]{:S(2)}, u32[]{:S(2)}) %collective-permute-start.9) | collective-permute-done | bytes 33312 | tf_op jit(solution)/shard_map/ppermute | solution.py:23
  123.7 6.8 %maximum_maximum_fusion.1 = (bf16[129,130,128]{2,1,0:T(8,128)(2,1)S(1)}, bf16[129,130,128]{2,1,0:T(8,128)(2,1)S(1)}) fusion(bf16[128,1,128]{2,1,0:T(2,128)(2,1)S(1)} %collective-permute-done.6, bf16[128,128,128]{2,1,0:T(8,128)(2,1)S(1)} %bitcast.137, bf16[128,1,128]{2,1,0:T(2,128)(2,1)S(1)} %collective-permute-done.5, ...), kind=kLoop, calls=%fused_computation.50 | loop fusion | flops 34344960 | bytes 12912640 | tf_op jit(solution)/shard_map/concatenate | solution.py:76
  130.6 23.3 %multiply_reduce_fusion = (f32[128,128]{1,0:T(8,128)S(1)}, f32[128,128,128]{2,1,0:T(8,128)S(1)}) fusion(bf16[129,130,128]{2,1,0:T(8,128)(2,1)S(1)} %get-tuple-element.10, f32[128]{0:T(128)S(1)} %copy-done.3, f32[128,128]{1,0:T(8,128)S(1)} %get-tuple-element.28, f32[128]{0:T(128)S(1)} %copy-done.4, f32[128,128]{1,0:T(8,128)S(1)} %get-tuple-element.29, ...), kind=kLoop, calls=%fused_computation.43 | loop fusion | flops 90161152 | bytes 38474240 | tf_op jit(solution)/shard_map/reduce_sum | solution.py:48
  154.0 4.7 %multiply_convert_fusion = bf16[128,128,128]{2,1,0:T(8,128)(2,1)S(1)} fusion(f32[128,128,128]{2,1,0:T(8,128)S(1)} %get-tuple-element.6, f32[128]{0:T(128)S(1)} %get-tuple-element.60, f32[128,128]{1,0:T(8,128)S(1)} %add_rsqrt_fusion), kind=kLoop, calls=%fused_computation.42 | loop fusion | flops 6291456 | bytes 12648960 | tf_op jit(solution)/shard_map/convert_element_type | solution.py:49
  162.5 4.5 %convolution_add_fusion.1 = f32[16384,128]{1,0:T(8,128)} fusion(bf16[16384,128]{1,0:T(8,128)(2,1)S(1)} %fusion.27, f32[128]{0:T(128)S(1)} %get-tuple-element.59, bf16[2,896,128]{2,1,0:T(8,128)(2,1)S(1)} %all_gather.7), kind=kOutput, calls=%fused_computation.9 | convolution fusion | flops 538968064 | bytes 12616192 | tf_op jit(solution)/shard_map/dot_general | solution.py:65
  167.0 4.5 %fusion.31 = f32[16384,128]{1,0:T(8,128)} fusion(f32[16384,128]{1,0:T(8,128)S(1)} %fusion.32, bf16[16384,128]{1,0:T(8,128)(2,1)S(1)} %fusion.25, f32[128]{0:T(128)S(1)} %copy-done.6, bf16[2,896,128]{2,1,0:T(8,128)(2,1)S(1)} %all_gather.7), kind=kOutput, calls=%fused_computation.41 | convolution fusion | flops 547356672 | bytes 21004800 | tf_op jit(solution)/shard_map/dot_general | solution.py:61
  171.5 4.6 %fusion.30 = f32[16384,128]{1,0:T(8,128)} fusion(f32[16384,128]{1,0:T(8,128)S(1)} %fusion.33, bf16[16384,128]{1,0:T(8,128)(2,1)S(1)} %fusion.25, f32[128]{0:T(128)S(1)} %copy-done.5, bf16[2,896,128]{2,1,0:T(8,128)(2,1)S(1)} %all_gather.7), kind=kOutput, calls=%fused_computation.40 | convolution fusion | flops 547356672 | bytes 21004800 | tf_op jit(solution)/shard_map/dot_general | solution.py:56
  176.1 11.8 %fusion.24 = bf16[16384,128]{1,0:T(8,128)(2,1)} fusion(f32[16384,128]{1,0:T(8,128)} %convolution_add_fusion.1, f32[16384,128]{1,0:T(8,128)} %fusion.31, bf16[16384,128]{1,0:T(8,128)(2,1)S(1)} %fusion.25, f32[16384,128]{1,0:T(8,128)} %fusion.30, bf16[2,896,128]{2,1,0:T(8,128)(2,1)S(1)} %all_gather.7), kind=kOutput, calls=%fused_computation.34 | convolution fusion | flops 553648128 | bytes 37781504 | tf_op jit(solution)/shard_map/dot_general | solution.py:67
  (51 shorter events, 15.9 us)
Async XLA Ops:
  1.1 23.7 %collective-permute-start = (bf16[128,1,128]{2,1,0:T(2,128)(2,1)S(1)}, bf16[128,1,128]{2,1,0:T(2,128)(2,1)S(1)}, u32[]{:S(2)}, u32[]{:S(2)}) collective-permute-start(bf16[128,1,128]{2,1,0:T(2,128)(2,1)S(1)} %get-tuple-element.19), channel_id=1, source_target_pairs={{0,1},{1,2},{2,3},{3,4},{4,5},{5,6},{6,7},{7,0},{8,9},{9,10},{10,1... | collective-permute-start | bytes 98312 | tf_op jit(solution)/shard_map/ppermute | solution.py:21
  1.6 23.2 %collective-permute-start.1 = (bf16[128,1,128]{2,1,0:T(2,128)(2,1)S(1)}, bf16[128,1,128]{2,1,0:T(2,128)(2,1)S(1)}, u32[]{:S(2)}, u32[]{:S(2)}) collective-permute-start(bf16[128,1,128]{2,1,0:T(2,128)(2,1)S(1)} %get-tuple-element.20), channel_id=1, source_target_pairs={{1,0},{2,1},{3,2},{4,3},{5,4},{6,5},{7,6},{0,7},{9,8},{10,9},{11,1... | collective-permute-start | bytes 98312 | tf_op jit(solution)/shard_map/ppermute | solution.py:23
  25.6 17.9 %collective-permute-start.3 = (bf16[1,130,128]{2,1,0:T(8,128)(2,1)S(1)}, bf16[1,130,128]{2,1,0:T(8,128)(2,1)S(1)}, u32[]{:S(2)}, u32[]{:S(2)}) collective-permute-start(bf16[1,130,128]{2,1,0:T(8,128)(2,1)S(1)} %get-tuple-element.15), channel_id=1, source_target_pairs={{0,8},{8,16},{16,24},{1,9},{9,17},{17,25},{2,10},{10,18},{18,26},{... | collective-permute-start | bytes 99848 | tf_op jit(solution)/shard_map/ppermute | solution.py:21
  29.5 14.1 %collective-permute-start.4 = (bf16[1,130,128]{2,1,0:T(8,128)(2,1)S(1)}, bf16[1,130,128]{2,1,0:T(8,128)(2,1)S(1)}, u32[]{:S(2)}, u32[]{:S(2)}) collective-permute-start(bf16[1,130,128]{2,1,0:T(8,128)(2,1)S(1)} %get-tuple-element.16), channel_id=1, source_target_pairs={{8,0},{16,8},{24,16},{9,1},{17,9},{25,17},{10,2},{18,10},{26,18},{... | collective-permute-start | bytes 99848 | tf_op jit(solution)/shard_map/ppermute | solution.py:23
  30.8 12.8 %collective-permute-start.2 = (bf16[2,130,128]{2,1,0:T(8,128)(2,1)S(1)}, bf16[2,130,128]{2,1,0:T(8,128)(2,1)S(1)}, u32[]{:S(2)}, u32[]{:S(2)}) collective-permute-start(bf16[2,130,128]{2,1,0:T(8,128)(2,1)S(1)} %pad_maximum_fusion.6), channel_id=1, source_target_pairs={{4,0},{5,1},{6,2},{7,3},{0,4},{1,5},{2,6},{3,7},{12,8},{13,9},{14,... | collective-permute-start | bytes 199688 | tf_op jit(solution)/shard_map/ppermute | solution.py:33
  43.6 9.6 %copy-start = (bf16[128,128,128]{2,1,0:T(8,128)(2,1)S(1)}, bf16[128,128,128]{2,1,0:T(8,128)(2,1)}, u32[]{:S(2)}) copy-start(bf16[128,128,128]{2,1,0:T(8,128)(2,1)} %param.6) | copy-start | bytes 12582916
  85.9 4.5 %copy-start.8 = (f32[128]{0:T(128)S(1)}, f32[128]{0:T(128)}, u32[]{:S(2)}) copy-start(f32[128]{0:T(128)} %get-tuple-element.54) | copy-start | bytes 1540
  90.4 4.5 %copy-start.7 = (f32[128]{0:T(128)S(1)}, f32[128]{0:T(128)}, u32[]{:S(2)}) copy-start(f32[128]{0:T(128)} %get-tuple-element.56) | copy-start | bytes 1540
  109.5 6.0 %collective-permute-start.5 = (bf16[128,1,128]{2,1,0:T(2,128)(2,1)S(1)}, bf16[128,1,128]{2,1,0:T(2,128)(2,1)S(1)}, u32[]{:S(2)}, u32[]{:S(2)}) collective-permute-start(bf16[128,1,128]{2,1,0:T(2,128)(2,1)S(1)} %get-tuple-element.17), channel_id=1, source_target_pairs={{0,1},{1,2},{2,3},{3,4},{4,5},{5,6},{6,7},{7,0},{8,9},{9,10},{10,1... | collective-permute-start | bytes 98312 | tf_op jit(solution)/shard_map/ppermute | solution.py:21
  109.5 21.1 %copy-start.1 = (f32[128]{0:T(128)S(1)}, f32[128]{0:T(128)}, u32[]{:S(2)}) copy-start(f32[128]{0:T(128)} %get-tuple-element.39) | copy-start | bytes 1540
  109.5 21.1 %copy-start.2 = (f32[128]{0:T(128)S(1)}, f32[128]{0:T(128)}, u32[]{:S(2)}) copy-start(f32[128]{0:T(128)} %get-tuple-element.40) | copy-start | bytes 1540
  109.5 21.1 %copy-start.3 = (f32[128]{0:T(128)S(1)}, f32[128]{0:T(128)}, u32[]{:S(2)}) copy-start(f32[128]{0:T(128)} %get-tuple-element.50) | copy-start | bytes 1540
  109.6 21.1 %copy-start.4 = (f32[128]{0:T(128)S(1)}, f32[128]{0:T(128)}, u32[]{:S(2)}) copy-start(f32[128]{0:T(128)} %get-tuple-element.51) | copy-start | bytes 1540
  109.6 5.9 %collective-permute-start.6 = (bf16[128,1,128]{2,1,0:T(2,128)(2,1)S(1)}, bf16[128,1,128]{2,1,0:T(2,128)(2,1)S(1)}, u32[]{:S(2)}, u32[]{:S(2)}) collective-permute-start(bf16[128,1,128]{2,1,0:T(2,128)(2,1)S(1)} %get-tuple-element.18), channel_id=1, source_target_pairs={{1,0},{2,1},{3,2},{4,3},{5,4},{6,5},{7,6},{0,7},{9,8},{10,9},{11,1... | collective-permute-start | bytes 98312 | tf_op jit(solution)/shard_map/ppermute | solution.py:23
  115.5 8.2 %collective-permute-start.7 = (bf16[2,130,128]{2,1,0:T(8,128)(2,1)S(1)}, bf16[2,130,128]{2,1,0:T(8,128)(2,1)S(1)}, u32[]{:S(2)}, u32[]{:S(2)}) collective-permute-start(bf16[2,130,128]{2,1,0:T(8,128)(2,1)S(1)} %pad_maximum_fusion.7), channel_id=1, source_target_pairs={{4,0},{5,1},{6,2},{7,3},{0,4},{1,5},{2,6},{3,7},{12,8},{13,9},{14,... | collective-permute-start | bytes 199688 | tf_op jit(solution)/shard_map/ppermute | solution.py:33
  115.7 3.8 %collective-permute-start.8 = (bf16[1,130,128]{2,1,0:T(8,128)(2,1)S(1)}, bf16[1,130,128]{2,1,0:T(8,128)(2,1)S(1)}, u32[]{:S(2)}, u32[]{:S(2)}) collective-permute-start(bf16[1,130,128]{2,1,0:T(8,128)(2,1)S(1)} %get-tuple-element.11), channel_id=1, source_target_pairs={{0,8},{8,16},{16,24},{1,9},{9,17},{17,25},{2,10},{10,18},{18,26},{... | collective-permute-start | bytes 99848 | tf_op jit(solution)/shard_map/ppermute | solution.py:21
  117.9 5.8 %collective-permute-start.9 = (bf16[1,130,128]{2,1,0:T(8,128)(2,1)S(1)}, bf16[1,130,128]{2,1,0:T(8,128)(2,1)S(1)}, u32[]{:S(2)}, u32[]{:S(2)}) collective-permute-start(bf16[1,130,128]{2,1,0:T(8,128)(2,1)S(1)} %get-tuple-element.12), channel_id=1, source_target_pairs={{8,0},{16,8},{24,16},{9,1},{17,9},{25,17},{10,2},{18,10},{26,18},{... | collective-permute-start | bytes 99848 | tf_op jit(solution)/shard_map/ppermute | solution.py:23
  162.5 4.5 %copy-start.6 = (f32[128]{0:T(128)S(1)}, f32[128]{0:T(128)}, u32[]{:S(2)}) copy-start(f32[128]{0:T(128)} %get-tuple-element.58) | copy-start | bytes 1540
  167.0 4.5 %copy-start.5 = (f32[128]{0:T(128)S(1)}, f32[128]{0:T(128)}, u32[]{:S(2)}) copy-start(f32[128]{0:T(128)} %get-tuple-element.52) | copy-start | bytes 1540
where the time goes:
time: 189 us; the launch traced here: 188 us
  other arithmetic  74.4 us (39%)
  matrix products  56.3 us (30%)
  blocking collectives  26.3 us (14%)
  starting transfers between devices  17.7 us (9%)
  waiting for transfers between devices  6.88 us (4%)
  local copies, waits for them, and re-layouts  6.16 us (3%)
    reduce_sum x2, other arithmetic, grid_update(): jnp.mean(summed * summed, axis=-1, keepdims=True) + EPSILON  47.6 us
    dot_general x2, matrix products, grid_update(): jnp.dot(hidden, mats[6], preferred_element_type=jnp.float32)  21.6 us
    concatenate x2, other arithmetic, place_poles(): return jnp.concatenate([north[None], tall[1:-1], south[None]], axis=0)  16.4 us
    all_gather x1, blocking collectives, on_device(): by_tiles = lax.all_gather(weights, 'lon', axis=1, tiled=True)  14.2 us
    all_gather x1, blocking collectives, on_device(): gathered = lax.all_gather(by_tiles, 'lat', axis=1, tiled=True)  12.1 us
    ppermute x4, starting transfers between devices, extended(): lax.ppermute(head, axis, [((i + 1) % count, i) for i in range(ends)])  10.2 us
    convert_element_type x2, other arithmetic, grid_update(): normed = (summed * scale * gain).astype(jnp.bfloat16).reshape(-1, channels)  9.45 us
    dot_general x2, matrix products, grid_update(): jnp.dot(hidden, mats[4], preferred_element_type=jnp.float32)  9.18 us
  transfers between devices with their start and end apart: 10, of which 3 were waited for; matrix products, arithmetic and copies ran while one was open for 3% of the time, Pallas kernels for 0%

commit v1 on v0

v1 whole, which is shorter than its diff:
```python
import functools

import jax
import jax.numpy as jnp
from jax import lax
from jax.experimental import pallas as pl
from jax.experimental.pallas import tpu as pltpu
from jax.sharding import PartitionSpec as P

KMAT = 7
ITERS = 2
EPSILON = 1e-05
LANES = 128
BLOCK = 4
DEPTH = 4 * BLOCK
LINE = 136
F32 = jnp.float32
BF16 = jnp.bfloat16


def twice(a):
    return jnp.concatenate([a, a], axis=1)


def load_vectors(it, coef_ref, gain_ref, bias_ref, rows_s, coef_s, vec_s):
    rows_s[...] = jnp.zeros_like(rows_s)
    rows_s[0:9, :] = coef_ref[it]
    rows_s[9:10, :] = gain_ref[it : it + 1, :]
    rows_s[10:14, :] = bias_ref[it]
    columns = rows_s[...].T
    for d in range(9):
        coef_s[d] = jnp.broadcast_to(columns[:, d : d + 1], (LANES, LANES))
    for k in range(5):
        factor = 0.5 if k in (2, 3) else 1.0
        vec_s[k] = jnp.broadcast_to(columns[:, 9 + k : 10 + k] * factor, (LANES, LANES))


def load_weights(it, w_ref, m0_s, wg_s):
    def mat(k):
        return w_ref[it, k * LANES : (k + 1) * LANES, :].astype(F32).T

    m0_s[...] = mat(0).astype(BF16)
    h1, h2, h4, h5, h6 = (mat(k) * 0.5 for k in (1, 2, 4, 5, 6))
    parts = [
        jnp.concatenate([h1, h4], 1),
        jnp.concatenate([h2, h5], 1),
        jnp.concatenate([mat(3), h6], 1),
        jnp.concatenate([jnp.zeros_like(h6), h6], 1),
    ]
    for g in range(8):
        for n, part in enumerate(parts):
            wg_s[64 * g + 16 * n : 64 * g + 16 * n + 16, :] = part[16 * g : 16 * g + 16].astype(BF16)


def fill_row(ring, slot, row, west, east, lane):
    ring[slot, 1] = row
    ring[slot, 0] = jnp.where(lane == 0, west, pltpu.roll(row, 1, 1))
    ring[slot, 2] = jnp.where(lane == 127, east, pltpu.roll(row, 127, 1))


def fill_pole(ring, slot, line):
    wide = line.astype(F32)
    for b in range(3):
        ring[slot, b] = wide[1 + b : 129 + b].T


def fill_sides(side_s, west, east):
    side_s[0] = west.astype(F32).T
    side_s[1] = pltpu.roll(east.astype(F32).T, 127, 1)


def prep_block(g, read_row, ring, side_s, lane):
    for r in range(BLOCK):
        q = g * BLOCK + r
        turn = lax.rem(2 * LANES - q, LANES)
        row = read_row(q).astype(F32)
        fill_row(
            ring,
            lax.rem(q, DEPTH),
            row,
            pltpu.roll(side_s[0], turn, 1),
            pltpu.roll(side_s[1], turn, 1),
            lane,
        )


def stencil_block(g, ring, metric_ref, coef_s, vec_s, acc_s, write):
    for pair in range(BLOCK // 2):
        first = g * BLOCK + 2 * pair
        slots = [lax.rem(first + k - 1 + DEPTH, DEPTH) for k in range(4)]
        squares = [None, None]
        metric = [
            [jnp.broadcast_to(metric_ref[d, pl.ds(first + r, 1), :], (8, LANES)) for r in range(2)]
            for d in range(9)
        ]
        for group in range(LANES // 8):
            cs = slice(8 * group, 8 * group + 8)
            acc = [None, None]
            for k in range(4):
                for b in range(3):
                    cell = ring[slots[k], b, cs, :]
                    for a in range(3):
                        r = k - a
                        if 0 <= r < 2:
                            d = 3 * a + b
                            term = (cell * coef_s[d, cs, :]) * metric[d][r]
                            acc[r] = term if acc[r] is None else acc[r] + term
            for r in range(2):
                square = acc[r] * acc[r]
                squares[r] = square if squares[r] is None else squares[r] + square
                acc_s[cs, LANES * r : LANES * r + LANES] = acc[r]
        for r in range(2):
            mean = jnp.sum(squares[r], axis=0, keepdims=True) * (1.0 / LANES)
            scale = lax.rsqrt(mean + EPSILON)
            total = acc_s[:, LANES * r : LANES * r + LANES]
            write(2 * pair + r, (total * scale * vec_s[0]).astype(BF16))


def message_block(normed, m0_s, vec_s, write):
    product = jnp.dot(m0_s[...], normed, preferred_element_type=F32)
    for pair in range(BLOCK // 2):
        ls = slice(2 * LANES * pair, 2 * LANES * (pair + 1))
        write(ls, (product[:, ls] + twice(vec_s[1])).astype(BF16))


def gates_block(read_message, read_row, wg_s, vec_s, write):
    products = []
    for pair in range(BLOCK // 2):
        ls = slice(2 * LANES * pair, 2 * LANES * (pair + 1))
        current = jnp.concatenate([read_row(2 * pair), read_row(2 * pair + 1)], axis=1)
        both = jnp.concatenate([read_message(ls), current], axis=0)
        products.append((current, jnp.dot(wg_s[...], both, preferred_element_type=F32)))
    for pair in range(BLOCK // 2):
        current, w = products[pair]
        for g in range(8):
            o = 64 * g
            cs = slice(16 * g, 16 * g + 16)
            old = current[cs].astype(F32)
            update = jnp.tanh(w[o : o + 16] + twice(vec_s[2, cs, :]))
            reset = jnp.tanh(w[o + 16 : o + 32] + twice(vec_s[3, cs, :]))
            inner = (w[o + 32 : o + 48] + twice(vec_s[4, cs, :])) + reset * w[o + 48 : o + 64]
            new = jnp.tanh(inner)
            blend = ((old + new) + update * (old - new)) * 0.5
            blend = blend.astype(BF16)
            for r in range(2):
                write(2 * pair + r, cs, blend[:, LANES * r : LANES * r + LANES])


def run_stages(stages, order, first, last, count, guarded):
    def step(s, carry):
        for name in order:
            fn, lag = stages[name]
            if guarded:

                @pl.when((s >= lag) & (s - lag < count))
                def _():
                    fn(s - lag)

            else:
                fn(s - lag)
        return carry

    lax.fori_loop(first, last, step, 0)


def first_kernel(x_ref, metric_ref, north_ref, south_ref, west_ref, east_ref, coef_ref, gain_ref, bias_ref,
                 row_ref, normed_ref, ring, side_s, acc_s, rows_s, coef_s, vec_s):
    count = x_ref.shape[0] // BLOCK
    lane = lax.broadcasted_iota(jnp.int32, (LANES, LANES), 1)
    load_vectors(0, coef_ref, gain_ref, bias_ref, rows_s, coef_s, vec_s)
    fill_sides(side_s, west_ref[0], east_ref[0])
    fill_pole(ring, DEPTH - 1, north_ref[0])

    def read_row(q):
        row = x_ref[q].T
        row_ref[q] = row
        return row

    def prep(g):
        prep_block(g, read_row, ring, side_s, lane)

    def stencil(g):
        def write(r, normed):
            normed_ref[g * BLOCK + r] = normed

        stencil_block(g, ring, metric_ref, coef_s, vec_s, acc_s, write)

    prep(0)
    stages = {"P": (prep, 0), "S": (stencil, 1)}
    run_stages(stages, "PS", 1, count, count, False)
    fill_pole(ring, (count * BLOCK) % DEPTH, south_ref[0])
    stencil(count - 1)


def second_kernel(normed_ref, row_ref, metric_ref, lines_ref, sides_ref, coef_ref, gain_ref, bias_ref, w_ref,
                  out_ref, ring, state_s, side_s, acc_s, rows_s, coef_s, vec_s, old_vec_s, m0_s, wg_s,
                  msg1_s, msg2_s, normed_s, flip_s):
    count = out_ref.shape[0] // BLOCK
    lane = lax.broadcasted_iota(jnp.int32, (LANES, LANES), 1)
    load_vectors(0, coef_ref, gain_ref, bias_ref, rows_s, coef_s, old_vec_s)
    load_vectors(1, coef_ref, gain_ref, bias_ref, rows_s, coef_s, vec_s)
    for it in range(2):
        load_weights(it, w_ref, m0_s.at[it], wg_s.at[it])
    fill_sides(side_s, sides_ref[0], sides_ref[1])
    fill_pole(ring, DEPTH - 1, lines_ref[0])

    def message_one(g):
        buf = lax.rem(g, 2)
        normed = jnp.concatenate([normed_ref[g * BLOCK + r] for r in range(BLOCK)], axis=1)

        def write(ls, value):
            msg1_s[buf, :, ls] = value

        message_block(normed, m0_s.at[0], old_vec_s, write)

    def gates_one(g):
        buf = lax.rem(g, 2)

        def write(r, cs, value):
            state_s[lax.rem(g * BLOCK + r, 2 * DEPTH), cs, :] = value

        gates_block(lambda ls: msg1_s[buf, :, ls], lambda r: row_ref[g * BLOCK + r], wg_s.at[0], old_vec_s, write)

    def prep(g):
        prep_block(g, lambda q: state_s[lax.rem(q, 2 * DEPTH)], ring, side_s, lane)

    def stencil(g):
        buf = lax.rem(g, 2)

        def write(r, normed):
            normed_s[buf, :, LANES * r : LANES * r + LANES] = normed

        stencil_block(g, ring, metric_ref, coef_s, vec_s, acc_s, write)

    def message_two(g):
        buf = lax.rem(g, 2)

        def write(ls, value):
            msg2_s[buf, :, ls] = value

        message_block(normed_s[buf], m0_s.at[1], vec_s, write)

    def gates_two(g):
        buf = lax.rem(g, 2)

        def write(r, cs, value):
            flip_s[r, cs, :] = value

        gates_block(
            lambda ls: msg2_s[buf, :, ls],
            lambda r: state_s[lax.rem(g * BLOCK + r, 2 * DEPTH)],
            wg_s.at[1],
            vec_s,
            write,
        )
        for r in range(BLOCK):
            out_ref[g * BLOCK + r] = flip_s[r].T

    stages = {
        "m": (message_one, 0),
        "g": (gates_one, 1),
        "P": (prep, 2),
        "S": (stencil, 3),
        "M": (message_two, 4),
        "G": (gates_two, 5),
    }
    order = "PgGmMS"
    run_stages(stages, order, 0, 5, count, True)
    run_stages(stages, order, 5, count, count, False)
    fill_pole(ring, (count * BLOCK) % DEPTH, lines_ref[1])
    run_stages(stages, order, count, count + 5, count, True)


def ring_kernel(flags_ref, north_ref, south_ref, west_ref, east_ref, own_rows_ref, own_cols_ref,
                row_metric_ref, col_metric_ref, coef_ref, gain_ref, bias_ref, w_ref,
                lines_ref, sides_ref, line_s, new_s):
    polar = [flags_ref[0] == 1, flags_ref[1] == 1]
    ghost = [north_ref, south_ref]
    side = [west_ref, east_ref]

    def put(strip, n, value):
        line_s[strip, n, 8 : 8 + LINE, :] = value

    for e in range(2):
        outer = ghost[e][1].astype(F32)
        inner = own_rows_ref[e].astype(F32)
        before, after = (outer, inner) if e == 0 else (inner, outer)
        put(e, 0, jnp.where(polar[e], after, before))
        put(e, 1, ghost[e][0].astype(F32))
        put(e, 2, jnp.where(polar[e], before, after))
    for e in range(2):
        columns = [side[e][1], side[e][0], own_cols_ref[e]]
        if e == 1:
            columns = columns[::-1]
        for n in range(3):
            at = n if e == 0 else 129 + n
            line_s[2 + e, n, 0:8, :] = jnp.zeros((8, LANES), F32)
            line_s[2 + e, n, 136:152, :] = jnp.zeros((16, LANES), F32)
            line_s[2 + e, n, 10:138, :] = columns[n].astype(F32)
            line_s[2 + e, n, 9:10, :] = line_s[0, 1, 8 + at : 9 + at, :]
            line_s[2 + e, n, 138:139, :] = line_s[1, 1, 8 + at : 9 + at, :]
    normed = []
    old = []
    for strip in range(4):
        metric_ref = row_metric_ref if strip < 2 else col_metric_ref
        packed = metric_ref[strip % 2].astype(F32)
        metric = packed[:, 0:16] + packed[:, 16:32]
        total = None
        for n in range(3):
            for shift in range(3):
                d = 3 * n + shift if strip < 2 else 3 * shift + n
                cells = line_s[strip, n, 7 + shift : 7 + shift + LINE, :]
                term = metric[:, d : d + 1] * coef_ref[0, d : d + 1, :] * cells
                total = term if total is None else total + term
        scale = lax.rsqrt(jnp.mean(total * total, axis=1, keepdims=True) + EPSILON)
        normed.append(total * scale * gain_ref[0:1, :])
        old.append(line_s[strip, 1, 8 : 8 + LINE, :])
    normed = jnp.concatenate(normed, 0).astype(BF16)
    old = jnp.concatenate(old, 0)

    def mat(k):
        return w_ref[0, k * LANES : (k + 1) * LANES, :]

    def dot(a, k):
        return jnp.dot(a, mat(k), preferred_element_type=F32)

    message = (dot(normed, 0) + bias_ref[0, 0:1, :]).astype(BF16)
    hidden = old.astype(BF16)
    update = 0.5 * jnp.tanh(0.5 * (dot(message, 1) + dot(hidden, 4) + bias_ref[0, 1:2, :])) + 0.5
    reset = 0.5 * jnp.tanh(0.5 * (dot(message, 2) + dot(hidden, 5) + bias_ref[0, 2:3, :])) + 0.5
    new = jnp.tanh(dot(message, 3) + bias_ref[0, 3:4, :] + reset * dot(hidden, 6))
    new_s[...] = (1.0 - update) * new + update * old
    for e in range(2):
        lines_ref[e] = new_s[e * LINE : (e + 1) * LINE, :].astype(BF16)
        sides_ref[e] = new_s[(2 + e) * LINE + 2 : (2 + e) * LINE + 130, :].astype(BF16)


def call(kernel, name, outs, scratch, args, smem=0, flops=0, traffic=0):
    vmem = pl.BlockSpec(memory_space=pltpu.VMEM)
    scalar = pl.BlockSpec(memory_space=pltpu.SMEM)
    return pl.pallas_call(
        kernel,
        in_specs=[scalar] * smem + [vmem] * (len(args) - smem),
        out_specs=[vmem] * len(outs),
        out_shape=[jax.ShapeDtypeStruct(s, BF16) for s in outs],
        scratch_shapes=scratch,
        compiler_params=pltpu.CompilerParams(vmem_limit_bytes=40 * 1024 * 1024),
        cost_estimate=pl.CostEstimate(flops=flops, bytes_accessed=traffic, transcendentals=0),
        name=name,
    )(*args)


def split_metric(columns):
    high = lax.reduce_precision(columns, 8, 7)
    low = columns - high
    pad = ((0, 0), (0, 7))
    both = jnp.concatenate([jnp.pad(high, pad), jnp.pad(low, pad)], axis=1)
    return jnp.pad(both, ((0, 0), (0, LANES - 32))).astype(BF16)


def swap(mesh_shape, partner, value):
    lat, lon = mesh_shape
    pairs = [(i * lon + k, partner(i, k)[0] * lon + partner(i, k)[1]) for i in range(lat) for k in range(lon)]
    return lax.ppermute(value, ("lat", "lon"), pairs)


def on_device(state, edge_metric, stencil_coef, norm_gain, biases, weights):
    lat, lon = lax.axis_size("lat"), lax.axis_size("lon")
    shape = (lat, lon)
    half = lon // 2
    i, k = lax.axis_index("lat"), lax.axis_index("lon")
    rows, cols, channels = state.shape
    k_even = k % 2 == 0
    i_even = i % 2 == 0
    far = k >= half
    place = jnp.where(far, 2 * lat - 1 - i, i)

    def ordered(first, mine, theirs):
        return jnp.where(first, jnp.concatenate([mine, theirs]), jnp.concatenate([theirs, mine]))

    def halves(first, a, b):
        return jnp.where(first, a, b), jnp.where(first, b, a)

    shard = weights.transpose(1, 0, 2).reshape(-1, channels)

    col_w = jnp.stack([state[:, 0], state[:, 1]])
    col_e = jnp.stack([state[:, cols - 1], state[:, cols - 2]])
    met_w = split_metric(edge_metric[:, :, 0].T)
    met_e = split_metric(edge_metric[:, :, cols - 1].T)
    out_w = jnp.concatenate([col_w.reshape(-1, channels), met_w])
    out_e = jnp.concatenate([col_e.reshape(-1, channels), met_e])
    size = out_w.shape[0]
    send_near, send_far = halves(k_even, out_e, out_w)
    got_near = swap(shape, lambda i, k: (i, k ^ 1), jnp.concatenate([send_near, shard]))
    shard = ordered(k_even, shard, got_near[size:])
    got_far = swap(
        shape, lambda i, k: (i, (k + 1) % lon if k % 2 else (k - 1) % lon), jnp.concatenate([send_far, shard])
    )
    shard = ordered(jnp.logical_not(k_even), shard, got_far[size:])
    in_e, in_w = halves(k_even, got_near[:size], got_far[:size])
    ghost_w, ghost_e = (a[: 2 * rows].reshape(2, rows, channels) for a in (in_w, in_e))
    ghost_met_w, ghost_met_e = in_w[2 * rows :], in_e[2 * rows :]
    bit = 4
    while bit < half:
        got = swap(shape, lambda i, k, bit=bit: (i, k ^ bit), shard)
        shard = ordered((k & bit) == 0, shard, got)
        bit *= 2

    def extended(near, other):
        picked = jnp.stack([near, other])
        body = state[near : near + 1] if False else jnp.stack([state[near], state[other]])
        west = jnp.stack([ghost_w[1, near : near + 1], ghost_w[1, other : other + 1]])
        west1 = jnp.stack([ghost_w[0, near : near + 1], ghost_w[0, other : other + 1]])
        east1 = jnp.stack([ghost_e[0, near : near + 1], ghost_e[0, other : other + 1]])
        east = jnp.stack([ghost_e[1, near : near + 1], ghost_e[1, other : other + 1]])
        del picked
        fill = jnp.zeros((2, LINE - cols - 4, channels), BF16)
        return jnp.concatenate([west, west1, body, east1, east, fill], axis=1)

    def extended_metric(row):
        body = split_metric(edge_metric[:, row, :].T)
        zero = jnp.zeros((1, LANES), BF16)
        tail = jnp.zeros((LINE - cols - 3, LANES), BF16)
        return jnp.concatenate(
            [zero, ghost_met_w[row : row + 1], body, ghost_met_e[row : row + 1], tail]
        )

    row_n, row_s = extended(0, 1), extended(rows - 1, rows - 2)
    out_n = jnp.concatenate([row_n.reshape(-1, channels), extended_metric(0)])
    out_s = jnp.concatenate([row_s.reshape(-1, channels), extended_metric(rows - 1)])
    size = out_n.shape[0]
    send_a, send_b = halves(i_even, out_s, out_n)
    got_a = swap(shape, lambda i, k: (i ^ 1, k), jnp.concatenate([send_a, shard]))
    shard = ordered(place % 2 == 0, shard, got_a[size:])

    def across(i, k):
        if i == 0 or i == lat - 1:
            return i, (k + half) % lon
        return (i + 1, k) if i % 2 else (i - 1, k)

    got_b = swap(shape, across, jnp.concatenate([send_b, shard]))
    shard = ordered(place % 2 == 1, shard, got_b[size:])
    in_s, in_n = halves(i_even, got_a[:size], got_b[:size])
    ghost_n, ghost_s = (a[: 2 * LINE].reshape(2, LINE, channels) for a in (in_n, in_s))
    row_metric = jnp.stack([in_n[2 * LINE :], in_s[2 * LINE :]])

    def along(i, k, bit):
        m = (2 * lat - 1 - i if k >= half else i) ^ bit
        return (m, k % half) if m < lat else (2 * lat - 1 - m, k % half + half)

    bit = 4
    while bit < 2 * lat:
        got = swap(shape, lambda i, k, bit=bit: along(i, k, bit), shard)
        shard = ordered((place & bit) == 0, shard, got)
        bit *= 2

    def start(n):
        n = n % 4
        return jnp.where(n % 2 == 0, n - 2, n - 1)

    ring = jnp.roll(shard.reshape(2 * lat, -1), start(place), axis=0)
    ring = ring.reshape(2 * lat, half, -1)
    grid = jnp.concatenate([ring[:lat], ring[lat:][::-1]], axis=1)
    grid = jnp.roll(grid, start(k % half), axis=1)
    full = grid.reshape(-1, ITERS, channels).transpose(1, 0, 2)

    tile = state.shape
    square = (LANES, LANES)
    vmem = pltpu.VMEM
    row_t, normed = call(
        first_kernel,
        "aggregate",
        [tile, tile],
        [
            vmem((DEPTH, 3) + square, F32),
            vmem((2,) + square, F32),
            vmem((LANES, 2 * LANES), F32),
            vmem(square, F32),
            vmem((9,) + square, F32),
            vmem((5,) + square, F32),
        ],
        (state, edge_metric, ghost_n, ghost_s, ghost_w, ghost_e, stencil_coef, norm_gain, biases),
        flops=60 * state.size,
        traffic=8 * state.size,
    )
    pad = ((2, LINE - rows - 2), (0, 0))
    col_metric = jnp.stack([jnp.pad(ghost_met_w, pad), jnp.pad(ghost_met_e, pad)])
    flags = jnp.stack([i == 0, i == lat - 1]).astype(jnp.int32)
    lines, sides = call(
        ring_kernel,
        "border",
        [(2, LINE, channels), (2, rows, channels)],
        [vmem((4, 3, LINE + 16, LANES), F32), vmem((4 * LINE, LANES), F32)],
        (
            flags,
            ghost_n,
            ghost_s,
            ghost_w,
            ghost_e,
            jnp.stack([row_n[0], row_s[0]]),
            jnp.stack([col_w[0], col_e[0]]),
            row_metric,
            col_metric,
            stencil_coef,
            norm_gain,
            biases,
            full,
        ),
        smem=1,
    )
    (out,) = call(
        second_kernel,
        "refine",
        [tile],
        [
            vmem((DEPTH, 3) + square, F32),
            vmem((2 * DEPTH,) + square, BF16),
            vmem((2,) + square, F32),
            vmem((LANES, 2 * LANES), F32),
            vmem(square, F32),
            vmem((9,) + square, F32),
            vmem((5,) + square, F32),
            vmem((5,) + square, F32),
            vmem((2,) + square, BF16),
            vmem((2, 4 * LANES, 2 * LANES), BF16),
            vmem((2, LANES, BLOCK * LANES), BF16),
            vmem((2, LANES, BLOCK * LANES), BF16),
            vmem((2, LANES, BLOCK * LANES), BF16),
            vmem((BLOCK,) + square, BF16),
        ],
        (normed, row_t, edge_metric, lines, sides, stencil_coef, norm_gain, biases, full),
    )
    return out


def solution(mesh):
    in_specs = (
        P("lat", "lon", None),
        P(None, "lat", "lon"),
        P(),
        P(),
        P(),
        P(None, ("lat", "lon"), None),
    )
    out_specs = P("lat", "lon", None)
    return jax.shard_map(on_device, mesh=mesh, in_specs=in_specs, out_specs=out_specs, check_vma=False)
```

time: 189 us -> 111 us (0.59)
  other arithmetic: 74.4 us -> 1.94 us
  Pallas kernels: 0 us -> 61.3 us
  matrix products: 56.3 us -> 0 us
  blocking collectives: 26.3 us -> 0 us
  local copies, waits for them, and re-layouts: 6.16 us -> 18.3 us
  waiting for transfers between devices: 6.88 us -> 16.5 us
  starting transfers between devices: 17.7 us -> 11 us
    pallas_call x0 -> x3, Pallas kernels: none -> 61.3 us  [call(): pl.pallas_call(kernel, in_specs=[scalar] * smem + [vmem] * (len(args) - s...]
    dot_general x14 -> x0, matrix products: 56.3 us -> none  [the longest x2 21.6 us: grid_update(): jnp.dot(hidden, mats[6], preferred_element_type=jnp.float32)]
    reduce_sum x2 -> x0, other arithmetic: 47.6 us -> none  [grid_update(): jnp.mean(summed * summed, axis=-1, keepdims=True) + EPSILON]
    all_gather x2 -> x0, blocking collectives: 26.3 us -> none  [the longest x1 14.2 us: on_device(): by_tiles = lax.all_gather(weights, 'lon', axis=1, tiled=True)]
    concatenate x4 -> x10, other arithmetic: 17.2 us -> 1.3 us  [the longest x1 0.89 us: on_device(): grid = jnp.roll(grid, start(k % half), axis=1)]
    unnamed x18 -> x23, local copies, waits for them, and re-layouts: 0.04 us -> 11.2 us
    ppermute x10 -> x5, waiting for transfers between devices: 6.88 us -> 16.5 us  [swap(): return lax.ppermute(value, ('lat', 'lon'), pairs)]
    convert_element_type x2 -> x1, other arithmetic: 9.45 us -> 0.07 us  [on_device(): flags = jnp.stack([i == 0, i == lat - 1]).astype(jnp.int32)]
  transfers between devices with their start and end apart: 10 -> 5, of which waited for: 3 -> 4; matrix products, arithmetic and copies ran while one was open for 3% -> 1% of each run, Pallas kernels for 0% -> 18%
where the time goes in v1:
time: 111 us; the launch traced here: 110 us
  Pallas kernels  61.3 us (55%)
  local copies, waits for them, and re-layouts  18.3 us (16%)
  waiting for transfers between devices  16.5 us (15%)
  starting transfers between devices  11 us (10%)
  other arithmetic  1.94 us (2%)
    pallas_call x3, Pallas kernels, call(): pl.pallas_call(kernel, in_specs=[scalar] * smem + [vmem] * (len(args) - s...  61.3 us
    ppermute x5, waiting for transfers between devices, swap(): return lax.ppermute(value, ('lat', 'lon'), pairs)  16.5 us
    unnamed x23, local copies, waits for them, and re-layouts  11.2 us
    ppermute x5, starting transfers between devices, swap(): return lax.ppermute(value, ('lat', 'lon'), pairs)  11 us
  transfers between devices with their start and end apart: 5, of which 4 were waited for; matrix products, arithmetic and copies ran while one was open for 1% of the time, Pallas kernels for 18%

profile of v1, /device:TPU:0, one launch (start us, length us, event | category | flops | bytes accessed | tf_op | source)
XLA Modules:
  0.0 109.6 jit_solution(9388512050352413107)
XLA Ops:
  0.0 1.6 %fusion.25 = (bf16[128,1,128]{2,1,0:T(2,128)(2,1)S(1)}, bf16[128,1,128]{2,1,0:T(2,128)(2,1)S(1)}, bf16[128,1,128]{2,1,0:T(2,128)(2,1)S(1)}, bf16[128,1,128]{2,1,0:T(2,128)(2,1)S(1)}) fusion(bf16[128,128,128]{2,1,0:T(8,128)(2,1)} %x_ref.1), kind=kLoop, calls=%fused_computation.86 | loop fusion | bytes 262144 | tf_op jit(solution)/shard_map/slice | solution.py:386
  1.6 1.5 %fusion.27 = (f32[9,128,1]{2,1,0:T(8,128)S(1)}, f32[9,128,1]{2,1,0:T(8,128)S(1)}) fusion(f32[9,128,128]{2,1,0:T(8,128)} %metric_ref.3), kind=kLoop, calls=%fused_computation.88 | loop fusion | bytes 18432 | tf_op jit(solution)/shard_map/slice | solution.py:388
  3.4 0.3 copy.51
  4.2 0.5 collective-permute-start
  4.8 0.8 fusion.24
  5.7 4.8 %collective-permute-start.1 = (bf16[496,128]{1,0:T(8,128)(2,1)S(1)}, bf16[496,128]{1,0:T(8,128)(2,1)S(1)}, u32[]{:S(2)}, u32[]{:S(2)}) collective-permute-start(bf16[496,128]{1,0:T(8,128)(2,1)S(1)} %pad_maximum_fusion.2), channel_id=1, source_target_pairs={{0,7},{1,2},{2,1},{3,4},{4,3},{5,6},{6,5},{7,0},{8,15},{9,10},{10,... | collective-permute-start | bytes 380936 | tf_op jit(solution)/shard_map/ppermute | solution.py:364
  10.9 2.9 %collective-permute-done.1 = bf16[496,128]{1,0:T(8,128)(2,1)S(1)} collective-permute-done((bf16[496,128]{1,0:T(8,128)(2,1)S(1)}, bf16[496,128]{1,0:T(8,128)(2,1)S(1)}, u32[]{:S(2)}, u32[]{:S(2)}) %collective-permute-start.1) | collective-permute-done | bytes 127008 | tf_op jit(solution)/shard_map/ppermute | solution.py:364
  14.1 0.3 concatenate.97
  14.4 0.3 concatenate.94
  14.8 0.3 concatenate.96
  15.5 1.9 %collective-permute-start.2 = (bf16[632,128]{1,0:T(8,128)(2,1)S(1)}, bf16[632,128]{1,0:T(8,128)(2,1)S(1)}, u32[]{:S(2)}, u32[]{:S(2)}) collective-permute-start(bf16[632,128]{1,0:T(8,128)(2,1)S(1)} %pad_maximum_fusion.1), channel_id=1, source_target_pairs={{0,8},{1,9},{2,10},{3,11},{4,12},{5,13},{6,14},{7,15},{8,0},{9,1},... | collective-permute-start | bytes 485384 | tf_op jit(solution)/shard_map/ppermute | solution.py:364
  17.6 3.3 %collective-permute-done.2 = bf16[632,128]{1,0:T(8,128)(2,1)S(1)} collective-permute-done((bf16[632,128]{1,0:T(8,128)(2,1)S(1)}, bf16[632,128]{1,0:T(8,128)(2,1)S(1)}, u32[]{:S(2)}, u32[]{:S(2)}) %collective-permute-start.2) | collective-permute-done | bytes 161824 | tf_op jit(solution)/shard_map/ppermute | solution.py:364
  21.0 1.9 %collective-permute-start.3 = (bf16[856,128]{1,0:T(8,128)(2,1)S(1)}, bf16[856,128]{1,0:T(8,128)(2,1)S(1)}, u32[]{:S(2)}, u32[]{:S(2)}) collective-permute-start(bf16[856,128]{1,0:T(8,128)(2,1)S(1)} %pad_maximum_fusion), channel_id=1, source_target_pairs={{0,4},{1,5},{2,6},{3,7},{4,0},{5,1},{6,2},{7,3},{8,16},{9,17},{10,... | collective-permute-start | bytes 657416 | tf_op jit(solution)/shard_map/ppermute | solution.py:364
  22.9 10.1 %collective-permute-done.3 = bf16[856,128]{1,0:T(8,128)(2,1)S(1)} collective-permute-done((bf16[856,128]{1,0:T(8,128)(2,1)S(1)}, bf16[856,128]{1,0:T(8,128)(2,1)S(1)}, u32[]{:S(2)}, u32[]{:S(2)}) %collective-permute-start.3) | collective-permute-done | bytes 219168 | tf_op jit(solution)/shard_map/ppermute | solution.py:364
  33.2 1.9 %collective-permute-start.4 = (bf16[896,128]{1,0:T(8,128)(2,1)S(1)}, bf16[896,128]{1,0:T(8,128)(2,1)S(1)}, u32[]{:S(2)}, u32[]{:S(2)}) collective-permute-start(bf16[896,128]{1,0:T(8,128)(2,1)S(1)} %maximum_select_fusion.1), channel_id=1, source_target_pairs={{0,28},{1,29},{2,30},{3,31},{4,24},{5,25},{6,26},{7,27},{8,20},{9,... | collective-permute-start | bytes 688136 | tf_op jit(solution)/shard_map/ppermute | solution.py:364
  35.1 2.2 %copy-done.1 = bf16[128,128,128]{2,1,0:T(8,128)(2,1)S(1)} copy-done((bf16[128,128,128]{2,1,0:T(8,128)(2,1)S(1)}, bf16[128,128,128]{2,1,0:T(8,128)(2,1)}, u32[]{:S(2)}) %copy-start.1) | copy-done | bytes 4194328
  37.3 19.9 %aggregate.1 = (bf16[128,128,128]{2,1,0:T(8,128)(2,1)S(1)}, bf16[128,128,128]{2,1,0:T(8,128)(2,1)S(1)}) custom-call(bf16[128,128,128]{2,1,0:T(8,128)(2,1)S(1)} %copy-done.1, f32[9,128,128]{2,1,0:T(8,128)S(1)} %copy-done, bf16[2,136,128]{2,1,0:T(8,128)(2,1)S(1)} %bitcast.62, bf16[2,136,128]{2,1,0:T(8,128)(2,1)S(1)} %bitcast.60, ...), custom_call_target="tpu_custom_call" | custom-call | flops 125829120 | bytes 16777216 | tf_op jit(solution)/shard_map/aggregate/pallas_call | solution.py:341
  57.2 2.0 %copy-done.2 = bf16[128,128,128]{2,1,0:T(8,128)(2,1)} copy-done((bf16[128,128,128]{2,1,0:T(8,128)(2,1)}, bf16[128,128,128]{2,1,0:T(8,128)(2,1)S(1)}, u32[]{:S(2)}) %copy-start.2) | copy-done | bytes 4194328
  59.2 2.0 %copy-done.4 = bf16[128,128,128]{2,1,0:T(8,128)(2,1)} copy-done((bf16[128,128,128]{2,1,0:T(8,128)(2,1)}, bf16[128,128,128]{2,1,0:T(8,128)(2,1)S(1)}, u32[]{:S(2)}) %copy-start.4) | copy-done | bytes 4194328
  62.6 0.9 fusion.2
  63.8 2.3 %border.1 = (bf16[2,136,128]{2,1,0:T(8,128)(2,1)S(1)}, bf16[2,128,128]{2,1,0:T(8,128)(2,1)S(1)}) custom-call(s32[2]{0:T(128)S(1)} %add_convert_fusion.flags_ref, bf16[2,136,128]{2,1,0:T(8,128)(2,1)S(1)} %bitcast.63, bf16[2,136,128]{2,1,0:T(8,128)(2,1)S(1)} %bitcast.61, bf16[2,128,128]{2,1,0:T(8,128)(2,1)S(1)} %bitcast.69, bf16[2,128,128]{2,1,0:T(8,128)(2,1)S(1)} %bitcast.66, ...), custom_call_target="tpu_custom_call" | custom-call | tf_op jit(solution)/shard_map/border/pallas_call | solution.py:341
  66.1 2.2 %copy-done.3 = bf16[128,128,128]{2,1,0:T(8,128)(2,1)S(1)} copy-done((bf16[128,128,128]{2,1,0:T(8,128)(2,1)S(1)}, bf16[128,128,128]{2,1,0:T(8,128)(2,1)}, u32[]{:S(2)}) %copy-start.3) | copy-done | bytes 4194328
  68.3 2.2 %copy-done.5 = bf16[128,128,128]{2,1,0:T(8,128)(2,1)S(1)} copy-done((bf16[128,128,128]{2,1,0:T(8,128)(2,1)S(1)}, bf16[128,128,128]{2,1,0:T(8,128)(2,1)}, u32[]{:S(2)}) %copy-start.5) | copy-done | bytes 4194328
  70.5 39.1 %refine.1 = bf16[128,128,128]{2,1,0:T(8,128)(2,1)} custom-call(bf16[128,128,128]{2,1,0:T(8,128)(2,1)S(1)} %copy-done.5, bf16[128,128,128]{2,1,0:T(8,128)(2,1)S(1)} %copy-done.3, f32[9,128,128]{2,1,0:T(8,128)S(1)} %copy-done, bf16[2,136,128]{2,1,0:T(8,128)(2,1)S(1)} %get-tuple-element.11.lines_ref, bf16[2,128,128]{2,1,0:T(8,128)(2,1)S(1)} %get-tuple-element.12.sides_ref, ...), custom_call_target="tpu_custom_call" | custom-call | tf_op jit(solution)/shard_map/refine/pallas_call | solution.py:341
  (96 shorter events, 3.7 us)
Async XLA Ops:
  0.0 14.4 %slice-start = ((bf16[128,128,128]{2,1,0:T(8,128)(2,1)}), bf16[2,128,128]{2,1,0:T(8,128)(2,1)S(1)}, s32[]{:S(2)}) async-start(bf16[128,128,128]{2,1,0:T(8,128)(2,1)} %x_ref.1), calls=%async_computation | async-start | bytes 131072 | tf_op jit(solution)/shard_map/stack | solution.py:411
  0.0 4.7 %copy-start = (f32[9,128,128]{2,1,0:T(8,128)S(1)}, f32[9,128,128]{2,1,0:T(8,128)}, u32[]{:S(2)}) copy-start(f32[9,128,128]{2,1,0:T(8,128)} %metric_ref.3) | copy-start | bytes 1769476
  0.0 4.2 %copy-start.8 = (bf16[2,28,128]{2,0,1:T(2,128)(2,1)S(1)}, bf16[2,28,128]{2,0,1:T(2,128)(2,1)}, u32[]{:S(2)}) copy-start(bf16[2,28,128]{2,0,1:T(2,128)(2,1)} %param.11) | copy-start | bytes 43012
  0.0 10.6 %copy-start.9 = (f32[2,9,128]{2,0,1:T(2,128)S(1)}, f32[2,9,128]{2,0,1:T(2,128)}, u32[]{:S(2)}) copy-start(f32[2,9,128]{2,0,1:T(2,128)} %param.8) | copy-start | bytes 27652
  3.8 31.3 %copy-start.6 = (f32[2,4,128]{2,1,0:T(4,128)S(1)}, f32[2,4,128]{2,1,0:T(4,128)}, u32[]{:S(2)}) copy-start(f32[2,4,128]{2,1,0:T(4,128)} %bias_ref.5) | copy-start | bytes 12292
  3.8 31.3 %copy-start.7 = (f32[2,128]{1,0:T(2,128)S(1)}, f32[2,128]{1,0:T(2,128)}, u32[]{:S(2)}) copy-start(f32[2,128]{1,0:T(2,128)} %gain_ref.5) | copy-start | bytes 3076
  4.2 1.5 %collective-permute-start = (bf16[440,128]{1,0:T(8,128)(2,1)S(1)}, bf16[440,128]{1,0:T(8,128)(2,1)S(1)}, u32[]{:S(2)}, u32[]{:S(2)}) collective-permute-start(bf16[440,128]{1,0:T(8,128)(2,1)S(1)} %pad_maximum_fusion.3), channel_id=1, source_target_pairs={{0,1},{1,0},{2,3},{3,2},{4,5},{5,4},{6,7},{7,6},{8,9},{9,8},{10,11... | collective-permute-start | bytes 337928 | tf_op jit(solution)/shard_map/ppermute | solution.py:364
  5.7 8.0 %collective-permute-start.1 = (bf16[496,128]{1,0:T(8,128)(2,1)S(1)}, bf16[496,128]{1,0:T(8,128)(2,1)S(1)}, u32[]{:S(2)}, u32[]{:S(2)}) collective-permute-start(bf16[496,128]{1,0:T(8,128)(2,1)S(1)} %pad_maximum_fusion.2), channel_id=1, source_target_pairs={{0,7},{1,2},{2,1},{3,4},{4,3},{5,6},{6,5},{7,0},{8,15},{9,10},{10,... | collective-permute-start | bytes 380936 | tf_op jit(solution)/shard_map/ppermute | solution.py:364
  15.5 5.4 %collective-permute-start.2 = (bf16[632,128]{1,0:T(8,128)(2,1)S(1)}, bf16[632,128]{1,0:T(8,128)(2,1)S(1)}, u32[]{:S(2)}, u32[]{:S(2)}) collective-permute-start(bf16[632,128]{1,0:T(8,128)(2,1)S(1)} %pad_maximum_fusion.1), channel_id=1, source_target_pairs={{0,8},{1,9},{2,10},{3,11},{4,12},{5,13},{6,14},{7,15},{8,0},{9,1},... | collective-permute-start | bytes 485384 | tf_op jit(solution)/shard_map/ppermute | solution.py:364
  21.0 12.1 %collective-permute-start.3 = (bf16[856,128]{1,0:T(8,128)(2,1)S(1)}, bf16[856,128]{1,0:T(8,128)(2,1)S(1)}, u32[]{:S(2)}, u32[]{:S(2)}) collective-permute-start(bf16[856,128]{1,0:T(8,128)(2,1)S(1)} %pad_maximum_fusion), channel_id=1, source_target_pairs={{0,4},{1,5},{2,6},{3,7},{4,0},{5,1},{6,2},{7,3},{8,16},{9,17},{10,... | collective-permute-start | bytes 657416 | tf_op jit(solution)/shard_map/ppermute | solution.py:364
  33.2 28.0 %collective-permute-start.4 = (bf16[896,128]{1,0:T(8,128)(2,1)S(1)}, bf16[896,128]{1,0:T(8,128)(2,1)S(1)}, u32[]{:S(2)}, u32[]{:S(2)}) collective-permute-start(bf16[896,128]{1,0:T(8,128)(2,1)S(1)} %maximum_select_fusion.1), channel_id=1, source_target_pairs={{0,28},{1,29},{2,30},{3,31},{4,24},{5,25},{6,26},{7,27},{8,20},{9,... | collective-permute-start | bytes 688136 | tf_op jit(solution)/shard_map/ppermute | solution.py:364
  35.1 2.2 %copy-start.1 = (bf16[128,128,128]{2,1,0:T(8,128)(2,1)S(1)}, bf16[128,128,128]{2,1,0:T(8,128)(2,1)}, u32[]{:S(2)}) copy-start(bf16[128,128,128]{2,1,0:T(8,128)(2,1)} %x_ref.1) | copy-start | bytes 12582916
  57.2 2.0 %copy-start.2 = (bf16[128,128,128]{2,1,0:T(8,128)(2,1)}, bf16[128,128,128]{2,1,0:T(8,128)(2,1)S(1)}, u32[]{:S(2)}) copy-start(bf16[128,128,128]{2,1,0:T(8,128)(2,1)S(1)} %get-tuple-element.10.row_ref) | copy-start | bytes 12582916
  59.2 2.0 %copy-start.4 = (bf16[128,128,128]{2,1,0:T(8,128)(2,1)}, bf16[128,128,128]{2,1,0:T(8,128)(2,1)S(1)}, u32[]{:S(2)}) copy-start(bf16[128,128,128]{2,1,0:T(8,128)(2,1)S(1)} %get-tuple-element.9.normed_ref) | copy-start | bytes 12582916
  66.1 2.2 %copy-start.3 = (bf16[128,128,128]{2,1,0:T(8,128)(2,1)S(1)}, bf16[128,128,128]{2,1,0:T(8,128)(2,1)}, u32[]{:S(2)}) copy-start(bf16[128,128,128]{2,1,0:T(8,128)(2,1)} %copy-done.2) | copy-start | bytes 12582916
  68.3 2.2 %copy-start.5 = (bf16[128,128,128]{2,1,0:T(8,128)(2,1)S(1)}, bf16[128,128,128]{2,1,0:T(8,128)(2,1)}, u32[]{:S(2)}) copy-start(bf16[128,128,128]{2,1,0:T(8,128)(2,1)} %copy-done.4) | copy-start | bytes 12582916

commit v2 on v1

v2 whole, which is shorter than its diff:
```python
import functools

import jax
import jax.numpy as jnp
from jax import lax
from jax.experimental import pallas as pl
from jax.experimental.pallas import tpu as pltpu
from jax.sharding import PartitionSpec as P

KMAT = 7
ITERS = 2
EPSILON = 1e-05
LANES = 128
BLOCK = 4
DEPTH = 4 * BLOCK
LINE = 136
ORDER_ONE = ("S", "PT")
ORDER_TWO = ("G", "M", "S", "P", "g", "m")
DELAY = 2
F32 = jnp.float32
BF16 = jnp.bfloat16


def twice(a):
    return jnp.concatenate([a, a], axis=1)


def load_vectors(it, coef_ref, gain_ref, bias_ref, rows_s, coef_s, vec_s):
    rows_s[...] = jnp.zeros_like(rows_s)
    rows_s[0:9, :] = coef_ref[it]
    rows_s[9:10, :] = gain_ref[it : it + 1, :]
    rows_s[10:14, :] = bias_ref[it]
    columns = rows_s[...].T
    for d in range(9):
        coef_s[d] = jnp.broadcast_to(columns[:, d : d + 1], (LANES, LANES))
    for k in range(5):
        factor = 0.5 if k in (2, 3) else 1.0
        vec_s[k] = jnp.broadcast_to(columns[:, 9 + k : 10 + k] * factor, (LANES, LANES))


def load_weights(it, w_ref, m0_s, wg_s):
    def mat(k):
        return w_ref[it, k * LANES : (k + 1) * LANES, :].astype(F32).T

    m0_s[...] = mat(0).astype(BF16)
    h1, h2, h4, h5, h6 = (mat(k) * 0.5 for k in (1, 2, 4, 5, 6))
    parts = [
        jnp.concatenate([h1, h4], 1),
        jnp.concatenate([h2, h5], 1),
        jnp.concatenate([mat(3), h6], 1),
        jnp.concatenate([jnp.zeros_like(h6), h6], 1),
    ]
    for g in range(8):
        for n, part in enumerate(parts):
            wg_s[64 * g + 16 * n : 64 * g + 16 * n + 16, :] = part[16 * g : 16 * g + 16].astype(BF16)


def fill_pole(ring, slot, line):
    wide = line.astype(F32)
    for b in range(3):
        ring[slot, b] = wide[1 + b : 129 + b].T


def fill_sides(side_s, west, east):
    odd = lax.broadcasted_iota(jnp.int32, (LANES, LANES), 1) % 2 == 1
    west = west.astype(F32).T
    east = pltpu.roll(east.astype(F32).T, 127, 1)
    side_s[0] = jnp.where(odd, east, west).astype(BF16)
    side_s[1] = jnp.where(odd, west, east).astype(BF16)


def prep_block(g, read_part, ring, side_s, lane):
    pending = []

    def put():
        slot, cs, planes = pending.pop(0)
        for b, plane in enumerate(planes):
            ring[slot, b, cs, :] = plane.astype(F32)

    for r in range(BLOCK):
        q = g * BLOCK + r
        slot = lax.rem(q, ring.shape[0])
        turn = lax.rem(2 * LANES - q, LANES)
        for n in range(LANES // 16):
            cs = slice(16 * n, 16 * n + 16)
            part = read_part(q, cs)
            side = pltpu.roll(side_s[r % 2, cs, :], turn, 1)
            west = jnp.where(lane == 0, side, pltpu.roll(part, 1, 1))
            east = jnp.where(lane == 127, side, pltpu.roll(part, 127, 1))
            pending.append((slot, cs, (west, part, east)))
            if len(pending) > DELAY:
                put()
            yield
    while pending:
        put()


def stencil_block(g, ring, metric_ref, coef_s, vec_s, acc_s, write):
    for pair in range(BLOCK // 2):
        first = g * BLOCK + 2 * pair
        depth = ring.shape[0]
        slots = [lax.rem(first + k - 1 + depth, depth) for k in range(4)]
        squares = [None, None]
        metric = [
            [jnp.broadcast_to(metric_ref[d, pl.ds(first + r, 1), :], (8, LANES)) for r in range(2)]
            for d in range(9)
        ]
        for group in range(LANES // 8):
            cs = slice(8 * group, 8 * group + 8)
            acc = [None, None]
            for k in range(4):
                for b in range(3):
                    cell = ring[slots[k], b, cs, :]
                    for a in range(3):
                        r = k - a
                        if 0 <= r < 2:
                            d = 3 * a + b
                            term = (cell * coef_s[d, cs, :]) * metric[d][r]
                            acc[r] = term if acc[r] is None else acc[r] + term
            for r in range(2):
                square = acc[r] * acc[r]
                squares[r] = square if squares[r] is None else squares[r] + square
                acc_s[cs, LANES * r : LANES * r + LANES] = acc[r]
            yield
        for r in range(2):
            mean = jnp.sum(squares[r], axis=0, keepdims=True) * (1.0 / LANES)
            scale = lax.rsqrt(mean + EPSILON)
            total = acc_s[:, LANES * r : LANES * r + LANES]
            write(2 * pair + r, (total * scale * vec_s[0]).astype(BF16))


def message_block(normed, m0_s, vec_s, write):
    product = jnp.dot(m0_s[...], normed, preferred_element_type=F32)
    for pair in range(BLOCK // 2):
        ls = slice(2 * LANES * pair, 2 * LANES * (pair + 1))
        write(ls, (product[:, ls] + twice(vec_s[1])).astype(BF16))
        yield


def gates_block(read_message, read_row, wg_s, vec_s, write):
    products = []
    for pair in range(BLOCK // 2):
        ls = slice(2 * LANES * pair, 2 * LANES * (pair + 1))
        current = jnp.concatenate([read_row(2 * pair), read_row(2 * pair + 1)], axis=1)
        both = jnp.concatenate([read_message(ls), current], axis=0)
        products.append((current, jnp.dot(wg_s[...], both, preferred_element_type=F32)))
    for pair in range(BLOCK // 2):
        current, w = products[pair]
        for g in range(8):
            o = 64 * g
            cs = slice(16 * g, 16 * g + 16)
            old = current[cs].astype(F32)
            update = jnp.tanh(w[o : o + 16] + twice(vec_s[2, cs, :]))
            reset = jnp.tanh(w[o + 16 : o + 32] + twice(vec_s[3, cs, :]))
            inner = (w[o + 32 : o + 48] + twice(vec_s[4, cs, :])) + reset * w[o + 48 : o + 64]
            new = jnp.tanh(inner)
            blend = ((old + new) + update * (old - new)) * 0.5
            blend = blend.astype(BF16)
            for r in range(2):
                write(2 * pair + r, cs, blend[:, LANES * r : LANES * r + LANES])
            yield


def weave(parts):
    live = [[part, size, 0] for part, size in parts]
    while live:
        live.sort(key=lambda t: (t[2] + 0.5) / t[1])
        turn = live[0]
        turn[2] += 1
        if next(turn[0], True):
            live.remove(turn)


def run_stages(stages, order, first, last, guarded):
    def step(s, carry):
        for word in order:
            if guarded:
                for name in word:
                    fn, lag, size, low, high = stages[name]

                    @pl.when((s >= lag + low) & (s < lag + high))
                    def _():
                        weave([(fn(s - lag), size)])

            else:
                weave([(stages[name][0](s - stages[name][1]), stages[name][2]) for name in word])
        return carry

    lax.fori_loop(first, last, step, 0)


def first_kernel(begin, end, before, wrap, *refs):
    x_ref, metric_ref, west_ref, east_ref, coef_ref, gain_ref, bias_ref = refs[:7]
    rest = refs[7:]
    if wrap:
        north_ref, south_ref = rest[:2]
        rest = rest[2:]
    if before:
        old_row_ref, old_normed_ref = rest[:2]
        rest = rest[2:]
    row_ref, normed_ref, ring, side_s, acc_s, rows_s, coef_s, vec_s = rest
    lane = lax.broadcasted_iota(jnp.int32, (16, LANES), 1)
    load_vectors(0, coef_ref, gain_ref, bias_ref, rows_s, coef_s, vec_s)
    fill_sides(side_s, west_ref[...], east_ref[...])

    def turn(g):
        for r in range(BLOCK):
            row = x_ref[g * BLOCK + r].T
            yield
            row_ref[g * BLOCK + r] = row
            yield

    def prep(g):
        yield from prep_block(g, lambda q, cs: row_ref[q, cs, :], ring, side_s, lane)

    def stencil(g):
        def write(r, normed):
            normed_ref[g * BLOCK + r] = normed

        yield from stencil_block(g, ring, metric_ref, coef_s, vec_s, acc_s, write)

    def copy(g, carry):
        for r in range(BLOCK):
            row_ref[g * BLOCK + r] = old_row_ref[g * BLOCK + r]
            normed_ref[g * BLOCK + r] = old_normed_ref[g * BLOCK + r]
        return carry

    count = x_ref.shape[0] // BLOCK

    def span(lo, hi):
        low, high = max(lo - 1, 0), min(hi + 1, count)
        stages = {
            "T": (turn, 0, 8, low, high),
            "P": (prep, 1, 32, low, high),
            "S": (stencil, 3, 32, lo, hi),
        }
        if lo == 0:
            fill_pole(ring, DEPTH - 1, north_ref[...])
        run_stages(stages, ("P", "T"), low, lo + 3, True)
        full = min(high, hi + 3)
        run_stages(stages, ORDER_ONE, lo + 3, full, False)
        if hi == count:
            fill_pole(ring, (count * BLOCK) % DEPTH, south_ref[...])
        run_stages(stages, ("S", "P"), full, hi + 3, True)

    if before:
        lax.fori_loop(1, 1 + before, copy, 0)
    if wrap:
        span(0, 1)
    span(begin, end)


def second_kernel(normed_ref, row_ref, metric_ref, lines_ref, sides_ref, coef_ref, gain_ref, bias_ref, w_ref,
                  out_ref, ring, state_s, side_s, acc_s, rows_s, coef_s, vec_s, old_vec_s, m0_s, wg_s,
                  msg1_s, msg2_s, normed_s, flip_s):
    count = out_ref.shape[0] // BLOCK
    lane = lax.broadcasted_iota(jnp.int32, (16, LANES), 1)
    load_vectors(0, coef_ref, gain_ref, bias_ref, rows_s, coef_s, old_vec_s)
    load_vectors(1, coef_ref, gain_ref, bias_ref, rows_s, coef_s, vec_s)
    for it in range(2):
        load_weights(it, w_ref, m0_s.at[it], wg_s.at[it])
    fill_sides(side_s, sides_ref[0], sides_ref[1])
    fill_pole(ring, 2 * DEPTH - 1, lines_ref[0])

    def message_one(g):
        buf = lax.rem(g, 2)
        normed = jnp.concatenate([normed_ref[g * BLOCK + r] for r in range(BLOCK)], axis=1)

        def write(ls, value):
            msg1_s[buf, :, ls] = value

        yield from message_block(normed, m0_s.at[0], old_vec_s, write)

    def gates_one(g):
        buf = lax.rem(g, 2)

        def write(r, cs, value):
            state_s[lax.rem(g * BLOCK + r, 2 * DEPTH), cs, :] = value

        yield from gates_block(lambda ls: msg1_s[buf, :, ls], lambda r: row_ref[g * BLOCK + r], wg_s.at[0], old_vec_s, write)

    def prep(g):
        yield from prep_block(g, lambda q, cs: state_s[lax.rem(q, 2 * DEPTH), cs, :], ring, side_s, lane)

    def stencil(g):
        buf = lax.rem(g, 2)

        def write(r, normed):
            normed_s[buf, :, LANES * r : LANES * r + LANES] = normed

        yield from stencil_block(g, ring, metric_ref, coef_s, vec_s, acc_s, write)

    def message_two(g):
        buf = lax.rem(g, 2)

        def write(ls, value):
            msg2_s[buf, :, ls] = value

        yield from message_block(normed_s[buf], m0_s.at[1], vec_s, write)

    def gates_two(g):
        buf = lax.rem(g, 2)

        def write(r, cs, value):
            flip_s[r, cs, :] = value

        yield from gates_block(
            lambda ls: msg2_s[buf, :, ls],
            lambda r: state_s[lax.rem(g * BLOCK + r, 2 * DEPTH)],
            wg_s.at[1],
            vec_s,
            write,
        )
        for r in range(BLOCK):
            out_ref[g * BLOCK + r] = flip_s[r].T

    stages = {
        "m": (message_one, 0, 2, 0, count),
        "g": (gates_one, 1, 16, 0, count),
        "P": (prep, 2, 32, 0, count),
        "S": (stencil, 4, 32, 0, count),
        "M": (message_two, 5, 2, 0, count),
        "G": (gates_two, 6, 16, 0, count),
    }
    run_stages(stages, ORDER_TWO, 0, 6, True)
    run_stages(stages, ORDER_TWO, 6, count, False)
    fill_pole(ring, (count * BLOCK) % (2 * DEPTH), lines_ref[1])
    run_stages(stages, ORDER_TWO, count, count + 6, True)


def ring_kernel(flags_ref, north_ref, south_ref, west_ref, east_ref, own_rows_ref, own_cols_ref,
                row_metric_ref, col_metric_ref, coef_ref, gain_ref, bias_ref, w_ref,
                lines_ref, sides_ref, line_s, metric_s, new_s):
    polar = [flags_ref[0] == 1, flags_ref[1] == 1]
    ghost = [north_ref, south_ref]
    side = [west_ref, east_ref]

    def put(strip, n, value):
        line_s[strip, n, 8 : 8 + LINE, :] = value

    for e in range(2):
        outer = ghost[e][1].astype(F32)
        inner = own_rows_ref[e].astype(F32)
        before, after = (outer, inner) if e == 0 else (inner, outer)
        put(e, 0, jnp.where(polar[e], after, before))
        put(e, 1, ghost[e][0].astype(F32))
        put(e, 2, jnp.where(polar[e], before, after))
    for e in range(2):
        columns = [side[e][0], side[e][1], own_cols_ref[e]] if e == 0 else [side[e][1], side[e][0], own_cols_ref[e]]
        if e == 1:
            columns = columns[::-1]
        for n in range(3):
            at = n if e == 0 else 129 + n
            line_s[2 + e, n, 0:8, :] = jnp.zeros((8, LANES), F32)
            line_s[2 + e, n, 136:152, :] = jnp.zeros((16, LANES), F32)
            line_s[2 + e, n, 10:138, :] = columns[n].astype(F32)
            line_s[2 + e, n, 9:10, :] = line_s[0, 1, 8 + at : 9 + at, :]
            line_s[2 + e, n, 138:139, :] = line_s[1, 1, 8 + at : 9 + at, :]

    def upright(packed):
        both = packed.astype(F32)
        tall = jnp.concatenate([both[0:16] + both[16:32], jnp.zeros((LANES - 16, LANES), F32)], axis=0)
        return tall.T

    metric_s[...] = jnp.zeros_like(metric_s)
    for e in range(2):
        metric_s[e, 2:130, :] = upright(row_metric_ref[e, 0:32])
        ends = upright(row_metric_ref[e, 32:64])
        metric_s[e, 1:2, :] = ends[0:1]
        metric_s[e, 130:131, :] = ends[1:2]
        metric_s[2 + e, 2:130, :] = upright(col_metric_ref[e])
    normed = []
    old = []
    for strip in range(4):
        metric = metric_s[strip]
        total = None
        for n in range(3):
            for shift in range(3):
                d = 3 * n + shift if strip < 2 else 3 * shift + n
                cells = line_s[strip, n, 7 + shift : 7 + shift + LINE, :]
                term = metric[:, d : d + 1] * coef_ref[0, d : d + 1, :] * cells
                total = term if total is None else total + term
        scale = lax.rsqrt(jnp.mean(total * total, axis=1, keepdims=True) + EPSILON)
        normed.append(total * scale * gain_ref[0:1, :])
        old.append(line_s[strip, 1, 8 : 8 + LINE, :])
    normed = jnp.concatenate(normed, 0).astype(BF16)
    old = jnp.concatenate(old, 0)

    def mat(k):
        return w_ref[0, k * LANES : (k + 1) * LANES, :]

    def dot(a, k):
        return jnp.dot(a, mat(k), preferred_element_type=F32)

    message = (dot(normed, 0) + bias_ref[0, 0:1, :]).astype(BF16)
    hidden = old.astype(BF16)
    update = 0.5 * jnp.tanh(0.5 * (dot(message, 1) + dot(hidden, 4) + bias_ref[0, 1:2, :])) + 0.5
    reset = 0.5 * jnp.tanh(0.5 * (dot(message, 2) + dot(hidden, 5) + bias_ref[0, 2:3, :])) + 0.5
    new = jnp.tanh(dot(message, 3) + bias_ref[0, 3:4, :] + reset * dot(hidden, 6))
    new_s[...] = (1.0 - update) * new + update * old
    for e in range(2):
        lines_ref[e] = new_s[e * LINE : (e + 1) * LINE, :].astype(BF16)
        sides_ref[e] = new_s[(2 + e) * LINE + 2 : (2 + e) * LINE + 130, :].astype(BF16)


def call(kernel, name, outs, scratch, args, smem=0, flops=0, traffic=0, limit=24):
    vmem = pl.BlockSpec(memory_space=pltpu.VMEM)
    scalar = pl.BlockSpec(memory_space=pltpu.SMEM)
    return pl.pallas_call(
        kernel,
        in_specs=[scalar] * smem + [vmem] * (len(args) - smem),
        out_specs=[vmem] * len(outs),
        out_shape=[jax.ShapeDtypeStruct(s, BF16) for s in outs],
        scratch_shapes=scratch,
        compiler_params=pltpu.CompilerParams(vmem_limit_bytes=limit * 1024 * 1024),
        cost_estimate=pl.CostEstimate(flops=flops, bytes_accessed=traffic, transcendentals=0),
        name=name,
    )(*args)


def split_metric(values):
    high = lax.reduce_precision(values, 8, 7)
    pad = ((0, 7), (0, 0))
    return jnp.concatenate([jnp.pad(high, pad), jnp.pad(values - high, pad)]).astype(BF16)


def swap(mesh_shape, partner, value):
    lat, lon = mesh_shape
    pairs = [(i * lon + k, partner(i, k)[0] * lon + partner(i, k)[1]) for i in range(lat) for k in range(lon)]
    return lax.ppermute(value, ("lat", "lon"), pairs)


def on_device(state, edge_metric, stencil_coef, norm_gain, biases, weights):
    lat, lon = lax.axis_size("lat"), lax.axis_size("lon")
    shape = (lat, lon)
    half = lon // 2
    i, k = lax.axis_index("lat"), lax.axis_index("lon")
    rows, cols, channels = state.shape
    k_even = k % 2 == 0
    i_even = i % 2 == 0

    def ordered(first, mine, theirs):
        return jnp.where(first, jnp.concatenate([mine, theirs]), jnp.concatenate([theirs, mine]))

    def halves(first, a, b):
        return jnp.where(first, a, b), jnp.where(first, b, a)

    def after(value, *others):
        return lax.optimization_barrier((value,) + others)[0]

    shard = weights.transpose(1, 0, 2).reshape(-1, channels)

    def edge(east):
        first = jnp.where(east, cols - 2, 0)
        last = jnp.where(east, cols - 1, 0)
        columns = lax.dynamic_slice(state, (0, first, 0), (rows, 2, channels)).transpose(1, 0, 2)
        metric = lax.dynamic_slice(edge_metric, (0, 0, last), (9, rows, 1)).reshape(9, rows)
        return columns.reshape(-1, channels), split_metric(metric)

    near, near_metric = edge(k_even)
    got_near = swap(shape, lambda i, k: (i, k ^ 1), jnp.concatenate([near, near_metric, shard]))
    far, far_metric = edge(jnp.logical_not(k_even))
    size = 2 * rows + 32
    shard = ordered(k_even, shard, got_near[size:])
    got_far = swap(
        shape,
        lambda i, k: (i, (k + 1) % lon if k % 2 else (k - 1) % lon),
        jnp.concatenate([far, far_metric, shard]),
    )
    shard = ordered(jnp.logical_not(k_even), shard, got_far[size:])
    in_e, in_w = halves(k_even, got_near[:size], got_far[:size])
    ghost_w, ghost_e = (a[: 2 * rows].reshape(2, rows, channels) for a in (in_w, in_e))
    metric_w, metric_e = in_w[2 * rows :], in_e[2 * rows :]
    own_e, own_w = halves(k_even, near, far)

    def extended(row, inner):
        lines = []
        for q in (row, inner):
            fill = jnp.zeros((LINE - cols - 4, channels), BF16)
            lines.append(jnp.concatenate([ghost_w[:, q], state[q], ghost_e[:, q], fill]))
        return jnp.stack(lines)

    def extended_metric(row):
        ends = jnp.concatenate([metric_w[:, row : row + 1], metric_e[:, row : row + 1]], axis=1)
        ends = jnp.pad(ends, ((0, 0), (0, LANES - 2)))
        return jnp.concatenate([split_metric(edge_metric[:, row]), ends])

    row_n, row_s = extended(0, 1), extended(rows - 1, rows - 2)
    out_n = jnp.concatenate([row_n.reshape(-1, channels), extended_metric(0)])
    out_s = jnp.concatenate([row_s.reshape(-1, channels), extended_metric(rows - 1)])
    size = out_n.shape[0]
    send_a, send_b = halves(i_even, out_s, out_n)
    send_a = jnp.concatenate([send_a, shard])

    def across(i, k):
        if i == 0 or i == lat - 1:
            return i, (k + half) % lon
        return (i + 1, k) if i % 2 else (i - 1, k)

    got_a = swap(shape, lambda i, k: (i ^ 1, k), send_a)
    got_b = swap(shape, across, send_b)

    tile = state.shape
    square = (LANES, LANES)
    vmem = pltpu.VMEM
    count = rows // BLOCK
    cuts = [1, 1 + (count - 1) // 3, 1 + 2 * (count - 1) // 3, count]

    def aggregate(part, side_w, more):
        begin, end = cuts[part], cuts[part + 1]
        return call(
            functools.partial(first_kernel, begin, end, begin - 1, part == 2),
            "aggregate%d" % part,
            [tile, tile],
            [
                vmem((DEPTH, 3) + square, F32),
                vmem((2,) + square, BF16),
                vmem((LANES, 2 * LANES), F32),
                vmem(square, F32),
                vmem((9,) + square, F32),
                vmem((5,) + square, F32),
            ],
            (state, edge_metric, side_w, ghost_e[0], stencil_coef, norm_gain, biases) + more,
            flops=20 * state.size,
            traffic=8 * state.size,
        )

    held = aggregate(0, after(ghost_w[1], send_a, send_b), ())

    shard = ordered((i & 1) == 0, shard, got_a[size:])
    in_s, in_n = halves(i_even, got_a[:size], got_b)
    ghost_n, ghost_s = (a[: 2 * LINE].reshape(2, LINE, channels) for a in (in_n, in_s))
    row_metric = jnp.stack([in_n[2 * LINE :], in_s[2 * LINE :]])

    shard = shard.reshape(2, 4, -1, channels)
    bit = 4
    while bit < lon:
        mine = after(shard, *held) if bit == 4 else shard
        got = swap(shape, lambda i, k, bit=bit: (i, k ^ bit), mine)
        low = (k & bit) == 0
        shard = jnp.where(
            low, jnp.concatenate([shard, got], axis=1), jnp.concatenate([got, shard], axis=1)
        )
        if bit == 4:
            held = aggregate(1, after(ghost_w[1], mine), tuple(held))
        bit *= 2
    place = k % 4
    shard = jnp.where(
        place == 0,
        jnp.roll(shard, -2, axis=1),
        jnp.where(place == 3, jnp.roll(shard, 2, axis=1), shard),
    )
    shard = shard.reshape(-1, channels)
    bit = 2
    while bit < lat:
        mine = after(shard, *held) if bit == 2 else shard
        got = swap(shape, lambda i, k, bit=bit: (i ^ bit, k), mine)
        shard = ordered((i & bit) == 0, shard, got)
        if bit == 2:
            held = aggregate(2, after(ghost_w[1], mine), (ghost_n[0], ghost_s[0]) + tuple(held))
        bit *= 2
    row_t, normed = held
    full = shard.reshape(-1, ITERS, channels).transpose(1, 0, 2)

    flags = jnp.stack([i == 0, i == lat - 1]).astype(jnp.int32)
    lines, sides = call(
        ring_kernel,
        "border",
        [(2, LINE, channels), (2, rows, channels)],
        [vmem((4, 3, LINE + 16, LANES), F32), vmem((4, LINE, LANES), F32), vmem((4 * LINE, LANES), F32)],
        (
            flags,
            ghost_n,
            ghost_s,
            ghost_w,
            ghost_e,
            jnp.stack([row_n[0], row_s[0]]),
            jnp.stack([own_w[:rows], own_e[rows:]]),
            row_metric,
            jnp.stack([metric_w, metric_e]),
            stencil_coef,
            norm_gain,
            biases,
            full,
        ),
        smem=1,
        limit=12,
    )
    (out,) = call(
        second_kernel,
        "refine",
        [tile],
        [
            vmem((2 * DEPTH, 3) + square, F32),
            vmem((2 * DEPTH,) + square, BF16),
            vmem((2,) + square, BF16),
            vmem((LANES, 2 * LANES), F32),
            vmem(square, F32),
            vmem((9,) + square, F32),
            vmem((5,) + square, F32),
            vmem((5,) + square, F32),
            vmem((2,) + square, BF16),
            vmem((2, 4 * LANES, 2 * LANES), BF16),
            vmem((2, LANES, BLOCK * LANES), BF16),
            vmem((2, LANES, BLOCK * LANES), BF16),
            vmem((2, LANES, BLOCK * LANES), BF16),
            vmem((BLOCK,) + square, BF16),
        ],
        (normed, row_t, edge_metric, lines, sides, stencil_coef, norm_gain, biases, full),
    )
    return out


def solution(mesh):
    in_specs = (
        P("lat", "lon", None),
        P(None, "lat", "lon"),
        P(),
        P(),
        P(),
        P(None, ("lat", "lon"), None),
    )
    out_specs = P("lat", "lon", None)
    return jax.shard_map(on_device, mesh=mesh, in_specs=in_specs, out_specs=out_specs, check_vma=False)
```

time: 111 us -> 78.3 us (0.71)
  waiting for transfers between devices: 16.5 us -> 2.68 us
  local copies, waits for them, and re-layouts: 18.3 us -> 8.44 us
  Pallas kernels: 61.3 us -> 54.8 us
    ppermute x5 -> x6, waiting for transfers between devices: 16.5 us -> 2.68 us  [swap(): return lax.ppermute(value, ('lat', 'lon'), pairs)]
    unnamed x23 -> x15, local copies, waits for them, and re-layouts: 11.2 us -> 3.57 us
    pallas_call x3 -> x5, Pallas kernels: 61.3 us -> 54.8 us  [call(): pl.pallas_call(kernel, in_specs=[scalar] * smem + [vmem] * (len(args) - s...]
    slice x17 -> x11, local copies, waits for them, and re-layouts: 4.43 us -> 0.96 us  [the longest x1 0.79 us: extended_metric(): return jnp.concatenate([split_metric(edge_metric[:, row]), ends])]
    concatenate x8 -> x1, local copies, waits for them, and re-layouts: 1.85 us -> 0.08 us  [extended(): jnp.concatenate([ghost_w[:, q], state[q], ghost_e[:, q], fill])]
    dynamic_slice x0 -> x1, local copies, waits for them, and re-layouts: none -> 1.62 us  [edge(): lax.dynamic_slice(edge_metric, (0, 0, last), (9, rows, 1)).reshape(9, rows)]
    transpose x0 -> x3, local copies, waits for them, and re-layouts: none -> 1.27 us  [edge(): lax.dynamic_slice(state, (0, first, 0), (rows, 2, channels))]
    ppermute x5 -> x6, starting transfers between devices: 11 us -> 10 us  [swap(): return lax.ppermute(value, ('lat', 'lon'), pairs)]
  transfers between devices with their start and end apart: 5 -> 6, of which waited for: 4 -> 1; matrix products, arithmetic and copies ran while one was open for 1% -> 4% of each run, Pallas kernels for 18% -> 26%
where the time goes in v2:
time: 78.3 us; the launch traced here: 77.9 us
  Pallas kernels  54.8 us (70%)
  starting transfers between devices  10 us (13%)
  local copies, waits for them, and re-layouts  8.44 us (11%)
  waiting for transfers between devices  2.68 us (3%)
  other arithmetic  1.52 us (2%)
    pallas_call x5, Pallas kernels, call(): pl.pallas_call(kernel, in_specs=[scalar] * smem + [vmem] * (len(args) - s...  54.8 us
    ppermute x6, starting transfers between devices, swap(): return lax.ppermute(value, ('lat', 'lon'), pairs)  10 us
    unnamed x15, local copies, waits for them, and re-layouts  3.57 us
    ppermute x6, waiting for transfers between devices, swap(): return lax.ppermute(value, ('lat', 'lon'), pairs)  2.68 us
    dynamic_slice x1, local copies, waits for them, and re-layouts, edge(): lax.dynamic_slice(edge_metric, (0, 0, last), (9, rows, 1)).reshape(9, rows)  1.62 us
  transfers between devices with their start and end apart: 6, of which 1 were waited for; matrix products, arithmetic and copies ran while one was open for 4% of the time, Pallas kernels for 26%

profile of v2, /device:TPU:0, one launch (start us, length us, event | category | flops | bytes accessed | tf_op | source)
XLA Modules:
  0.0 77.9 jit_solution(10477260822661177043)
XLA Ops:
  0.0 1.2 %dynamic-slice_bitcast_fusion.1 = (bf16[2,128,128]{2,0,1:T(2,128)(2,1)S(1)}, bf16[2,128,128]{2,0,1:T(2,128)(2,1)S(1)}) fusion(bf16[128,128,128]{2,1,0:T(8,128)(2,1)} %refs_0_.5, s32[]{:T(128)S(6)} %select_n.146, s32[]{:T(128)S(6)} %select_n.149), kind=kLoop, calls=%fused_computation.56 | loop fusion | bytes 262152 | tf_op jit(solution)/shard_map/transpose | solution.py:456
  1.3 1.6 %constant_dynamic-slice_fusion.1 = (f32[9,128,1]{2,1,0:T(8,128)S(1)}, f32[9,128,1]{2,1,0:T(8,128)S(1)}) fusion(f32[9,128,128]{2,1,0:T(8,128)} %metric_ref.1, s32[]{:T(128)S(6)} %select_n.147, s32[]{:T(128)S(6)} %select_n.150), kind=kLoop, calls=%fused_computation.100 | loop fusion | bytes 18440 | tf_op jit(solution)/shard_map/dynamic_slice | solution.py:457
  2.9 0.3 copy.91
  3.2 0.7 fusion.18
  4.0 0.5 collective-permute-start
  4.5 0.8 %fusion.38 = (f32[9,1,128]{2,1,0:T(1,128)S(1)}, f32[9,1,128]{2,1,0:T(1,128)S(1)}) fusion(f32[9,128,128]{2,1,0:T(8,128)} %metric_ref.1), kind=kLoop, calls=%fused_computation.109 | loop fusion | bytes 18432 | tf_op jit(solution)/shard_map/slice | solution.py:486
  5.3 0.8 %slice_bitcast_fusion.3 = (bf16[128,128]{1,0:T(8,128)(2,1)S(1)}, bf16[128,128]{1,0:T(8,128)(2,1)S(1)}, bf16[128,128]{1,0:T(8,128)(2,1)S(1)}, bf16[128,128]{1,0:T(8,128)(2,1)S(1)}) fusion(bf16[128,128,128]{2,1,0:T(8,128)(2,1)} %refs_0_.5), kind=kLoop, calls=%fused_computation.70 | loop fusion | bytes 262144 | tf_op jit(solution)/shard_map/squeeze | solution.py:480
  6.2 0.7 copy.84.refs_4_.coef_ref
  6.9 0.3 copy.90
  7.4 4.8 %collective-permute-start.1 = (bf16[400,128]{1,0:T(8,128)(2,1)S(1)}, bf16[400,128]{1,0:T(8,128)(2,1)S(1)}, u32[]{:S(2)}, u32[]{:S(2)}) collective-permute-start(bf16[400,128]{1,0:T(8,128)(2,1)S(1)} %fusion.15), channel_id=1, source_target_pairs={{0,7},{1,2},{2,1},{3,4},{4,3},{5,6},{6,5},{7,0},{8,15},{9,10},{10,... | collective-permute-start | bytes 307208 | tf_op jit(solution)/shard_map/ppermute | solution.py:430
  12.3 2.7 %collective-permute-done.1 = bf16[400,128]{1,0:T(8,128)(2,1)S(1)} collective-permute-done((bf16[400,128]{1,0:T(8,128)(2,1)S(1)}, bf16[400,128]{1,0:T(8,128)(2,1)S(1)}, u32[]{:S(2)}, u32[]{:S(2)}) %collective-permute-start.1) | collective-permute-done | bytes 102432 | tf_op jit(solution)/shard_map/ppermute | solution.py:430
  15.1 0.1 fusion.36
  15.2 0.1 fusion.37
  15.3 0.1 maximum_bitcast_fusion
  15.5 1.6 %collective-permute-start.2 = (bf16[560,128]{1,0:T(8,128)(2,1)S(1)}, bf16[560,128]{1,0:T(8,128)(2,1)S(1)}, u32[]{:S(2)}, u32[]{:S(2)}) collective-permute-start(bf16[560,128]{1,0:T(8,128)(2,1)S(1)} %pad_maximum_fusion), channel_id=1, source_target_pairs={{0,8},{1,9},{2,10},{3,11},{4,12},{5,13},{6,14},{7,15},{8,0},{9,1},... | collective-permute-start | bytes 430088 | tf_op jit(solution)/shard_map/ppermute | solution.py:430
  17.1 0.3 collective-permute-start.4
  17.4 2.2 %copy-done = bf16[128,128,128]{2,1,0:T(8,128)(2,1)S(1)} copy-done((bf16[128,128,128]{2,1,0:T(8,128)(2,1)S(1)}, bf16[128,128,128]{2,1,0:T(8,128)(2,1)}, u32[]{:S(2)}) %copy-start) | copy-done | bytes 4194328
  19.6 6.2 %aggregate0.1 = (bf16[128,128,128]{2,1,0:T(8,128)(2,1)S(1)}, bf16[128,128,128]{2,1,0:T(8,128)(2,1)S(1)}) custom-call(bf16[128,128,128]{2,1,0:T(8,128)(2,1)S(1)} %copy-done, f32[9,128,128]{2,1,0:T(8,128)S(1)} %copy-done.2, bf16[128,128]{1,0:T(8,128)(2,1)S(1)} %slice.191.refs_2_, bf16[128,128]{1,0:T(8,128)(2,1)S(1)} %slice.208.refs_3_, ...), custom_call_target="tpu_custom_call" | custom-call | flops 41943040 | bytes 16777216 | tf_op jit(solution)/shard_map/aggregate0/pallas_call | solution.py:409
  25.9 2.7 %collective-permute-start.3 = (bf16[2,4,56,128]{3,2,1,0:T(8,128)(2,1)S(1)}, bf16[2,4,56,128]{3,2,1,0:T(8,128)(2,1)S(1)}, u32[]{:S(2)}, u32[]{:S(2)}) collective-permute-start(bf16[2,4,56,128]{3,2,1,0:T(8,128)(2,1)S(1)} %bitcast.100), channel_id=1, source_target_pairs={{0,4},{1,5},{2,6},{3,7},{4,0},{5,1},{6,2},{7,3},{8,12},{9,13},{10,... | collective-permute-start | bytes 344072 | tf_op jit(solution)/shard_map/ppermute | solution.py:430
  28.6 6.4 %aggregate1.1 = (bf16[128,128,128]{2,1,0:T(8,128)(2,1)S(1)}, bf16[128,128,128]{2,1,0:T(8,128)(2,1)S(1)}) custom-call(bf16[128,128,128]{2,1,0:T(8,128)(2,1)S(1)} %copy-done.1, f32[9,128,128]{2,1,0:T(8,128)S(1)} %copy-done.2, bf16[128,128]{1,0:T(8,128)(2,1)S(1)} %slice.191.refs_2_, bf16[128,128]{1,0:T(8,128)(2,1)S(1)} %slice.208.refs_3_, ...), custom_call_target="tpu_custom_call" | custom-call | flops 41943040 | bytes 16777216 | tf_op jit(solution)/shard_map/aggregate1/pallas_call | solution.py:409
  35.3 8.0 %aggregate2.1 = (bf16[128,128,128]{2,1,0:T(8,128)(2,1)S(1)}, bf16[128,128,128]{2,1,0:T(8,128)(2,1)S(1)}) custom-call(bf16[128,128,128]{2,1,0:T(8,128)(2,1)S(1)} %copy-done.1, f32[9,128,128]{2,1,0:T(8,128)S(1)} %copy-done.2, bf16[128,128]{1,0:T(8,128)(2,1)S(1)} %slice.191.refs_2_, bf16[128,128]{1,0:T(8,128)(2,1)S(1)} %slice.208.refs_3_, ...), custom_call_target="tpu_custom_call" | custom-call | flops 41943040 | bytes 16777216 | tf_op jit(solution)/shard_map/aggregate2/pallas_call | solution.py:409
  43.4 0.1 maximum_select_fusion
  43.6 2.2 %border.1 = (bf16[2,136,128]{2,1,0:T(8,128)(2,1)S(1)}, bf16[2,128,128]{2,1,0:T(8,128)(2,1)S(1)}) custom-call(s32[2]{0:T(128)S(1)} %add_convert_fusion.flags_ref, bf16[2,136,128]{2,1,0:T(8,128)(2,1)S(1)} %bitcast.92, bf16[2,136,128]{2,1,0:T(8,128)(2,1)S(1)} %bitcast.91, bf16[2,128,128]{2,1,0:T(8,128)(2,1)S(1)} %bitcast.90, bf16[2,128,128]{2,1,0:T(8,128)(2,1)S(1)} %bitcast.88, ...), custom_call_target="tpu_custom_call" | custom-call | tf_op jit(solution)/shard_map/border/pallas_call | solution.py:409
  45.8 32.1 %refine.1 = bf16[128,128,128]{2,1,0:T(8,128)(2,1)} custom-call(bf16[128,128,128]{2,1,0:T(8,128)(2,1)S(1)} %get-tuple-element.27.normed_ref, bf16[128,128,128]{2,1,0:T(8,128)(2,1)S(1)} %get-tuple-element.28.row_ref, f32[9,128,128]{2,1,0:T(8,128)S(1)} %copy-done.2, bf16[2,136,128]{2,1,0:T(8,128)(2,1)S(1)} %get-tuple-element.29.lines_ref, ...), custom_call_target="tpu_custom_call" | custom-call | tf_op jit(solution)/shard_map/refine/pallas_call | solution.py:409
  (64 shorter events, 0.9 us)
Async XLA Ops:
  0.0 17.4 %copy-start.2 = (f32[9,128,128]{2,1,0:T(8,128)S(1)}, f32[9,128,128]{2,1,0:T(8,128)}, u32[]{:S(2)}) copy-start(f32[9,128,128]{2,1,0:T(8,128)} %metric_ref.1) | copy-start | bytes 1769476
  0.0 7.4 %copy-start.5 = (bf16[2,28,128]{2,0,1:T(2,128)(2,1)S(1)}, bf16[2,28,128]{2,0,1:T(2,128)(2,1)}, u32[]{:S(2)}) copy-start(bf16[2,28,128]{2,0,1:T(2,128)(2,1)} %param.11) | copy-start | bytes 43012
  0.0 17.4 %copy-start.3 = (f32[2,4,128]{2,1,0:T(4,128)S(1)}, f32[2,4,128]{2,1,0:T(4,128)}, u32[]{:S(2)}) copy-start(f32[2,4,128]{2,1,0:T(4,128)} %bias_ref.3) | copy-start | bytes 12292
  0.0 17.4 %copy-start.4 = (f32[2,128]{1,0:T(2,128)S(1)}, f32[2,128]{1,0:T(2,128)}, u32[]{:S(2)}) copy-start(f32[2,128]{1,0:T(2,128)} %gain_ref.3) | copy-start | bytes 3076
  4.0 3.4 %collective-permute-start = (bf16[344,128]{1,0:T(8,128)(2,1)S(1)}, bf16[344,128]{1,0:T(8,128)(2,1)S(1)}, u32[]{:S(2)}, u32[]{:S(2)}) collective-permute-start(bf16[344,128]{1,0:T(8,128)(2,1)S(1)} %fusion.18), channel_id=1, source_target_pairs={{0,1},{1,0},{2,3},{3,2},{4,5},{5,4},{6,7},{7,6},{8,9},{9,8},{10,11... | collective-permute-start | bytes 264200 | tf_op jit(solution)/shard_map/ppermute | solution.py:430
  7.4 7.5 %collective-permute-start.1 = (bf16[400,128]{1,0:T(8,128)(2,1)S(1)}, bf16[400,128]{1,0:T(8,128)(2,1)S(1)}, u32[]{:S(2)}, u32[]{:S(2)}) collective-permute-start(bf16[400,128]{1,0:T(8,128)(2,1)S(1)} %fusion.15), channel_id=1, source_target_pairs={{0,7},{1,2},{2,1},{3,4},{4,3},{5,6},{6,5},{7,0},{8,15},{9,10},{10,... | collective-permute-start | bytes 307208 | tf_op jit(solution)/shard_map/ppermute | solution.py:430
  15.5 10.3 %collective-permute-start.2 = (bf16[560,128]{1,0:T(8,128)(2,1)S(1)}, bf16[560,128]{1,0:T(8,128)(2,1)S(1)}, u32[]{:S(2)}, u32[]{:S(2)}) collective-permute-start(bf16[560,128]{1,0:T(8,128)(2,1)S(1)} %pad_maximum_fusion), channel_id=1, source_target_pairs={{0,8},{1,9},{2,10},{3,11},{4,12},{5,13},{6,14},{7,15},{8,0},{9,1},... | collective-permute-start | bytes 430088 | tf_op jit(solution)/shard_map/ppermute | solution.py:430
  17.1 17.9 %collective-permute-start.4 = (bf16[336,128]{1,0:T(8,128)(2,1)S(1)}, bf16[336,128]{1,0:T(8,128)(2,1)S(1)}, u32[]{:S(2)}, u32[]{:S(2)}) collective-permute-start(bf16[336,128]{1,0:T(8,128)(2,1)S(1)} %get-tuple-element.49), channel_id=1, source_target_pairs={{0,4},{1,5},{2,6},{3,7},{4,0},{5,1},{6,2},{7,3},{8,16},{9,17},{10,... | collective-permute-start | bytes 258056 | tf_op jit(solution)/shard_map/ppermute | solution.py:430
  17.4 2.2 %copy-start = (bf16[128,128,128]{2,1,0:T(8,128)(2,1)S(1)}, bf16[128,128,128]{2,1,0:T(8,128)(2,1)}, u32[]{:S(2)}) copy-start(bf16[128,128,128]{2,1,0:T(8,128)(2,1)} %refs_0_.5) | copy-start | bytes 12582916
  19.6 9.0 %copy-start.1 = (bf16[128,128,128]{2,1,0:T(8,128)(2,1)S(1)}, bf16[128,128,128]{2,1,0:T(8,128)(2,1)}, u32[]{:S(2)}) copy-start(bf16[128,128,128]{2,1,0:T(8,128)(2,1)} %refs_0_.5) | copy-start | bytes 12582916
  25.9 9.1 %collective-permute-start.3 = (bf16[2,4,56,128]{3,2,1,0:T(8,128)(2,1)S(1)}, bf16[2,4,56,128]{3,2,1,0:T(8,128)(2,1)S(1)}, u32[]{:S(2)}, u32[]{:S(2)}) collective-permute-start(bf16[2,4,56,128]{3,2,1,0:T(8,128)(2,1)S(1)} %bitcast.100), channel_id=1, source_target_pairs={{0,4},{1,5},{2,6},{3,7},{4,0},{5,1},{6,2},{7,3},{8,12},{9,13},{10,... | collective-permute-start | bytes 344072 | tf_op jit(solution)/shard_map/ppermute | solution.py:430
  35.2 8.2 %collective-permute-start.5 = (bf16[896,128]{1,0:T(8,128)(2,1)S(1)}, bf16[896,128]{1,0:T(8,128)(2,1)S(1)}, u32[]{:S(2)}, u32[]{:S(2)}) collective-permute-start(bf16[896,128]{1,0:T(8,128)(2,1)S(1)} %bitcast.94), channel_id=1, source_target_pairs={{0,16},{1,17},{2,18},{3,19},{4,20},{5,21},{6,22},{7,23},{8,24},{9,... | collective-permute-start | bytes 688136 | tf_op jit(solution)/shard_map/ppermute | solution.py:430

commit v3 on v2

v3 whole, which is shorter than its diff:
```python
import functools

import jax
import jax.numpy as jnp
from jax import lax
from jax.experimental import pallas as pl
from jax.experimental.pallas import tpu as pltpu
from jax.sharding import PartitionSpec as P

KMAT = 7
ITERS = 2
EPSILON = 1e-05
LANES = 128
BLOCK = 4
DEPTH = 4 * BLOCK
LINE = 136
ORDER_ONE = (("S", 0), ("T", 0))
ORDER_TWO = (("G", 99), ("M", 99), ("S", 99), ("g", 99), ("m", 99), ("O", 99))
F32 = jnp.float32
BF16 = jnp.bfloat16


def twice(a):
    return jnp.concatenate([a, a], axis=1)


def load_vectors(it, coef_ref, gain_ref, bias_ref, rows_s, coef_s, vec_s):
    rows_s[...] = jnp.zeros_like(rows_s)
    rows_s[0:9, :] = coef_ref[:, it, :]
    rows_s[9:10, :] = gain_ref[it : it + 1, :]
    rows_s[10:14, :] = bias_ref[it]
    columns = rows_s[...].T
    for d in range(9):
        coef_s[d] = jnp.broadcast_to(columns[:, d : d + 1], (LANES, LANES))
    for k in range(5):
        factor = 0.5 if k in (2, 3) else 1.0
        vec_s[k] = jnp.broadcast_to(columns[:, 9 + k : 10 + k] * factor, (LANES, LANES))


def load_weights(it, w_ref, m0_s, wg_s):
    def mat(k):
        return w_ref[it, k * LANES : (k + 1) * LANES, :].astype(F32).T

    m0_s[...] = mat(0).astype(BF16)
    h1, h2, h4, h5, h6 = (mat(k) * 0.5 for k in (1, 2, 4, 5, 6))
    parts = [
        jnp.concatenate([h1, h4], 1),
        jnp.concatenate([h2, h5], 1),
        jnp.concatenate([mat(3), h6], 1),
        jnp.concatenate([jnp.zeros_like(h6), h6], 1),
    ]
    for g in range(8):
        for n, part in enumerate(parts):
            wg_s[64 * g + 16 * n : 64 * g + 16 * n + 16, :] = part[16 * g : 16 * g + 16].astype(BF16)


def turned_lines(line):
    wide = line.astype(F32)
    return [wide[1 + b : 129 + b].T for b in range(3)]


def fill_sides(side_s, west, east, side_metric_ref, coef_s, north, south):
    lane = lax.broadcasted_iota(jnp.int32, (LANES, LANES), 1)

    def part(side, column, above, below):
        middle = side.astype(F32).T
        upper, lower = pltpu.roll(middle, 1, 1), pltpu.roll(middle, LANES - 1, 1)
        if above is not None:
            upper = jnp.where(lane == 0, above, upper)
            lower = jnp.where(lane == LANES - 1, below, lower)
        total = None
        for a, cells in enumerate((upper, middle, lower)):
            d = 3 * a + 2 * column
            term = (cells * coef_s[d]) * side_metric_ref[column, d : d + 1, :]
            total = term if total is None else total + term
        return total

    ends = [None] * 4
    if north is not None:
        ends = [north[0][:, 0:1], south[0][:, 0:1], north[2][:, LANES - 1 :], south[2][:, LANES - 1 :]]
    first = part(west, 0, ends[0], ends[1])
    last = pltpu.roll(part(east, 1, ends[2], ends[3]), LANES - 1, 1)
    odd = lane % 2 == 1
    side_s[0] = jnp.where(odd, last, first)
    side_s[1] = jnp.where(odd, first, last)


def stencil_block(g, read_part, metric_ref, side_s, coef_s, vec_s, acc_s, lane, write):
    for pair in range(BLOCK // 2):
        first = g * BLOCK + 2 * pair
        squares = [None, None]
        turns = [lax.rem(2 * LANES - first - r, LANES) for r in range(2)]
        metric = [
            [jnp.broadcast_to(metric_ref[d, pl.ds(first + r, 1), :], (8, LANES)) for r in range(2)]
            for d in range(9)
        ]
        for group in range(LANES // 16):
            rows = [read_part(first - 1 + k, slice(16 * group, 16 * group + 16)).astype(F32) for k in range(4)]
            for half in range(2):
                cs = slice(16 * group + 8 * half, 16 * group + 8 * half + 8)
                cells = [row[8 * half : 8 * half + 8] for row in rows]
                for r in range(2):
                    sums = []
                    for b in range(3):
                        total = None
                        for a in range(3):
                            d = 3 * a + b
                            term = (cells[r + a] * coef_s[d, cs, :]) * metric[d][r]
                            total = term if total is None else total + term
                        sums.append(total)
                    side = pltpu.roll(side_s[r, cs, :], turns[r], 1)
                    west = jnp.where(lane == 0, side, pltpu.roll(sums[0], 1, 1))
                    east = jnp.where(lane == LANES - 1, side, pltpu.roll(sums[2], LANES - 1, 1))
                    total = (sums[1] + west) + east
                    square = total * total
                    squares[r] = square if squares[r] is None else squares[r] + square
                    acc_s[cs, LANES * r : LANES * r + LANES] = total
                yield
        for r in range(2):
            mean = jnp.sum(squares[r], axis=0, keepdims=True) * (1.0 / LANES)
            scale = lax.rsqrt(mean + EPSILON)
            total = acc_s[:, LANES * r : LANES * r + LANES]
            write(2 * pair + r, (total * scale * vec_s[0]).astype(BF16))


def message_block(normed, m0_s, vec_s, write):
    product = jnp.dot(m0_s[...], normed, preferred_element_type=F32)
    yield
    for pair in range(BLOCK // 2):
        ls = slice(2 * LANES * pair, 2 * LANES * (pair + 1))
        write(ls, (product[:, ls] + twice(vec_s[1])).astype(BF16))
        yield


def gates_block(read_message, read_part, wg_s, vec_s, write):
    products = []
    for pair in range(BLOCK // 2):
        ls = slice(2 * LANES * pair, 2 * LANES * (pair + 1))
        whole = slice(0, LANES)
        current = jnp.concatenate([read_part(2 * pair, whole), read_part(2 * pair + 1, whole)], axis=1)
        both = jnp.concatenate([read_message(ls), current], axis=0)
        products.append(jnp.dot(wg_s[...], both, preferred_element_type=F32))
    yield
    for pair in range(BLOCK // 2):
        w = products[pair]
        for g in range(8):
            o = 64 * g
            cs = slice(16 * g, 16 * g + 16)
            old = jnp.concatenate([read_part(2 * pair, cs), read_part(2 * pair + 1, cs)], axis=1).astype(F32)
            update = jnp.tanh(w[o : o + 16] + twice(vec_s[2, cs, :]))
            reset = jnp.tanh(w[o + 16 : o + 32] + twice(vec_s[3, cs, :]))
            inner = (w[o + 32 : o + 48] + twice(vec_s[4, cs, :])) + reset * w[o + 48 : o + 64]
            new = jnp.tanh(inner)
            blend = ((old + new) + update * (old - new)) * 0.5
            blend = blend.astype(BF16)
            for r in range(2):
                write(2 * pair + r, cs, blend[:, LANES * r : LANES * r + LANES])
            yield


def run_stages(stages, order, first, last, guarded):
    names = list(dict.fromkeys(name for name, _ in order))

    def step(s, carry):
        if guarded:
            for name in names:
                fn, lag, low, high = stages[name]

                @pl.when((s >= lag + low) & (s < lag + high))
                def _():
                    for _ in fn(s - lag):
                        pass

            return carry
        parts = {name: stages[name][0](s - stages[name][1]) for name in names}
        for name, pieces in order:
            for _ in range(pieces):
                next(parts[name], None)
        for name in names:
            for _ in parts[name]:
                pass
        return carry

    lax.fori_loop(first, last, step, 0)


def first_kernel(begin, end, before, wrap, *refs):
    x_ref, metric_ref, side_metric_ref, west_ref, east_ref, coef_ref, gain_ref, bias_ref = refs[:8]
    rest = refs[8:]
    if wrap:
        north_ref, south_ref = rest[:2]
        rest = rest[2:]
    if before:
        old_row_ref, old_normed_ref = rest[:2]
        rest = rest[2:]
    row_ref, normed_ref, side_s, acc_s, rows_s, coef_s, vec_s = rest
    lane = lax.broadcasted_iota(jnp.int32, (8, LANES), 1)
    count = x_ref.shape[0] // BLOCK
    load_vectors(0, coef_ref, gain_ref, bias_ref, rows_s, coef_s, vec_s)
    north = south = None
    if wrap:
        north, south = turned_lines(north_ref[...]), turned_lines(south_ref[...])
        row_ref[BLOCK - 1] = north[1].astype(BF16)
        row_ref[(count + 1) * BLOCK] = south[1].astype(BF16)
    fill_sides(side_s, west_ref[...], east_ref[...], side_metric_ref, coef_s, north, south)

    def turn(g):
        for r in range(BLOCK):
            row = x_ref[g * BLOCK + r].T
            yield
            row_ref[(g + 1) * BLOCK + r] = row
            yield

    def stencil(g):
        def write(r, normed):
            normed_ref[g * BLOCK + r] = normed

        yield from stencil_block(
            g, lambda q, cs: row_ref[q + BLOCK, cs, :], metric_ref, side_s, coef_s, vec_s, acc_s, lane, write
        )

    def copy(g, carry):
        for r in range(BLOCK):
            row_ref[(g + 1) * BLOCK + r] = old_row_ref[(g + 1) * BLOCK + r]
            normed_ref[g * BLOCK + r] = old_normed_ref[g * BLOCK + r]
        return carry

    def span(lo, hi):
        low, high = max(lo - 1, 0), min(hi + 1, count)
        stages = {"T": (turn, 0, low, high), "S": (stencil, 2, lo, hi)}
        run_stages(stages, (("T", 0),), low, lo + 2, True)
        full = min(high, hi + 2)
        run_stages(stages, ORDER_ONE, lo + 2, full, False)
        run_stages(stages, (("S", 0),), full, hi + 2, True)

    if before:
        lax.fori_loop(1, 1 + before, copy, 0)
    if wrap:
        span(0, 1)
    span(begin, end)


def second_kernel(normed_ref, row_ref, metric_ref, side_metric_ref, lines_ref, sides_ref, coef_ref, gain_ref, bias_ref, w_ref,
                  out_hbm, out_ref, state_s, side_s, acc_s, rows_s, coef_s, vec_s, old_vec_s, m0_s, wg_s,
                  msg1_s, msg2_s, normed_s, flip_s, south_s, sem):
    count = out_ref.shape[0] // BLOCK
    lane = lax.broadcasted_iota(jnp.int32, (8, LANES), 1)
    load_vectors(0, coef_ref, gain_ref, bias_ref, rows_s, coef_s, old_vec_s)
    load_vectors(1, coef_ref, gain_ref, bias_ref, rows_s, coef_s, vec_s)
    for it in range(2):
        load_weights(it, w_ref, m0_s.at[it], wg_s.at[it])
    north, south = turned_lines(lines_ref[0]), turned_lines(lines_ref[1])
    state_s[2 * DEPTH - 1] = north[1].astype(BF16)
    south_s[...] = south[1].astype(BF16)
    fill_sides(side_s, sides_ref[0], sides_ref[1], side_metric_ref, coef_s, north, south)

    def message_one(g):
        buf = lax.rem(g, 2)
        normed = jnp.concatenate([normed_ref[g * BLOCK + r] for r in range(BLOCK)], axis=1)

        def write(ls, value):
            msg1_s[buf, :, ls] = value

        yield from message_block(normed, m0_s.at[0], old_vec_s, write)

    def gates_one(g):
        buf = lax.rem(g, 2)

        def write(r, cs, value):
            state_s[lax.rem(g * BLOCK + r, 2 * DEPTH), cs, :] = value

        yield from gates_block(lambda ls: msg1_s[buf, :, ls], lambda r, cs: row_ref[(g + 1) * BLOCK + r, cs, :], wg_s.at[0], old_vec_s, write)

    def stencil(g):
        buf = lax.rem(g, 2)

        def write(r, normed):
            normed_s[buf, :, LANES * r : LANES * r + LANES] = normed

        def part(q, cs):
            return state_s[lax.rem(q + 2 * DEPTH, 2 * DEPTH), cs, :]

        yield from stencil_block(g, part, metric_ref, side_s, coef_s, vec_s, acc_s, lane, write)

    def message_two(g):
        buf = lax.rem(g, 2)

        def write(ls, value):
            msg2_s[buf, :, ls] = value

        yield from message_block(normed_s[buf], m0_s.at[1], vec_s, write)

    def gates_two(g):
        buf = lax.rem(g, 2)

        def write(r, cs, value):
            flip_s[r, cs, :] = value

        yield from gates_block(
            lambda ls: msg2_s[buf, :, ls],
            lambda r, cs: state_s[lax.rem(g * BLOCK + r, 2 * DEPTH), cs, :],
            wg_s.at[1],
            vec_s,
            write,
        )
        for r in range(BLOCK):
            out_ref[g * BLOCK + r] = flip_s[r].T

    def store(g):
        at = pl.ds(g * BLOCK, BLOCK)
        pltpu.make_async_copy(out_ref.at[at], out_hbm.at[at], sem).start()
        yield

    stages = {
        "m": (message_one, 0, 0, count),
        "g": (gates_one, 1, 0, count),
        "S": (stencil, 3, 0, count),
        "M": (message_two, 4, 0, count),
        "G": (gates_two, 5, 0, count),
        "O": (store, 5, 0, count),
    }
    run_stages(stages, ORDER_TWO, 0, 5, True)
    run_stages(stages, ORDER_TWO, 5, count, False)
    state_s[(count * BLOCK) % (2 * DEPTH)] = south_s[...]
    run_stages(stages, ORDER_TWO, count, count + 5, True)
    pltpu.make_async_copy(out_ref, out_hbm, sem).wait()


def fetch_kernel(state_hbm, metric_hbm, state_ref, metric_ref, sems):
    part = state_ref.shape[0] // 8
    copies = [pltpu.make_async_copy(metric_hbm, metric_ref, sems.at[8])]
    for n in range(8):
        at = pl.ds(n * part, part)
        copies.append(pltpu.make_async_copy(state_hbm.at[at], state_ref.at[at], sems.at[n]))
    for copy in copies:
        copy.start()
    for copy in copies:
        copy.wait()
    for a in range(3):
        metric_ref[3 * a] = pltpu.roll(metric_ref[3 * a], LANES - 1, 1)
        metric_ref[3 * a + 2] = pltpu.roll(metric_ref[3 * a + 2], 1, 1)


def edge_kernel(flags_ref, state_hbm, metric_hbm, near_ref, far_ref, rows_ref, sides_ref, west_s, east_s, metric_ref,
                strip_s, line_s, sems):
    rows, cols = state_hbm.shape[0], state_hbm.shape[1]
    copies = [
        pltpu.make_async_copy(state_hbm.at[:, 0:16, :], west_s, sems.at[0]),
        pltpu.make_async_copy(state_hbm.at[:, cols - 16 : cols, :], east_s, sems.at[1]),
        pltpu.make_async_copy(metric_hbm, metric_ref, sems.at[2]),
    ]
    for copy in copies:
        copy.start()
    for copy in copies:
        copy.wait()
    east_near = flags_ref[0] == 1
    out = lax.broadcasted_iota(jnp.int32, (32, 256), 0)
    source = lax.broadcasted_iota(jnp.int32, (32, 256), 1)

    def picker(first):
        return jnp.where(source == (out % 16) * 16 + first + out // 16, 1.0, 0.0).astype(BF16)

    pick_w, pick_e = picker(0), picker(14)
    for part in range(rows // 16):
        at = slice(16 * part, 16 * part + 16)
        west = west_s[at].reshape(256, LANES)
        east = east_s[at].reshape(256, LANES)
        west = jnp.dot(pick_w, west, preferred_element_type=F32)
        east = jnp.dot(pick_e, east, preferred_element_type=F32)
        near = jnp.where(east_near, east, west).astype(BF16)
        far = jnp.where(east_near, west, east).astype(BF16)
        for n in range(2):
            to = n * rows + 16 * part
            near_ref[to : to + 16, :] = near[16 * n : 16 * n + 16]
            far_ref[to : to + 16, :] = far[16 * n : 16 * n + 16]
    line_s[...] = jnp.zeros_like(line_s)
    for d in range(9):
        upright = metric_ref[d].T
        line_s[0, d : d + 1, :] = upright[0:1]
        line_s[1, d : d + 1, :] = upright[LANES - 1 : LANES]
        line_s[2, d : d + 1, :] = metric_ref[d, 0:1, :]
        line_s[3, d : d + 1, :] = metric_ref[d, rows - 1 : rows, :]
    for n in range(4):
        high = line_s[n].astype(BF16)
        strip_s[n, 0:16, :] = high
        strip_s[n, 16:32, :] = (line_s[n] - high.astype(F32)).astype(BF16)
    west, east = strip_s[0].astype(F32), strip_s[1].astype(F32)
    near_ref[2 * rows : 2 * rows + 32, :] = jnp.where(east_near, east, west).astype(BF16)
    far_ref[2 * rows : 2 * rows + 32, :] = jnp.where(east_near, west, east).astype(BF16)
    sides_ref[...] = line_s[0:2]
    rows_ref[0] = strip_s[2]
    rows_ref[1] = strip_s[3]


def ring_kernel(flags_ref, north_ref, south_ref, west_ref, east_ref, own_rows_ref, own_cols_ref,
                row_metric_ref, col_metric_ref, coef_ref, gain_ref, bias_ref, w_ref,
                lines_ref, sides_ref, line_s, metric_s, new_s):
    polar = [flags_ref[1] == 1, flags_ref[2] == 1]
    ghost = [north_ref, south_ref]
    side = [west_ref, east_ref]

    def put(strip, n, value):
        line_s[strip, n, 8 : 8 + LINE, :] = value

    for e in range(2):
        outer = ghost[e][1].astype(F32)
        inner = own_rows_ref[e].astype(F32)
        before, after = (outer, inner) if e == 0 else (inner, outer)
        put(e, 0, jnp.where(polar[e], after, before))
        put(e, 1, ghost[e][0].astype(F32))
        put(e, 2, jnp.where(polar[e], before, after))
    for e in range(2):
        columns = [side[e][0], side[e][1], own_cols_ref[e]] if e == 0 else [side[e][1], side[e][0], own_cols_ref[e]]
        if e == 1:
            columns = columns[::-1]
        for n in range(3):
            at = n if e == 0 else 129 + n
            line_s[2 + e, n, 0:8, :] = jnp.zeros((8, LANES), F32)
            line_s[2 + e, n, 136:152, :] = jnp.zeros((16, LANES), F32)
            line_s[2 + e, n, 10:138, :] = columns[n].astype(F32)
            line_s[2 + e, n, 9:10, :] = line_s[0, 1, 8 + at : 9 + at, :]
            line_s[2 + e, n, 138:139, :] = line_s[1, 1, 8 + at : 9 + at, :]

    def upright(packed):
        both = packed.astype(F32)
        tall = jnp.concatenate([both[0:16] + both[16:32], jnp.zeros((LANES - 16, LANES), F32)], axis=0)
        return tall.T

    metric_s[...] = jnp.zeros_like(metric_s)
    for e in range(2):
        metric_s[e, 2:130, :] = upright(row_metric_ref[e, 0:32])
        ends = upright(row_metric_ref[e, 32:64])
        metric_s[e, 1:2, :] = ends[0:1]
        metric_s[e, 130:131, :] = ends[1:2]
        metric_s[2 + e, 2:130, :] = upright(col_metric_ref[e])
    normed = []
    old = []
    for strip in range(4):
        metric = metric_s[strip]
        total = None
        for n in range(3):
            for shift in range(3):
                d = 3 * n + shift if strip < 2 else 3 * shift + n
                cells = line_s[strip, n, 7 + shift : 7 + shift + LINE, :]
                term = metric[:, d : d + 1] * coef_ref[d, 0:1, :] * cells
                total = term if total is None else total + term
        scale = lax.rsqrt(jnp.mean(total * total, axis=1, keepdims=True) + EPSILON)
        normed.append(total * scale * gain_ref[0:1, :])
        old.append(line_s[strip, 1, 8 : 8 + LINE, :])
    normed = jnp.concatenate(normed, 0).astype(BF16)
    old = jnp.concatenate(old, 0)

    def mat(k):
        return w_ref[0, k * LANES : (k + 1) * LANES, :]

    def dot(a, k):
        return jnp.dot(a, mat(k), preferred_element_type=F32)

    message = (dot(normed, 0) + bias_ref[0, 0:1, :]).astype(BF16)
    hidden = old.astype(BF16)
    update = 0.5 * jnp.tanh(0.5 * (dot(message, 1) + dot(hidden, 4) + bias_ref[0, 1:2, :])) + 0.5
    reset = 0.5 * jnp.tanh(0.5 * (dot(message, 2) + dot(hidden, 5) + bias_ref[0, 2:3, :])) + 0.5
    new = jnp.tanh(dot(message, 3) + bias_ref[0, 3:4, :] + reset * dot(hidden, 6))
    new_s[...] = (1.0 - update) * new + update * old
    for e in range(2):
        lines_ref[e] = new_s[e * LINE : (e + 1) * LINE, :].astype(BF16)
        sides_ref[e] = new_s[(2 + e) * LINE + 2 : (2 + e) * LINE + 130, :].astype(BF16)


def call(kernel, name, outs, scratch, args, smem=0, hbm=0, far_out=False, flops=0, traffic=0, limit=24):
    vmem = pl.BlockSpec(memory_space=pltpu.VMEM)
    scalar = pl.BlockSpec(memory_space=pltpu.SMEM)
    far = pl.BlockSpec(memory_space=pltpu.HBM)
    return pl.pallas_call(
        kernel,
        in_specs=[scalar] * smem + [far] * hbm + [vmem] * (len(args) - smem - hbm),
        out_specs=[far if far_out else vmem] * len(outs),
        out_shape=[s if hasattr(s, "dtype") else jax.ShapeDtypeStruct(s, BF16) for s in outs],
        scratch_shapes=scratch,
        compiler_params=pltpu.CompilerParams(vmem_limit_bytes=limit * 1024 * 1024),
        cost_estimate=pl.CostEstimate(flops=flops, bytes_accessed=traffic, transcendentals=0),
        name=name,
    )(*args)


def swap(mesh_shape, partner, value):
    lat, lon = mesh_shape
    pairs = [(i * lon + k, partner(i, k)[0] * lon + partner(i, k)[1]) for i in range(lat) for k in range(lon)]
    return lax.ppermute(value, ("lat", "lon"), pairs)


def on_device(state, edge_metric, stencil_coef, norm_gain, biases, weights):
    lat, lon = lax.axis_size("lat"), lax.axis_size("lon")
    shape = (lat, lon)
    half = lon // 2
    i, k = lax.axis_index("lat"), lax.axis_index("lon")
    rows, cols, channels = state.shape
    k_even = k % 2 == 0
    i_even = i % 2 == 0

    def ordered(first, mine, theirs):
        return jnp.where(first, jnp.concatenate([mine, theirs]), jnp.concatenate([theirs, mine]))

    def halves(first, a, b):
        return jnp.where(first, a, b), jnp.where(first, b, a)

    def after(value, *others):
        return lax.optimization_barrier((value,) + others)[0]

    shard = weights.transpose(1, 0, 2).reshape(-1, channels)
    stencil_coef = stencil_coef.transpose(1, 0, 2)

    vmem = pltpu.VMEM
    flags = jnp.stack([k_even, i == 0, i == lat - 1]).astype(jnp.int32)
    size = 2 * rows + 32
    near, far, row_metrics, side_metric = call(
        edge_kernel,
        "edges",
        [(size, channels), (size, channels), (2, 32, cols), jax.ShapeDtypeStruct((2, 16, rows), F32)],
        [
            vmem((rows, 16, channels), BF16),
            vmem((rows, 16, channels), BF16),
            vmem(edge_metric.shape, F32),
            vmem((4, 32, LANES), BF16),
            vmem((4, 16, LANES), F32),
            pltpu.SemaphoreType.DMA((3,)),
        ],
        (flags, state, edge_metric),
        smem=1,
        hbm=2,
        limit=12,
    )
    got_near = swap(shape, lambda i, k: (i, k ^ 1), jnp.concatenate([near, shard]))
    size = 2 * rows + 32
    shard = ordered(k_even, shard, got_near[size:])
    far_shard = jnp.concatenate([far, shard])
    got_far = swap(shape, lambda i, k: (i, (k + 1) % lon if k % 2 else (k - 1) % lon), far_shard)
    near_state, near_metric = call(
        fetch_kernel,
        "fetch",
        [state, edge_metric],
        [pltpu.SemaphoreType.DMA((9,))],
        (after(state, far_shard), edge_metric),
        hbm=2,
        traffic=8 * state.size,
        limit=12,
    )
    shard = ordered(jnp.logical_not(k_even), shard, got_far[size:])
    in_e, in_w = halves(k_even, got_near[:size], got_far[:size])
    ghost_w, ghost_e = (a[: 2 * rows].reshape(2, rows, channels) for a in (in_w, in_e))
    metric_w, metric_e = in_w[2 * rows :], in_e[2 * rows :]
    own_e, own_w = halves(k_even, near, far)

    def extended(row, inner):
        lines = []
        for q in (row, inner):
            fill = jnp.zeros((LINE - cols - 4, channels), BF16)
            lines.append(jnp.concatenate([ghost_w[:, q], near_state[q], ghost_e[:, q], fill]))
        return jnp.stack(lines)

    def extended_metric(row, body):
        ends = jnp.concatenate([metric_w[:, row : row + 1], metric_e[:, row : row + 1]], axis=1)
        ends = jnp.pad(ends, ((0, 0), (0, LANES - 2)))
        return jnp.concatenate([body, ends])

    row_n, row_s = extended(0, 1), extended(rows - 1, rows - 2)
    out_n = jnp.concatenate([row_n.reshape(-1, channels), extended_metric(0, row_metrics[0])])
    out_s = jnp.concatenate([row_s.reshape(-1, channels), extended_metric(rows - 1, row_metrics[1])])
    size = out_n.shape[0]
    send_a, send_b = halves(i_even, out_s, out_n)
    send_a = jnp.concatenate([send_a, shard])

    def across(i, k):
        if i == 0 or i == lat - 1:
            return i, (k + half) % lon
        return (i + 1, k) if i % 2 else (i - 1, k)

    got_a = swap(shape, lambda i, k: (i ^ 1, k), send_a)
    got_b = swap(shape, across, send_b)

    tile = state.shape
    square = (LANES, LANES)
    count = rows // BLOCK
    cuts = [1, 1 + (count - 1) // 3, 1 + 2 * (count - 1) // 3, count]

    def aggregate(part, side_w, more):
        begin, end = cuts[part], cuts[part + 1]
        return call(
            functools.partial(first_kernel, begin, end, begin - 1, part == 2),
            "aggregate%d" % part,
            [(rows + 2 * BLOCK,) + square, tile],
            [
                vmem((2,) + square, F32),
                vmem((LANES, 2 * LANES), F32),
                vmem(square, F32),
                vmem((9,) + square, F32),
                vmem((5,) + square, F32),
            ],
            (near_state, near_metric, side_metric, side_w, ghost_e[0], stencil_coef, norm_gain, biases) + more,
            flops=20 * state.size,
            traffic=8 * state.size,
        )

    held = aggregate(0, after(ghost_w[1], send_a, send_b), ())

    shard = ordered((i & 1) == 0, shard, got_a[size:])
    in_s, in_n = halves(i_even, got_a[:size], got_b)
    ghost_n, ghost_s = (a[: 2 * LINE].reshape(2, LINE, channels) for a in (in_n, in_s))
    row_metric = jnp.stack([in_n[2 * LINE :], in_s[2 * LINE :]])

    shard = shard.reshape(2, 4, -1, channels)
    bit = 4
    while bit < lon:
        mine = after(shard, *held) if bit == 4 else shard
        got = swap(shape, lambda i, k, bit=bit: (i, k ^ bit), mine)
        low = (k & bit) == 0
        shard = jnp.where(
            low, jnp.concatenate([shard, got], axis=1), jnp.concatenate([got, shard], axis=1)
        )
        if bit == 4:
            held = aggregate(1, after(ghost_w[1], mine), tuple(held))
        bit *= 2
    place = k % 4
    shard = jnp.where(
        place == 0,
        jnp.roll(shard, -2, axis=1),
        jnp.where(place == 3, jnp.roll(shard, 2, axis=1), shard),
    )
    shard = shard.reshape(-1, channels)
    bit = 2
    while bit < lat:
        mine = after(shard, *held) if bit == 2 else shard
        got = swap(shape, lambda i, k, bit=bit: (i ^ bit, k), mine)
        shard = ordered((i & bit) == 0, shard, got)
        if bit == 2:
            held = aggregate(2, after(ghost_w[1], mine), (ghost_n[0], ghost_s[0]) + tuple(held))
        bit *= 2
    row_t, normed = held
    full = shard.reshape(-1, ITERS, channels).transpose(1, 0, 2)

    lines, sides = call(
        ring_kernel,
        "border",
        [(2, LINE, channels), (2, rows, channels)],
        [vmem((4, 3, LINE + 16, LANES), F32), vmem((4, LINE, LANES), F32), vmem((4 * LINE, LANES), F32)],
        (
            flags,
            ghost_n,
            ghost_s,
            ghost_w,
            ghost_e,
            jnp.stack([row_n[0], row_s[0]]),
            jnp.stack([own_w[:rows], own_e[rows : 2 * rows]]),
            row_metric,
            jnp.stack([metric_w, metric_e]),
            stencil_coef,
            norm_gain,
            biases,
            full,
        ),
        smem=1,
        limit=12,
    )
    (out,) = call(
        second_kernel,
        "refine",
        [tile],
        [
            vmem(tile, BF16),
            vmem((2 * DEPTH,) + square, BF16),
            vmem((2,) + square, F32),
            vmem((LANES, 2 * LANES), F32),
            vmem(square, F32),
            vmem((9,) + square, F32),
            vmem((5,) + square, F32),
            vmem((5,) + square, F32),
            vmem((2,) + square, BF16),
            vmem((2, 4 * LANES, 2 * LANES), BF16),
            vmem((2, LANES, BLOCK * LANES), BF16),
            vmem((2, LANES, BLOCK * LANES), BF16),
            vmem((2, LANES, BLOCK * LANES), BF16),
            vmem((BLOCK,) + square, BF16),
            vmem(square, BF16),
            pltpu.SemaphoreType.DMA,
        ],
        (normed, row_t, near_metric, side_metric, lines, sides, stencil_coef, norm_gain, biases, full),
        far_out=True,
    )
    return out


def solution(mesh):
    in_specs = (
        P("lat", "lon", None),
        P(None, "lat", "lon"),
        P(),
        P(),
        P(),
        P(None, ("lat", "lon"), None),
    )
    out_specs = P("lat", "lon", None)
    return jax.shard_map(on_device, mesh=mesh, in_specs=in_specs, out_specs=out_specs, check_vma=False)
```

time: 78.3 us -> 68.8 us (0.88)
  Pallas kernels: 54.8 us -> 49.4 us
  local copies, waits for them, and re-layouts: 8.44 us -> 5.85 us
    pallas_call x5 -> x7, Pallas kernels: 54.8 us -> 49.4 us  [call(): pl.pallas_call(kernel, in_specs=[scalar] * smem + [far] * hbm + [vmem] *...]
    unnamed x15 -> x16, local copies, waits for them, and re-layouts: 3.57 us -> 5.47 us
    dynamic_slice x1 -> x0, local copies, waits for them, and re-layouts: 1.62 us -> none  [edge(): lax.dynamic_slice(edge_metric, (0, 0, last), (9, rows, 1)).reshape(9, rows)]
    transpose x3 -> x0, local copies, waits for them, and re-layouts: 1.27 us -> none  [edge(): lax.dynamic_slice(state, (0, first, 0), (rows, 2, channels))]
    squeeze x1 -> x2, local copies, waits for them, and re-layouts: 0.82 us -> 0.01 us  [the longest x1 0.01 us: extended(): near_state[q]]
    slice x1 -> x0, local copies, waits for them, and re-layouts: 0.79 us -> none  [extended_metric(): return jnp.concatenate([split_metric(edge_metric[:, row]), ends])]
  transfers between devices with their start and end apart: 6 -> 6, of which waited for: 1 -> 2; matrix products, arithmetic and copies ran while one was open for 4% -> 0% of each run, Pallas kernels for 26% -> 23%
where the time goes in v3:
time: 68.8 us; the launch traced here: 68.6 us
  Pallas kernels  49.4 us (72%)
  starting transfers between devices  10.2 us (15%)
  local copies, waits for them, and re-layouts  5.85 us (9%)
  waiting for transfers between devices  1.97 us (3%)
  other arithmetic  0.75 us (1%)
    pallas_call x7, Pallas kernels, call(): pl.pallas_call(kernel, in_specs=[scalar] * smem + [far] * hbm + [vmem] *...  49.4 us
    ppermute x6, starting transfers between devices, swap(): return lax.ppermute(value, ('lat', 'lon'), pairs)  10.2 us
    unnamed x16, local copies, waits for them, and re-layouts  5.47 us
    ppermute x6, waiting for transfers between devices, swap(): return lax.ppermute(value, ('lat', 'lon'), pairs)  1.97 us
  transfers between devices with their start and end apart: 6, of which 2 were waited for; matrix products, arithmetic and copies ran while one was open for 0% of the time, Pallas kernels for 23%

profile of v3, /device:TPU:0, one launch (start us, length us, event | category | flops | bytes accessed | tf_op | source)
XLA Modules:
  0.0 68.6 jit_solution(8097287962461247418)
XLA Ops:
  0.1 2.2 %copy-done = bf16[128,128,128]{2,1,0:T(8,128)(2,1)S(1)} copy-done((bf16[128,128,128]{2,1,0:T(8,128)(2,1)S(1)}, bf16[128,128,128]{2,1,0:T(8,128)(2,1)}, u32[]{:S(2)}) %copy-start) | copy-done | bytes 4194328
  2.3 1.1 %copy-done.2 = f32[9,128,128]{2,1,0:T(8,128)S(1)} copy-done((f32[9,128,128]{2,1,0:T(8,128)S(1)}, f32[9,128,128]{2,1,0:T(8,128)}, u32[]{:S(2)}) %copy-start.2) | copy-done | bytes 589848
  3.3 1.1 %edges.1 = (bf16[288,128]{1,0:T(8,128)(2,1)S(1)}, bf16[288,128]{1,0:T(8,128)(2,1)S(1)}, bf16[2,32,128]{2,1,0:T(8,128)(2,1)S(1)}, f32[2,16,128]{2,1,0:T(8,128)S(1)}) custom-call(s32[3]{0:T(128)S(1)} %add_convert_fusion.flags_ref, bf16[128,128,128]{2,1,0:T(8,128)(2,1)S(1)} %copy-done, f32[9,128,128]{2,1,0:T(8,128)S(1)} %copy-done.2), custom_call_target="tpu_custom_call" | custom-call | tf_op jit(solution)/shard_map/edges/pallas_call | solution.py:474
  4.5 0.5 collective-permute-start
  5.1 0.1 pad.64.clone
  5.2 0.8 %collective-permute-done = bf16[344,128]{1,0:T(8,128)(2,1)S(1)} collective-permute-done((bf16[344,128]{1,0:T(8,128)(2,1)S(1)}, bf16[344,128]{1,0:T(8,128)(2,1)S(1)}, u32[]{:S(2)}, u32[]{:S(2)}) %collective-permute-start) | collective-permute-done | bytes 88096 | tf_op jit(solution)/shard_map/ppermute | solution.py:489
  6.0 4.8 %collective-permute-start.1 = (bf16[400,128]{1,0:T(8,128)(2,1)S(1)}, bf16[400,128]{1,0:T(8,128)(2,1)S(1)}, u32[]{:S(2)}, u32[]{:S(2)}) collective-permute-start(bf16[400,128]{1,0:T(8,128)(2,1)S(1)} %pad_maximum_fusion.1), channel_id=1, source_target_pairs={{0,7},{1,2},{2,1},{3,4},{4,3},{5,6},{6,5},{7,0},{8,15},{9,10},{10,... | collective-permute-start | bytes 307208 | tf_op jit(solution)/shard_map/ppermute | solution.py:489
  10.8 2.2 %copy-done.1 = bf16[128,128,128]{2,1,0:T(8,128)(2,1)S(1)} copy-done((bf16[128,128,128]{2,1,0:T(8,128)(2,1)S(1)}, bf16[128,128,128]{2,1,0:T(8,128)(2,1)}, u32[]{:S(2)}) %copy-start.1) | copy-done | bytes 4194328
  13.0 0.7 fetch.1
  13.7 0.1 fusion.10
  13.9 0.1 fusion.6
  14.0 0.1 fusion.7
  14.1 0.1 maximum_bitcast_fusion
  14.3 1.8 %collective-permute-start.2 = (bf16[560,128]{1,0:T(8,128)(2,1)S(1)}, bf16[560,128]{1,0:T(8,128)(2,1)S(1)}, u32[]{:S(2)}, u32[]{:S(2)}) collective-permute-start(bf16[560,128]{1,0:T(8,128)(2,1)S(1)} %pad_maximum_fusion), channel_id=1, source_target_pairs={{0,8},{1,9},{2,10},{3,11},{4,12},{5,13},{6,14},{7,15},{8,0},{9,1},... | collective-permute-start | bytes 430088 | tf_op jit(solution)/shard_map/ppermute | solution.py:489
  16.1 0.3 collective-permute-start.4
  16.4 4.6 %aggregate0.1 = (bf16[136,128,128]{2,1,0:T(8,128)(2,1)S(1)}, bf16[128,128,128]{2,1,0:T(8,128)(2,1)S(1)}) custom-call(bf16[128,128,128]{2,1,0:T(8,128)(2,1)S(1)} %get-tuple-element.28.refs_0_, f32[9,128,128]{2,1,0:T(8,128)S(1)} %get-tuple-element.29.refs_1_.metric_ref, f32[2,16,128]{2,1,0:T(8,128)S(1)} %get-tuple-element.30.refs_2_.side_metric_ref, ...), custom_call_target="tpu_custom_call" | custom-call | flops 41943040 | bytes 16777216 | tf_op jit(solution)/shard_map/aggregate0/pallas_call | solution.py:474
  21.0 2.8 %collective-permute-start.3 = (bf16[2,4,56,128]{3,2,1,0:T(8,128)(2,1)S(1)}, bf16[2,4,56,128]{3,2,1,0:T(8,128)(2,1)S(1)}, u32[]{:S(2)}, u32[]{:S(2)}) collective-permute-start(bf16[2,4,56,128]{3,2,1,0:T(8,128)(2,1)S(1)} %bitcast.83), channel_id=1, source_target_pairs={{0,4},{1,5},{2,6},{3,7},{4,0},{5,1},{6,2},{7,3},{8,12},{9,13},{10,... | collective-permute-start | bytes 344072 | tf_op jit(solution)/shard_map/ppermute | solution.py:489
  23.8 4.7 %aggregate1.1 = (bf16[136,128,128]{2,1,0:T(8,128)(2,1)S(1)}, bf16[128,128,128]{2,1,0:T(8,128)(2,1)S(1)}) custom-call(bf16[128,128,128]{2,1,0:T(8,128)(2,1)S(1)} %get-tuple-element.28.refs_0_, f32[9,128,128]{2,1,0:T(8,128)S(1)} %get-tuple-element.29.refs_1_.metric_ref, f32[2,16,128]{2,1,0:T(8,128)S(1)} %get-tuple-element.30.refs_2_.side_metric_ref, ...), custom_call_target="tpu_custom_call" | custom-call | flops 41943040 | bytes 16777216 | tf_op jit(solution)/shard_map/aggregate1/pallas_call | solution.py:474
  28.5 1.1 %collective-permute-done.3 = bf16[2,4,56,128]{3,2,1,0:T(8,128)(2,1)S(1)} collective-permute-done((bf16[2,4,56,128]{3,2,1,0:T(8,128)(2,1)S(1)}, bf16[2,4,56,128]{3,2,1,0:T(8,128)(2,1)S(1)}, u32[]{:S(2)}, u32[]{:S(2)}) %collective-permute-start.3) | collective-permute-done | bytes 114720 | tf_op jit(solution)/shard_map/ppermute | solution.py:489
  29.8 0.1 collective-permute-start.5
  29.9 5.9 %aggregate2.1 = (bf16[136,128,128]{2,1,0:T(8,128)(2,1)S(1)}, bf16[128,128,128]{2,1,0:T(8,128)(2,1)S(1)}) custom-call(bf16[128,128,128]{2,1,0:T(8,128)(2,1)S(1)} %get-tuple-element.28.refs_0_, f32[9,128,128]{2,1,0:T(8,128)S(1)} %get-tuple-element.29.refs_1_.metric_ref, f32[2,16,128]{2,1,0:T(8,128)S(1)} %get-tuple-element.30.refs_2_.side_metric_ref, ...), custom_call_target="tpu_custom_call" | custom-call | flops 41943040 | bytes 16777216 | tf_op jit(solution)/shard_map/aggregate2/pallas_call | solution.py:474
  35.9 0.1 maximum_select_fusion
  36.1 2.2 %border.1 = (bf16[2,136,128]{2,1,0:T(8,128)(2,1)S(1)}, bf16[2,128,128]{2,1,0:T(8,128)(2,1)S(1)}) custom-call(s32[3]{0:T(128)S(1)} %add_convert_fusion.flags_ref, bf16[2,136,128]{2,1,0:T(8,128)(2,1)S(1)} %bitcast.74, bf16[2,136,128]{2,1,0:T(8,128)(2,1)S(1)} %bitcast.73, bf16[2,128,128]{2,1,0:T(8,128)(2,1)S(1)} %bitcast.72, bf16[2,128,128]{2,1,0:T(8,128)(2,1)S(1)} %bitcast.70, ...), custom_call_target="tpu_custom_call" | custom-call | tf_op jit(solution)/shard_map/border/pallas_call | solution.py:474
  38.2 30.3 %refine.1 = bf16[128,128,128]{2,1,0:T(8,128)(2,1)} custom-call(bf16[128,128,128]{2,1,0:T(8,128)(2,1)S(1)} %get-tuple-element.41.normed_ref, bf16[136,128,128]{2,1,0:T(8,128)(2,1)S(1)} %get-tuple-element.42.row_ref, f32[9,128,128]{2,1,0:T(8,128)S(1)} %get-tuple-element.29.refs_1_.metric_ref, f32[2,16,128]{2,1,0:T(8,128)S(1)} %get-tuple-element.30.refs_2_.side_metric_ref, ...), custom_call_target="tpu_custom_call" | custom-call | tf_op jit(solution)/shard_map/refine/pallas_call | solution.py:474
  (60 shorter events, 0.7 us)
Async XLA Ops:
  0.0 4.5 %copy-start.7 = (bf16[2,28,128]{2,0,1:T(2,128)(2,1)S(1)}, bf16[2,28,128]{2,0,1:T(2,128)(2,1)}, u32[]{:S(2)}) copy-start(bf16[2,28,128]{2,0,1:T(2,128)(2,1)} %param.11) | copy-start | bytes 43012
  0.1 2.2 %copy-start = (bf16[128,128,128]{2,1,0:T(8,128)(2,1)S(1)}, bf16[128,128,128]{2,1,0:T(8,128)(2,1)}, u32[]{:S(2)}) copy-start(bf16[128,128,128]{2,1,0:T(8,128)(2,1)} %state_hbm.2) | copy-start | bytes 12582916
  2.3 1.1 %copy-start.2 = (f32[9,128,128]{2,1,0:T(8,128)S(1)}, f32[9,128,128]{2,1,0:T(8,128)}, u32[]{:S(2)}) copy-start(f32[9,128,128]{2,1,0:T(8,128)} %metric_hbm.3) | copy-start | bytes 1769476
  3.3 7.5 %copy-start.3 = (f32[9,128,128]{2,1,0:T(8,128)S(1)}, f32[9,128,128]{2,1,0:T(8,128)}, u32[]{:S(2)}) copy-start(f32[9,128,128]{2,1,0:T(8,128)} %metric_hbm.3) | copy-start | bytes 1769476
  4.5 11.9 %copy-start.4 = (f32[2,9,128]{2,0,1:T(2,128)S(1)}, f32[2,9,128]{2,0,1:T(2,128)}, u32[]{:S(2)}) copy-start(f32[2,9,128]{2,0,1:T(2,128)} %param.8) | copy-start | bytes 27652
  4.5 11.9 %copy-start.5 = (f32[2,4,128]{2,1,0:T(4,128)S(1)}, f32[2,4,128]{2,1,0:T(4,128)}, u32[]{:S(2)}) copy-start(f32[2,4,128]{2,1,0:T(4,128)} %bias_ref.3) | copy-start | bytes 12292
  4.5 11.8 %copy-start.6 = (f32[2,128]{1,0:T(2,128)S(1)}, f32[2,128]{1,0:T(2,128)}, u32[]{:S(2)}) copy-start(f32[2,128]{1,0:T(2,128)} %gain_ref.3) | copy-start | bytes 3076
  4.5 1.4 %collective-permute-start = (bf16[344,128]{1,0:T(8,128)(2,1)S(1)}, bf16[344,128]{1,0:T(8,128)(2,1)S(1)}, u32[]{:S(2)}, u32[]{:S(2)}) collective-permute-start(bf16[344,128]{1,0:T(8,128)(2,1)S(1)} %pad_maximum_fusion.2), channel_id=1, source_target_pairs={{0,1},{1,0},{2,3},{3,2},{4,5},{5,4},{6,7},{7,6},{8,9},{9,8},{10,11... | collective-permute-start | bytes 264200 | tf_op jit(solution)/shard_map/ppermute | solution.py:489
  6.0 7.7 %collective-permute-start.1 = (bf16[400,128]{1,0:T(8,128)(2,1)S(1)}, bf16[400,128]{1,0:T(8,128)(2,1)S(1)}, u32[]{:S(2)}, u32[]{:S(2)}) collective-permute-start(bf16[400,128]{1,0:T(8,128)(2,1)S(1)} %pad_maximum_fusion.1), channel_id=1, source_target_pairs={{0,7},{1,2},{2,1},{3,4},{4,3},{5,6},{6,5},{7,0},{8,15},{9,10},{10,... | collective-permute-start | bytes 307208 | tf_op jit(solution)/shard_map/ppermute | solution.py:489
  10.8 2.2 %copy-start.1 = (bf16[128,128,128]{2,1,0:T(8,128)(2,1)S(1)}, bf16[128,128,128]{2,1,0:T(8,128)(2,1)}, u32[]{:S(2)}) copy-start(bf16[128,128,128]{2,1,0:T(8,128)(2,1)} %state_hbm.2) | copy-start | bytes 12582916
  14.3 6.6 %collective-permute-start.2 = (bf16[560,128]{1,0:T(8,128)(2,1)S(1)}, bf16[560,128]{1,0:T(8,128)(2,1)S(1)}, u32[]{:S(2)}, u32[]{:S(2)}) collective-permute-start(bf16[560,128]{1,0:T(8,128)(2,1)S(1)} %pad_maximum_fusion), channel_id=1, source_target_pairs={{0,8},{1,9},{2,10},{3,11},{4,12},{5,13},{6,14},{7,15},{8,0},{9,1},... | collective-permute-start | bytes 430088 | tf_op jit(solution)/shard_map/ppermute | solution.py:489
  16.1 12.4 %collective-permute-start.4 = (bf16[336,128]{1,0:T(8,128)(2,1)S(1)}, bf16[336,128]{1,0:T(8,128)(2,1)S(1)}, u32[]{:S(2)}, u32[]{:S(2)}) collective-permute-start(bf16[336,128]{1,0:T(8,128)(2,1)S(1)} %get-tuple-element.57), channel_id=1, source_target_pairs={{0,4},{1,5},{2,6},{3,7},{4,0},{5,1},{6,2},{7,3},{8,16},{9,17},{10,... | collective-permute-start | bytes 258056 | tf_op jit(solution)/shard_map/ppermute | solution.py:489
  21.0 8.6 %collective-permute-start.3 = (bf16[2,4,56,128]{3,2,1,0:T(8,128)(2,1)S(1)}, bf16[2,4,56,128]{3,2,1,0:T(8,128)(2,1)S(1)}, u32[]{:S(2)}, u32[]{:S(2)}) collective-permute-start(bf16[2,4,56,128]{3,2,1,0:T(8,128)(2,1)S(1)} %bitcast.83), channel_id=1, source_target_pairs={{0,4},{1,5},{2,6},{3,7},{4,0},{5,1},{6,2},{7,3},{8,12},{9,13},{10,... | collective-permute-start | bytes 344072 | tf_op jit(solution)/shard_map/ppermute | solution.py:489
  29.8 6.1 %collective-permute-start.5 = (bf16[896,128]{1,0:T(8,128)(2,1)S(1)}, bf16[896,128]{1,0:T(8,128)(2,1)S(1)}, u32[]{:S(2)}, u32[]{:S(2)}) collective-permute-start(bf16[896,128]{1,0:T(8,128)(2,1)S(1)} %bitcast.81), channel_id=1, source_target_pairs={{0,16},{1,17},{2,18},{3,19},{4,20},{5,21},{6,22},{7,23},{8,24},{9,... | collective-permute-start | bytes 688136 | tf_op jit(solution)/shard_map/ppermute | solution.py:489

commit v4 on v3

--- a/solution.py
+++ b/solution.py
@@ -161,27 +161,22 @@
 def run_stages(stages, order, first, last, guarded):
     names = list(dict.fromkeys(name for name, _ in order))
 
-    def step(s, carry):
-        if guarded:
-            for name in names:
-                fn, lag, low, high = stages[name]
-
-                @pl.when((s >= lag + low) & (s < lag + high))
-                def _():
-                    for _ in fn(s - lag):
-                        pass
-
-            return carry
-        parts = {name: stages[name][0](s - stages[name][1]) for name in names}
+    def step(s, carry, valid=None):
+        here = [name for name in names if valid is None or valid(name)]
+        parts = {name: stages[name][0](s - stages[name][1]) for name in here}
         for name, pieces in order:
-            for _ in range(pieces):
+            for _ in range(pieces if name in here else 0):
                 next(parts[name], None)
-        for name in names:
+        for name in here:
             for _ in parts[name]:
                 pass
         return carry
 
-    lax.fori_loop(first, last, step, 0)
+    if guarded:
+        for s in range(first, last):
+            step(s, 0, lambda name: stages[name][2] <= s - stages[name][1] < stages[name][3])
+    else:
+        lax.fori_loop(first, last, step, 0)
 
 
 def first_kernel(begin, end, before, wrap, *refs):

time: 68.8 us -> 65.6 us (0.953)
  Pallas kernels: 49.4 us -> 45.7 us
    pallas_call x7, Pallas kernels: 49.4 us -> 45.7 us  [call(): pl.pallas_call(kernel, in_specs=[scalar] * smem + [far] * hbm + [vmem] *...]
  transfers between devices with their start and end apart: 6 -> 6, of which waited for: 2 -> 3; matrix products, arithmetic and copies ran while one was open for 0% -> 0% of each run, Pallas kernels for 23% -> 23%
where the time goes in v4:
time: 65.6 us; the launch traced here: 65.4 us
  Pallas kernels  45.7 us (70%)
  starting transfers between devices  10.2 us (16%)
  local copies, waits for them, and re-layouts  5.85 us (9%)
  waiting for transfers between devices  2.43 us (4%)
  other arithmetic  0.75 us (1%)
    pallas_call x7, Pallas kernels, call(): pl.pallas_call(kernel, in_specs=[scalar] * smem + [far] * hbm + [vmem] *...  45.7 us
    ppermute x6, starting transfers between devices, swap(): return lax.ppermute(value, ('lat', 'lon'), pairs)  10.2 us
    unnamed x16, local copies, waits for them, and re-layouts  5.47 us
    ppermute x6, waiting for transfers between devices, swap(): return lax.ppermute(value, ('lat', 'lon'), pairs)  2.43 us
  transfers between devices with their start and end apart: 6, of which 3 were waited for; matrix products, arithmetic and copies ran while one was open for 0% of the time, Pallas kernels for 23%

profile of v4, /device:TPU:0, one launch (start us, length us, event | category | flops | bytes accessed | tf_op | source)
XLA Modules:
  0.0 65.4 jit_solution(17386125360123858069)
XLA Ops:
  0.1 2.2 %copy-done = bf16[128,128,128]{2,1,0:T(8,128)(2,1)S(1)} copy-done((bf16[128,128,128]{2,1,0:T(8,128)(2,1)S(1)}, bf16[128,128,128]{2,1,0:T(8,128)(2,1)}, u32[]{:S(2)}) %copy-start) | copy-done | bytes 4194328
  2.3 1.1 %copy-done.2 = f32[9,128,128]{2,1,0:T(8,128)S(1)} copy-done((f32[9,128,128]{2,1,0:T(8,128)S(1)}, f32[9,128,128]{2,1,0:T(8,128)}, u32[]{:S(2)}) %copy-start.2) | copy-done | bytes 589848
  3.3 1.1 %edges.1 = (bf16[288,128]{1,0:T(8,128)(2,1)S(1)}, bf16[288,128]{1,0:T(8,128)(2,1)S(1)}, bf16[2,32,128]{2,1,0:T(8,128)(2,1)S(1)}, f32[2,16,128]{2,1,0:T(8,128)S(1)}) custom-call(s32[3]{0:T(128)S(1)} %add_convert_fusion.flags_ref, bf16[128,128,128]{2,1,0:T(8,128)(2,1)S(1)} %copy-done, f32[9,128,128]{2,1,0:T(8,128)S(1)} %copy-done.2), custom_call_target="tpu_custom_call" | custom-call | tf_op jit(solution)/shard_map/edges/pallas_call | solution.py:469
  4.5 0.5 collective-permute-start
  5.2 0.8 %collective-permute-done = bf16[344,128]{1,0:T(8,128)(2,1)S(1)} collective-permute-done((bf16[344,128]{1,0:T(8,128)(2,1)S(1)}, bf16[344,128]{1,0:T(8,128)(2,1)S(1)}, u32[]{:S(2)}, u32[]{:S(2)}) %collective-permute-start) | collective-permute-done | bytes 88096 | tf_op jit(solution)/shard_map/ppermute | solution.py:484
  6.0 4.8 %collective-permute-start.1 = (bf16[400,128]{1,0:T(8,128)(2,1)S(1)}, bf16[400,128]{1,0:T(8,128)(2,1)S(1)}, u32[]{:S(2)}, u32[]{:S(2)}) collective-permute-start(bf16[400,128]{1,0:T(8,128)(2,1)S(1)} %pad_maximum_fusion.1), channel_id=1, source_target_pairs={{0,7},{1,2},{2,1},{3,4},{4,3},{5,6},{6,5},{7,0},{8,15},{9,10},{10,... | collective-permute-start | bytes 307208 | tf_op jit(solution)/shard_map/ppermute | solution.py:484
  10.8 2.2 %copy-done.1 = bf16[128,128,128]{2,1,0:T(8,128)(2,1)S(1)} copy-done((bf16[128,128,128]{2,1,0:T(8,128)(2,1)S(1)}, bf16[128,128,128]{2,1,0:T(8,128)(2,1)}, u32[]{:S(2)}) %copy-start.1) | copy-done | bytes 4194328
  13.0 0.7 %fetch.1 = (bf16[128,128,128]{2,1,0:T(8,128)(2,1)S(1)}, f32[9,128,128]{2,1,0:T(8,128)S(1)}) custom-call(bf16[128,128,128]{2,1,0:T(8,128)(2,1)S(1)} %copy-done.1, f32[9,128,128]{2,1,0:T(8,128)S(1)} %copy-done.3), custom_call_target="tpu_custom_call" | custom-call | bytes 16777216 | tf_op jit(solution)/shard_map/fetch/pallas_call | solution.py:469
  13.7 0.1 fusion.10
  13.9 0.1 fusion.6
  14.0 0.1 fusion.7
  14.1 0.1 maximum_bitcast_fusion
  14.3 1.8 %collective-permute-start.2 = (bf16[560,128]{1,0:T(8,128)(2,1)S(1)}, bf16[560,128]{1,0:T(8,128)(2,1)S(1)}, u32[]{:S(2)}, u32[]{:S(2)}) collective-permute-start(bf16[560,128]{1,0:T(8,128)(2,1)S(1)} %pad_maximum_fusion), channel_id=1, source_target_pairs={{0,8},{1,9},{2,10},{3,11},{4,12},{5,13},{6,14},{7,15},{8,0},{9,1},... | collective-permute-start | bytes 430088 | tf_op jit(solution)/shard_map/ppermute | solution.py:484
  16.1 0.3 collective-permute-start.4
  16.4 4.4 %aggregate0.1 = (bf16[136,128,128]{2,1,0:T(8,128)(2,1)S(1)}, bf16[128,128,128]{2,1,0:T(8,128)(2,1)S(1)}) custom-call(bf16[128,128,128]{2,1,0:T(8,128)(2,1)S(1)} %get-tuple-element.28.refs_0_, f32[9,128,128]{2,1,0:T(8,128)S(1)} %get-tuple-element.29.refs_1_.metric_ref, f32[2,16,128]{2,1,0:T(8,128)S(1)} %get-tuple-element.30.refs_2_.side_metric_ref, ...), custom_call_target="tpu_custom_call" | custom-call | flops 41943040 | bytes 16777216 | tf_op jit(solution)/shard_map/aggregate0/pallas_call | solution.py:469
  20.9 2.8 %collective-permute-start.3 = (bf16[2,4,56,128]{3,2,1,0:T(8,128)(2,1)S(1)}, bf16[2,4,56,128]{3,2,1,0:T(8,128)(2,1)S(1)}, u32[]{:S(2)}, u32[]{:S(2)}) collective-permute-start(bf16[2,4,56,128]{3,2,1,0:T(8,128)(2,1)S(1)} %bitcast.83), channel_id=1, source_target_pairs={{0,4},{1,5},{2,6},{3,7},{4,0},{5,1},{6,2},{7,3},{8,12},{9,13},{10,... | collective-permute-start | bytes 344072 | tf_op jit(solution)/shard_map/ppermute | solution.py:484
  23.7 4.5 %aggregate1.1 = (bf16[136,128,128]{2,1,0:T(8,128)(2,1)S(1)}, bf16[128,128,128]{2,1,0:T(8,128)(2,1)S(1)}) custom-call(bf16[128,128,128]{2,1,0:T(8,128)(2,1)S(1)} %get-tuple-element.28.refs_0_, f32[9,128,128]{2,1,0:T(8,128)S(1)} %get-tuple-element.29.refs_1_.metric_ref, f32[2,16,128]{2,1,0:T(8,128)S(1)} %get-tuple-element.30.refs_2_.side_metric_ref, ...), custom_call_target="tpu_custom_call" | custom-call | flops 41943040 | bytes 16777216 | tf_op jit(solution)/shard_map/aggregate1/pallas_call | solution.py:469
  28.2 1.2 %collective-permute-done.3 = bf16[2,4,56,128]{3,2,1,0:T(8,128)(2,1)S(1)} collective-permute-done((bf16[2,4,56,128]{3,2,1,0:T(8,128)(2,1)S(1)}, bf16[2,4,56,128]{3,2,1,0:T(8,128)(2,1)S(1)}, u32[]{:S(2)}, u32[]{:S(2)}) %collective-permute-start.3) | collective-permute-done | bytes 114720 | tf_op jit(solution)/shard_map/ppermute | solution.py:484
  29.6 0.1 collective-permute-start.5
  29.8 5.6 %aggregate2.1 = (bf16[136,128,128]{2,1,0:T(8,128)(2,1)S(1)}, bf16[128,128,128]{2,1,0:T(8,128)(2,1)S(1)}) custom-call(bf16[128,128,128]{2,1,0:T(8,128)(2,1)S(1)} %get-tuple-element.28.refs_0_, f32[9,128,128]{2,1,0:T(8,128)S(1)} %get-tuple-element.29.refs_1_.metric_ref, f32[2,16,128]{2,1,0:T(8,128)S(1)} %get-tuple-element.30.refs_2_.side_metric_ref, ...), custom_call_target="tpu_custom_call" | custom-call | flops 41943040 | bytes 16777216 | tf_op jit(solution)/shard_map/aggregate2/pallas_call | solution.py:469
  35.4 0.4 collective-permute-done.5
  35.7 0.1 maximum_select_fusion
  35.9 2.2 %border.1 = (bf16[2,136,128]{2,1,0:T(8,128)(2,1)S(1)}, bf16[2,128,128]{2,1,0:T(8,128)(2,1)S(1)}) custom-call(s32[3]{0:T(128)S(1)} %add_convert_fusion.flags_ref, bf16[2,136,128]{2,1,0:T(8,128)(2,1)S(1)} %bitcast.74, bf16[2,136,128]{2,1,0:T(8,128)(2,1)S(1)} %bitcast.73, bf16[2,128,128]{2,1,0:T(8,128)(2,1)S(1)} %bitcast.72, bf16[2,128,128]{2,1,0:T(8,128)(2,1)S(1)} %bitcast.70, ...), custom_call_target="tpu_custom_call" | custom-call | tf_op jit(solution)/shard_map/border/pallas_call | solution.py:469
  38.1 27.3 %refine.1 = bf16[128,128,128]{2,1,0:T(8,128)(2,1)} custom-call(bf16[128,128,128]{2,1,0:T(8,128)(2,1)S(1)} %get-tuple-element.41.normed_ref, bf16[136,128,128]{2,1,0:T(8,128)(2,1)S(1)} %get-tuple-element.42.row_ref, f32[9,128,128]{2,1,0:T(8,128)S(1)} %get-tuple-element.29.refs_1_.metric_ref, f32[2,16,128]{2,1,0:T(8,128)S(1)} %get-tuple-element.30.refs_2_.side_metric_ref, ...), custom_call_target="tpu_custom_call" | custom-call | tf_op jit(solution)/shard_map/refine/pallas_call | solution.py:469
  (60 shorter events, 0.7 us)
Async XLA Ops:
  0.0 4.5 %copy-start.7 = (bf16[2,28,128]{2,0,1:T(2,128)(2,1)S(1)}, bf16[2,28,128]{2,0,1:T(2,128)(2,1)}, u32[]{:S(2)}) copy-start(bf16[2,28,128]{2,0,1:T(2,128)(2,1)} %param.11) | copy-start | bytes 43012
  0.1 2.2 %copy-start = (bf16[128,128,128]{2,1,0:T(8,128)(2,1)S(1)}, bf16[128,128,128]{2,1,0:T(8,128)(2,1)}, u32[]{:S(2)}) copy-start(bf16[128,128,128]{2,1,0:T(8,128)(2,1)} %state_hbm.2) | copy-start | bytes 12582916
  2.3 1.1 %copy-start.2 = (f32[9,128,128]{2,1,0:T(8,128)S(1)}, f32[9,128,128]{2,1,0:T(8,128)}, u32[]{:S(2)}) copy-start(f32[9,128,128]{2,1,0:T(8,128)} %metric_hbm.3) | copy-start | bytes 1769476
  3.3 7.5 %copy-start.3 = (f32[9,128,128]{2,1,0:T(8,128)S(1)}, f32[9,128,128]{2,1,0:T(8,128)}, u32[]{:S(2)}) copy-start(f32[9,128,128]{2,1,0:T(8,128)} %metric_hbm.3) | copy-start | bytes 1769476
  4.5 11.9 %copy-start.4 = (f32[2,9,128]{2,0,1:T(2,128)S(1)}, f32[2,9,128]{2,0,1:T(2,128)}, u32[]{:S(2)}) copy-start(f32[2,9,128]{2,0,1:T(2,128)} %param.8) | copy-start | bytes 27652
  4.5 11.9 %copy-start.5 = (f32[2,4,128]{2,1,0:T(4,128)S(1)}, f32[2,4,128]{2,1,0:T(4,128)}, u32[]{:S(2)}) copy-start(f32[2,4,128]{2,1,0:T(4,128)} %bias_ref.3) | copy-start | bytes 12292
  4.5 11.8 %copy-start.6 = (f32[2,128]{1,0:T(2,128)S(1)}, f32[2,128]{1,0:T(2,128)}, u32[]{:S(2)}) copy-start(f32[2,128]{1,0:T(2,128)} %gain_ref.3) | copy-start | bytes 3076
  4.5 1.4 %collective-permute-start = (bf16[344,128]{1,0:T(8,128)(2,1)S(1)}, bf16[344,128]{1,0:T(8,128)(2,1)S(1)}, u32[]{:S(2)}, u32[]{:S(2)}) collective-permute-start(bf16[344,128]{1,0:T(8,128)(2,1)S(1)} %pad_maximum_fusion.2), channel_id=1, source_target_pairs={{0,1},{1,0},{2,3},{3,2},{4,5},{5,4},{6,7},{7,6},{8,9},{9,8},{10,11... | collective-permute-start | bytes 264200 | tf_op jit(solution)/shard_map/ppermute | solution.py:484
  6.0 7.7 %collective-permute-start.1 = (bf16[400,128]{1,0:T(8,128)(2,1)S(1)}, bf16[400,128]{1,0:T(8,128)(2,1)S(1)}, u32[]{:S(2)}, u32[]{:S(2)}) collective-permute-start(bf16[400,128]{1,0:T(8,128)(2,1)S(1)} %pad_maximum_fusion.1), channel_id=1, source_target_pairs={{0,7},{1,2},{2,1},{3,4},{4,3},{5,6},{6,5},{7,0},{8,15},{9,10},{10,... | collective-permute-start | bytes 307208 | tf_op jit(solution)/shard_map/ppermute | solution.py:484
  10.8 2.2 %copy-start.1 = (bf16[128,128,128]{2,1,0:T(8,128)(2,1)S(1)}, bf16[128,128,128]{2,1,0:T(8,128)(2,1)}, u32[]{:S(2)}) copy-start(bf16[128,128,128]{2,1,0:T(8,128)(2,1)} %state_hbm.2) | copy-start | bytes 12582916
  14.3 6.5 %collective-permute-start.2 = (bf16[560,128]{1,0:T(8,128)(2,1)S(1)}, bf16[560,128]{1,0:T(8,128)(2,1)S(1)}, u32[]{:S(2)}, u32[]{:S(2)}) collective-permute-start(bf16[560,128]{1,0:T(8,128)(2,1)S(1)} %pad_maximum_fusion), channel_id=1, source_target_pairs={{0,8},{1,9},{2,10},{3,11},{4,12},{5,13},{6,14},{7,15},{8,0},{9,1},... | collective-permute-start | bytes 430088 | tf_op jit(solution)/shard_map/ppermute | solution.py:484
  16.1 12.1 %collective-permute-start.4 = (bf16[336,128]{1,0:T(8,128)(2,1)S(1)}, bf16[336,128]{1,0:T(8,128)(2,1)S(1)}, u32[]{:S(2)}, u32[]{:S(2)}) collective-permute-start(bf16[336,128]{1,0:T(8,128)(2,1)S(1)} %get-tuple-element.57), channel_id=1, source_target_pairs={{0,4},{1,5},{2,6},{3,7},{4,0},{5,1},{6,2},{7,3},{8,16},{9,17},{10,... | collective-permute-start | bytes 258056 | tf_op jit(solution)/shard_map/ppermute | solution.py:484
  20.9 8.6 %collective-permute-start.3 = (bf16[2,4,56,128]{3,2,1,0:T(8,128)(2,1)S(1)}, bf16[2,4,56,128]{3,2,1,0:T(8,128)(2,1)S(1)}, u32[]{:S(2)}, u32[]{:S(2)}) collective-permute-start(bf16[2,4,56,128]{3,2,1,0:T(8,128)(2,1)S(1)} %bitcast.83), channel_id=1, source_target_pairs={{0,4},{1,5},{2,6},{3,7},{4,0},{5,1},{6,2},{7,3},{8,12},{9,13},{10,... | collective-permute-start | bytes 344072 | tf_op jit(solution)/shard_map/ppermute | solution.py:484
  29.6 6.1 %collective-permute-start.5 = (bf16[896,128]{1,0:T(8,128)(2,1)S(1)}, bf16[896,128]{1,0:T(8,128)(2,1)S(1)}, u32[]{:S(2)}, u32[]{:S(2)}) collective-permute-start(bf16[896,128]{1,0:T(8,128)(2,1)S(1)} %bitcast.81), channel_id=1, source_target_pairs={{0,16},{1,17},{2,18},{3,19},{4,20},{5,21},{6,22},{7,23},{8,24},{9,... | collective-permute-start | bytes 688136 | tf_op jit(solution)/shard_map/ppermute | solution.py:484

commit v5 on v4

--- a/solution.py
+++ b/solution.py
@@ -15,7 +15,7 @@
 DEPTH = 4 * BLOCK
 LINE = 136
 ORDER_ONE = (("S", 0), ("T", 0))
-ORDER_TWO = (("G", 99), ("M", 99), ("S", 99), ("g", 99), ("m", 99), ("O", 99))
+ORDER_TWO = (("G", 99), ("M", 99), ("S", 9), ("g", 1), ("S", 9), ("g", 99), ("m", 99), ("O", 9))
 F32 = jnp.float32
 BF16 = jnp.bfloat16
 

time: 65.6 us -> 64.9 us (0.989)
  no operation moved by 1% of the time
where the time goes in v5:
time: 64.9 us; the launch traced here: 64.7 us
  Pallas kernels  45.1 us (69%)
  starting transfers between devices  10.2 us (16%)
  local copies, waits for them, and re-layouts  5.85 us (9%)
  waiting for transfers between devices  2.43 us (4%)
  other arithmetic  0.75 us (1%)
    pallas_call x7, Pallas kernels, call(): pl.pallas_call(kernel, in_specs=[scalar] * smem + [far] * hbm + [vmem] *...  45.1 us
    ppermute x6, starting transfers between devices, swap(): return lax.ppermute(value, ('lat', 'lon'), pairs)  10.2 us
    unnamed x16, local copies, waits for them, and re-layouts  5.47 us
    ppermute x6, waiting for transfers between devices, swap(): return lax.ppermute(value, ('lat', 'lon'), pairs)  2.43 us
  transfers between devices with their start and end apart: 6, of which 3 were waited for; matrix products, arithmetic and copies ran while one was open for 0% of the time, Pallas kernels for 23%

profile of v5, /device:TPU:0, one launch (start us, length us, event | category | flops | bytes accessed | tf_op | source)
XLA Modules:
  0.0 64.7 jit_solution(1396370540908559096)
XLA Ops:
  0.1 2.2 %copy-done = bf16[128,128,128]{2,1,0:T(8,128)(2,1)S(1)} copy-done((bf16[128,128,128]{2,1,0:T(8,128)(2,1)S(1)}, bf16[128,128,128]{2,1,0:T(8,128)(2,1)}, u32[]{:S(2)}) %copy-start) | copy-done | bytes 4194328
  2.3 1.1 %copy-done.2 = f32[9,128,128]{2,1,0:T(8,128)S(1)} copy-done((f32[9,128,128]{2,1,0:T(8,128)S(1)}, f32[9,128,128]{2,1,0:T(8,128)}, u32[]{:S(2)}) %copy-start.2) | copy-done | bytes 589848
  3.3 1.1 %edges.1 = (bf16[288,128]{1,0:T(8,128)(2,1)S(1)}, bf16[288,128]{1,0:T(8,128)(2,1)S(1)}, bf16[2,32,128]{2,1,0:T(8,128)(2,1)S(1)}, f32[2,16,128]{2,1,0:T(8,128)S(1)}) custom-call(s32[3]{0:T(128)S(1)} %add_convert_fusion.flags_ref, bf16[128,128,128]{2,1,0:T(8,128)(2,1)S(1)} %copy-done, f32[9,128,128]{2,1,0:T(8,128)S(1)} %copy-done.2), custom_call_target="tpu_custom_call" | custom-call | tf_op jit(solution)/shard_map/edges/pallas_call | solution.py:469
  4.5 0.5 collective-permute-start
  5.2 0.8 %collective-permute-done = bf16[344,128]{1,0:T(8,128)(2,1)S(1)} collective-permute-done((bf16[344,128]{1,0:T(8,128)(2,1)S(1)}, bf16[344,128]{1,0:T(8,128)(2,1)S(1)}, u32[]{:S(2)}, u32[]{:S(2)}) %collective-permute-start) | collective-permute-done | bytes 88096 | tf_op jit(solution)/shard_map/ppermute | solution.py:484
  6.0 4.8 %collective-permute-start.1 = (bf16[400,128]{1,0:T(8,128)(2,1)S(1)}, bf16[400,128]{1,0:T(8,128)(2,1)S(1)}, u32[]{:S(2)}, u32[]{:S(2)}) collective-permute-start(bf16[400,128]{1,0:T(8,128)(2,1)S(1)} %pad_maximum_fusion.1), channel_id=1, source_target_pairs={{0,7},{1,2},{2,1},{3,4},{4,3},{5,6},{6,5},{7,0},{8,15},{9,10},{10,... | collective-permute-start | bytes 307208 | tf_op jit(solution)/shard_map/ppermute | solution.py:484
  10.8 2.2 %copy-done.1 = bf16[128,128,128]{2,1,0:T(8,128)(2,1)S(1)} copy-done((bf16[128,128,128]{2,1,0:T(8,128)(2,1)S(1)}, bf16[128,128,128]{2,1,0:T(8,128)(2,1)}, u32[]{:S(2)}) %copy-start.1) | copy-done | bytes 4194328
  13.0 0.7 %fetch.1 = (bf16[128,128,128]{2,1,0:T(8,128)(2,1)S(1)}, f32[9,128,128]{2,1,0:T(8,128)S(1)}) custom-call(bf16[128,128,128]{2,1,0:T(8,128)(2,1)S(1)} %copy-done.1, f32[9,128,128]{2,1,0:T(8,128)S(1)} %copy-done.3), custom_call_target="tpu_custom_call" | custom-call | bytes 16777216 | tf_op jit(solution)/shard_map/fetch/pallas_call | solution.py:469
  13.7 0.1 fusion.10
  13.9 0.1 fusion.6
  14.0 0.1 fusion.7
  14.1 0.1 maximum_bitcast_fusion
  14.3 1.8 %collective-permute-start.2 = (bf16[560,128]{1,0:T(8,128)(2,1)S(1)}, bf16[560,128]{1,0:T(8,128)(2,1)S(1)}, u32[]{:S(2)}, u32[]{:S(2)}) collective-permute-start(bf16[560,128]{1,0:T(8,128)(2,1)S(1)} %pad_maximum_fusion), channel_id=1, source_target_pairs={{0,8},{1,9},{2,10},{3,11},{4,12},{5,13},{6,14},{7,15},{8,0},{9,1},... | collective-permute-start | bytes 430088 | tf_op jit(solution)/shard_map/ppermute | solution.py:484
  16.1 0.3 collective-permute-start.4
  16.4 4.4 %aggregate0.1 = (bf16[136,128,128]{2,1,0:T(8,128)(2,1)S(1)}, bf16[128,128,128]{2,1,0:T(8,128)(2,1)S(1)}) custom-call(bf16[128,128,128]{2,1,0:T(8,128)(2,1)S(1)} %get-tuple-element.28.refs_0_, f32[9,128,128]{2,1,0:T(8,128)S(1)} %get-tuple-element.29.refs_1_.metric_ref, f32[2,16,128]{2,1,0:T(8,128)S(1)} %get-tuple-element.30.refs_2_.side_metric_ref, ...), custom_call_target="tpu_custom_call" | custom-call | flops 41943040 | bytes 16777216 | tf_op jit(solution)/shard_map/aggregate0/pallas_call | solution.py:469
  20.9 2.8 %collective-permute-start.3 = (bf16[2,4,56,128]{3,2,1,0:T(8,128)(2,1)S(1)}, bf16[2,4,56,128]{3,2,1,0:T(8,128)(2,1)S(1)}, u32[]{:S(2)}, u32[]{:S(2)}) collective-permute-start(bf16[2,4,56,128]{3,2,1,0:T(8,128)(2,1)S(1)} %bitcast.83), channel_id=1, source_target_pairs={{0,4},{1,5},{2,6},{3,7},{4,0},{5,1},{6,2},{7,3},{8,12},{9,13},{10,... | collective-permute-start | bytes 344072 | tf_op jit(solution)/shard_map/ppermute | solution.py:484
  23.7 4.5 %aggregate1.1 = (bf16[136,128,128]{2,1,0:T(8,128)(2,1)S(1)}, bf16[128,128,128]{2,1,0:T(8,128)(2,1)S(1)}) custom-call(bf16[128,128,128]{2,1,0:T(8,128)(2,1)S(1)} %get-tuple-element.28.refs_0_, f32[9,128,128]{2,1,0:T(8,128)S(1)} %get-tuple-element.29.refs_1_.metric_ref, f32[2,16,128]{2,1,0:T(8,128)S(1)} %get-tuple-element.30.refs_2_.side_metric_ref, ...), custom_call_target="tpu_custom_call" | custom-call | flops 41943040 | bytes 16777216 | tf_op jit(solution)/shard_map/aggregate1/pallas_call | solution.py:469
  28.2 1.2 %collective-permute-done.3 = bf16[2,4,56,128]{3,2,1,0:T(8,128)(2,1)S(1)} collective-permute-done((bf16[2,4,56,128]{3,2,1,0:T(8,128)(2,1)S(1)}, bf16[2,4,56,128]{3,2,1,0:T(8,128)(2,1)S(1)}, u32[]{:S(2)}, u32[]{:S(2)}) %collective-permute-start.3) | collective-permute-done | bytes 114720 | tf_op jit(solution)/shard_map/ppermute | solution.py:484
  29.6 0.1 collective-permute-start.5
  29.8 5.6 %aggregate2.1 = (bf16[136,128,128]{2,1,0:T(8,128)(2,1)S(1)}, bf16[128,128,128]{2,1,0:T(8,128)(2,1)S(1)}) custom-call(bf16[128,128,128]{2,1,0:T(8,128)(2,1)S(1)} %get-tuple-element.28.refs_0_, f32[9,128,128]{2,1,0:T(8,128)S(1)} %get-tuple-element.29.refs_1_.metric_ref, f32[2,16,128]{2,1,0:T(8,128)S(1)} %get-tuple-element.30.refs_2_.side_metric_ref, ...), custom_call_target="tpu_custom_call" | custom-call | flops 41943040 | bytes 16777216 | tf_op jit(solution)/shard_map/aggregate2/pallas_call | solution.py:469
  35.4 0.4 collective-permute-done.5
  35.7 0.1 maximum_select_fusion
  35.9 2.2 %border.1 = (bf16[2,136,128]{2,1,0:T(8,128)(2,1)S(1)}, bf16[2,128,128]{2,1,0:T(8,128)(2,1)S(1)}) custom-call(s32[3]{0:T(128)S(1)} %add_convert_fusion.flags_ref, bf16[2,136,128]{2,1,0:T(8,128)(2,1)S(1)} %bitcast.74, bf16[2,136,128]{2,1,0:T(8,128)(2,1)S(1)} %bitcast.73, bf16[2,128,128]{2,1,0:T(8,128)(2,1)S(1)} %bitcast.72, bf16[2,128,128]{2,1,0:T(8,128)(2,1)S(1)} %bitcast.70, ...), custom_call_target="tpu_custom_call" | custom-call | tf_op jit(solution)/shard_map/border/pallas_call | solution.py:469
  38.1 26.6 %refine.1 = bf16[128,128,128]{2,1,0:T(8,128)(2,1)} custom-call(bf16[128,128,128]{2,1,0:T(8,128)(2,1)S(1)} %get-tuple-element.41.normed_ref, bf16[136,128,128]{2,1,0:T(8,128)(2,1)S(1)} %get-tuple-element.42.row_ref, f32[9,128,128]{2,1,0:T(8,128)S(1)} %get-tuple-element.29.refs_1_.metric_ref, f32[2,16,128]{2,1,0:T(8,128)S(1)} %get-tuple-element.30.refs_2_.side_metric_ref, ...), custom_call_target="tpu_custom_call" | custom-call | tf_op jit(solution)/shard_map/refine/pallas_call | solution.py:469
  (60 shorter events, 0.7 us)
Async XLA Ops:
  0.0 4.5 %copy-start.7 = (bf16[2,28,128]{2,0,1:T(2,128)(2,1)S(1)}, bf16[2,28,128]{2,0,1:T(2,128)(2,1)}, u32[]{:S(2)}) copy-start(bf16[2,28,128]{2,0,1:T(2,128)(2,1)} %param.11) | copy-start | bytes 43012
  0.1 2.2 %copy-start = (bf16[128,128,128]{2,1,0:T(8,128)(2,1)S(1)}, bf16[128,128,128]{2,1,0:T(8,128)(2,1)}, u32[]{:S(2)}) copy-start(bf16[128,128,128]{2,1,0:T(8,128)(2,1)} %state_hbm.2) | copy-start | bytes 12582916
  2.3 1.1 %copy-start.2 = (f32[9,128,128]{2,1,0:T(8,128)S(1)}, f32[9,128,128]{2,1,0:T(8,128)}, u32[]{:S(2)}) copy-start(f32[9,128,128]{2,1,0:T(8,128)} %metric_hbm.3) | copy-start | bytes 1769476
  3.3 7.5 %copy-start.3 = (f32[9,128,128]{2,1,0:T(8,128)S(1)}, f32[9,128,128]{2,1,0:T(8,128)}, u32[]{:S(2)}) copy-start(f32[9,128,128]{2,1,0:T(8,128)} %metric_hbm.3) | copy-start | bytes 1769476
  4.5 11.9 %copy-start.4 = (f32[2,9,128]{2,0,1:T(2,128)S(1)}, f32[2,9,128]{2,0,1:T(2,128)}, u32[]{:S(2)}) copy-start(f32[2,9,128]{2,0,1:T(2,128)} %param.8) | copy-start | bytes 27652
  4.5 11.9 %copy-start.5 = (f32[2,4,128]{2,1,0:T(4,128)S(1)}, f32[2,4,128]{2,1,0:T(4,128)}, u32[]{:S(2)}) copy-start(f32[2,4,128]{2,1,0:T(4,128)} %bias_ref.3) | copy-start | bytes 12292
  4.5 11.8 %copy-start.6 = (f32[2,128]{1,0:T(2,128)S(1)}, f32[2,128]{1,0:T(2,128)}, u32[]{:S(2)}) copy-start(f32[2,128]{1,0:T(2,128)} %gain_ref.3) | copy-start | bytes 3076
  4.5 1.4 %collective-permute-start = (bf16[344,128]{1,0:T(8,128)(2,1)S(1)}, bf16[344,128]{1,0:T(8,128)(2,1)S(1)}, u32[]{:S(2)}, u32[]{:S(2)}) collective-permute-start(bf16[344,128]{1,0:T(8,128)(2,1)S(1)} %pad_maximum_fusion.2), channel_id=1, source_target_pairs={{0,1},{1,0},{2,3},{3,2},{4,5},{5,4},{6,7},{7,6},{8,9},{9,8},{10,11... | collective-permute-start | bytes 264200 | tf_op jit(solution)/shard_map/ppermute | solution.py:484
  6.0 7.7 %collective-permute-start.1 = (bf16[400,128]{1,0:T(8,128)(2,1)S(1)}, bf16[400,128]{1,0:T(8,128)(2,1)S(1)}, u32[]{:S(2)}, u32[]{:S(2)}) collective-permute-start(bf16[400,128]{1,0:T(8,128)(2,1)S(1)} %pad_maximum_fusion.1), channel_id=1, source_target_pairs={{0,7},{1,2},{2,1},{3,4},{4,3},{5,6},{6,5},{7,0},{8,15},{9,10},{10,... | collective-permute-start | bytes 307208 | tf_op jit(solution)/shard_map/ppermute | solution.py:484
  10.8 2.2 %copy-start.1 = (bf16[128,128,128]{2,1,0:T(8,128)(2,1)S(1)}, bf16[128,128,128]{2,1,0:T(8,128)(2,1)}, u32[]{:S(2)}) copy-start(bf16[128,128,128]{2,1,0:T(8,128)(2,1)} %state_hbm.2) | copy-start | bytes 12582916
  14.3 6.5 %collective-permute-start.2 = (bf16[560,128]{1,0:T(8,128)(2,1)S(1)}, bf16[560,128]{1,0:T(8,128)(2,1)S(1)}, u32[]{:S(2)}, u32[]{:S(2)}) collective-permute-start(bf16[560,128]{1,0:T(8,128)(2,1)S(1)} %pad_maximum_fusion), channel_id=1, source_target_pairs={{0,8},{1,9},{2,10},{3,11},{4,12},{5,13},{6,14},{7,15},{8,0},{9,1},... | collective-permute-start | bytes 430088 | tf_op jit(solution)/shard_map/ppermute | solution.py:484
  16.1 12.1 %collective-permute-start.4 = (bf16[336,128]{1,0:T(8,128)(2,1)S(1)}, bf16[336,128]{1,0:T(8,128)(2,1)S(1)}, u32[]{:S(2)}, u32[]{:S(2)}) collective-permute-start(bf16[336,128]{1,0:T(8,128)(2,1)S(1)} %get-tuple-element.57), channel_id=1, source_target_pairs={{0,4},{1,5},{2,6},{3,7},{4,0},{5,1},{6,2},{7,3},{8,16},{9,17},{10,... | collective-permute-start | bytes 258056 | tf_op jit(solution)/shard_map/ppermute | solution.py:484
  20.9 8.6 %collective-permute-start.3 = (bf16[2,4,56,128]{3,2,1,0:T(8,128)(2,1)S(1)}, bf16[2,4,56,128]{3,2,1,0:T(8,128)(2,1)S(1)}, u32[]{:S(2)}, u32[]{:S(2)}) collective-permute-start(bf16[2,4,56,128]{3,2,1,0:T(8,128)(2,1)S(1)} %bitcast.83), channel_id=1, source_target_pairs={{0,4},{1,5},{2,6},{3,7},{4,0},{5,1},{6,2},{7,3},{8,12},{9,13},{10,... | collective-permute-start | bytes 344072 | tf_op jit(solution)/shard_map/ppermute | solution.py:484
  29.6 6.1 %collective-permute-start.5 = (bf16[896,128]{1,0:T(8,128)(2,1)S(1)}, bf16[896,128]{1,0:T(8,128)(2,1)S(1)}, u32[]{:S(2)}, u32[]{:S(2)}) collective-permute-start(bf16[896,128]{1,0:T(8,128)(2,1)S(1)} %bitcast.81), channel_id=1, source_target_pairs={{0,16},{1,17},{2,18},{3,19},{4,20},{5,21},{6,22},{7,23},{8,24},{9,... | collective-permute-start | bytes 688136 | tf_op jit(solution)/shard_map/ppermute | solution.py:484
